TPU v7x, 32 devices: a whole 2x2x4 slice. The times are simulated.
32 devices in a mesh: gx: 2 (over x), gy: 4 (over y, core), gz: 4 (over z).
Axes of the slice: x: 2, y: 2, z: 4, core: 2. Of those that a mesh axis runs over, the one named last changes fastest.
Arguments:
- populations: float32 [19, 16, 64, 512], P(None, 'gx', 'gy', 'gz'), may hold values from 0.01 to 0.06
- adjoint_next: float32 [19, 16, 64, 512], P(None, 'gx', 'gy', 'gz'), may hold values from -6 to 6
Outputs:
- adjoint_before: float32 [19, 16, 64, 512], P(None, 'gx', 'gy', 'gz')
All inputs are finite; a program needn't handle non-finite values.
Results may differ from a plain program's by a relative error of at most 0.00002.
Values sent between devices are 32-bit elements; how exact they have to be, the bound alone decides.
No kernel may reach another device: no remote copies, remote signals or barrier semaphores. Data moves between devices by JAX's collectives and lax.ppermute only.
A program may use at most 64 MiB of HBM per device.

v0:
```python
import jax
import jax.numpy as jnp
from jax import lax
from jax.sharding import PartitionSpec as P

DIRECTIONS = (
    (0, 0, 0),
    (1, 0, 0),
    (-1, 0, 0),
    (0, 1, 0),
    (0, -1, 0),
    (0, 0, 1),
    (0, 0, -1),
    (1, 1, 0),
    (-1, -1, 0),
    (1, -1, 0),
    (-1, 1, 0),
    (1, 0, 1),
    (-1, 0, -1),
    (1, 0, -1),
    (-1, 0, 1),
    (0, 1, 1),
    (0, -1, -1),
    (0, 1, -1),
    (0, -1, 1),
)
WEIGHTS = (1.0 / 3.0,) + (1.0 / 18.0,) * 6 + (1.0 / 36.0,) * 12
RELAX_TIME = 0.8
COUPLING = -5.5


def padded_2(value, sides, width):
    for axis, dim in sides:
        count, length = (lax.axis_size(axis), value.shape[dim])
        up = [(i, (i + 1) % count) for i in range(count)]
        down = [(j, i) for i, j in up]
        last = lax.slice_in_dim(value, length - width, length, axis=dim)
        leading = lax.slice_in_dim(value, 0, width, axis=dim)
        before = lax.ppermute(last, axis, up)
        after = lax.ppermute(leading, axis, down)
        value = jnp.concatenate([before, value, after], axis=dim)
    return value


def project(vector, member):
    return (
        DIRECTIONS[member][0] * vector[0]
        + DIRECTIONS[member][1] * vector[1]
        + DIRECTIONS[member][2] * vector[2]
    )


def summed(populations):
    density = populations[0]
    for member in range(1, 19):
        density = density + populations[member]
    return density


def collide(populations, force_field):
    density = summed(populations)
    velocity = []
    for component in range(3):
        moment = 0.5 * force_field[component]
        for member in range(1, 19):
            heading = DIRECTIONS[member][component]
            if heading == 1:
                moment = moment + populations[member]
            elif heading == -1:
                moment = moment - populations[member]
        velocity.append(moment / density)
    speed_sq = velocity[0] * velocity[0] + velocity[1] * velocity[1] + velocity[2] * velocity[2]
    along_force = (
        velocity[0] * force_field[0] + velocity[1] * force_field[1] + velocity[2] * force_field[2]
    )
    results = []
    for member in range(19):
        lattice_u = project(velocity, member)
        lattice_f = project(force_field, member)
        equilibrium = (
            WEIGHTS[member]
            * density
            * (1.0 + 3.0 * lattice_u + 4.5 * lattice_u * lattice_u - 1.5 * speed_sq)
        )
        source = WEIGHTS[member] * (3.0 * (lattice_f - along_force) + 9.0 * lattice_u * lattice_f)
        results.append(
            populations[member]
            - (populations[member] - equilibrium) / RELAX_TIME
            + (1.0 - 0.5 / RELAX_TIME) * source
        )
    return jnp.stack(results)


def window(padded, offset):
    extent = padded.shape
    return padded[
        ...,
        1 + offset[0] : extent[-3] - 1 + offset[0],
        1 + offset[1] : extent[-2] - 1 + offset[1],
        1 + offset[2] : extent[-1] - 1 + offset[2],
    ]


def per_device(populations, adjoint_next):
    density = summed(populations)
    decay_factor = jnp.exp(-density)
    potential = 1.0 - decay_factor
    stacked = jnp.concatenate([adjoint_next, potential[None]], axis=0)
    padded = padded_2(stacked, (("gx", 1), ("gy", 2), ("gz", 3)), 1)
    arrived = jnp.stack([window(padded[member], DIRECTIONS[member]) for member in range(19)])
    potential_pad = padded[19]
    gradient = [jnp.zeros_like(potential) for component in range(3)]
    for member in range(1, 19):
        neighbour = WEIGHTS[member] * window(potential_pad, DIRECTIONS[member])
        for component in range(3):
            if DIRECTIONS[member][component] != 0:
                gradient[component] = (
                    gradient[component] + DIRECTIONS[member][component] * neighbour
                )
    force_field = jnp.stack([-COUPLING * potential * gradient[component] for component in range(3)])
    unused, pullback = jax.vjp(collide, populations, force_field)
    pop_bar, force_bar = pullback(arrived)
    flux_field = potential[None] * force_bar
    flux_pad = padded_2(flux_field, (("gx", 1), ("gy", 2), ("gz", 3)), 1)
    remote = jnp.zeros_like(potential)
    for member in range(1, 19):
        offset = DIRECTIONS[member]
        backward = (-offset[0], -offset[1], -offset[2])
        remote = remote + WEIGHTS[member] * project(window(flux_pad, backward), member)
    local_part = (
        force_bar[0] * gradient[0] + force_bar[1] * gradient[1] + force_bar[2] * gradient[2]
    )
    potential_bar = -COUPLING * (local_part + remote)
    return pop_bar + (potential_bar * decay_factor)[None]


def solution(mesh):
    return jax.shard_map(
        per_device,
        mesh=mesh,
        in_specs=(P(None, "gx", "gy", "gz"), P(None, "gx", "gy", "gz")),
        out_specs=P(None, "gx", "gy", "gz"),
        check_vma=False,
    )
```

profile of v0, /device:TPU:0, one launch (start us, length us, event | category | flops | bytes accessed | tf_op | source)
XLA Modules:
  0.0 82.5 jit_solution(17064111497332647355)
XLA Ops:
  0.0 1.5 %exponential_subtract_fusion = f32[1,8,16,128]{3,2,1,0:T(8,128)S(1)} fusion(f32[19,8,16,128]{3,2,1,0:T(8,128)} %param.2), kind=kLoop, calls=%fused_computation.530 | loop fusion | flops 327680 | bytes 1310720 | tf_op jit(solution)/shard_map/sub | solution.py:107
  1.8 3.0 %collective-permute-start.1 = (f32[20,1,16,128]{3,2,1,0:T(8,128)S(1)}, f32[20,1,16,128]{3,2,1,0:T(8,128)S(1)}, u32[]{:S(2)}, u32[]{:S(2)}) collective-permute-start(f32[20,1,16,128]{3,2,1,0:T(8,128)S(1)} %get-tuple-element.84), channel_id=1, source_target_pairs={{16,0},{0,16},{17,1},{1,17},{18,2},{2,18},{19,3},{3,19},{20,4},{4,... | collective-permute-start | bytes 491528 | tf_op jit(solution)/shard_map/ppermute | solution.py:40
  4.9 4.9 %collective-permute-done.1 = f32[20,1,16,128]{3,2,1,0:T(8,128)S(1)} collective-permute-done((f32[20,1,16,128]{3,2,1,0:T(8,128)S(1)}, f32[20,1,16,128]{3,2,1,0:T(8,128)S(1)}, u32[]{:S(2)}, u32[]{:S(2)}) %collective-permute-start.1) | collective-permute-done | bytes 163872 | tf_op jit(solution)/shard_map/ppermute | solution.py:40
  9.8 2.7 %collective-permute-done = f32[20,1,16,128]{3,2,1,0:T(8,128)S(1)} collective-permute-done((f32[20,1,16,128]{3,2,1,0:T(8,128)S(1)}, f32[20,1,16,128]{3,2,1,0:T(8,128)S(1)}, u32[]{:S(2)}, u32[]{:S(2)}) %collective-permute-start) | collective-permute-done | bytes 163872 | tf_op jit(solution)/shard_map/ppermute | solution.py:39
  13.2 2.2 %collective-permute-done.3 = f32[20,10,1,128]{3,2,1,0:T(1,128)S(1)} collective-permute-done((f32[20,10,1,128]{3,2,1,0:T(1,128)S(1)}, f32[20,10,1,128]{3,2,1,0:T(1,128)S(1)}, u32[]{:S(2)}, u32[]{:S(2)}) %collective-permute-start.3) | collective-permute-done | bytes 102432 | tf_op jit(solution)/shard_map/ppermute | solution.py:40
  15.4 2.8 %collective-permute-done.2 = f32[20,10,1,128]{3,2,1,0:T(1,128)S(1)} collective-permute-done((f32[20,10,1,128]{3,2,1,0:T(1,128)S(1)}, f32[20,10,1,128]{3,2,1,0:T(1,128)S(1)}, u32[]{:S(2)}, u32[]{:S(2)}) %collective-permute-start.2) | collective-permute-done | bytes 102432 | tf_op jit(solution)/shard_map/ppermute | solution.py:39
  18.6 3.0 %fusion.288 = (f32[20,10,18,1]{3,2,1,0:T(8,128)}, f32[20,10,18,1]{3,2,1,0:T(8,128)}) fusion(f32[20,10,18,128]{3,2,1,0:T(8,128)S(1)} %pad_maximum_fusion.1), kind=kLoop, calls=%fused_computation.617 | loop fusion | bytes 57600 | tf_op jit(solution)/shard_map/slice | solution.py:37
  21.6 2.5 %copy.25 = f32[20,10,18,1]{0,3,2,1:T(1,128)S(1)} copy(f32[20,10,18,1]{3,2,1,0:T(8,128)} %get-tuple-element.80) | data formatting | bytes 28800 | tf_op jit(solution)/shard_map/slice | solution.py:38
  24.1 3.6 %collective-permute-start.5 = (f32[20,10,18,1]{0,3,2,1:T(1,128)S(1)}, f32[20,10,18,1]{0,3,2,1:T(1,128)S(1)}, u32[]{:S(2)}, u32[]{:S(2)}) collective-permute-start(f32[20,10,18,1]{0,3,2,1:T(1,128)S(1)} %copy.25), channel_id=1, source_target_pairs={{1,0},{2,1},{3,2},{0,3},{5,4},{6,5},{7,6},{4,7},{9,8},{10,9},{11,1... | collective-permute-start | bytes 43208 | tf_op jit(solution)/shard_map/ppermute | solution.py:40
  27.8 2.6 %copy.24 = f32[20,10,18,1]{0,3,2,1:T(1,128)S(1)} copy(f32[20,10,18,1]{3,2,1,0:T(8,128)} %get-tuple-element.79) | data formatting | bytes 28800 | tf_op jit(solution)/shard_map/slice | solution.py:37
  30.8 2.8 %copy.27 = f32[20,10,18,1]{3,2,1,0:T(8,128)} copy(f32[20,10,18,1]{0,3,2,1:T(1,128)S(1)} %collective-permute-done.5) | data formatting | bytes 28800 | tf_op jit(solution)/shard_map/ppermute | solution.py:40
  33.5 3.4 %collective-permute-done.4 = f32[20,10,18,1]{0,3,2,1:T(1,128)S(1)} collective-permute-done((f32[20,10,18,1]{0,3,2,1:T(1,128)S(1)}, f32[20,10,18,1]{0,3,2,1:T(1,128)S(1)}, u32[]{:S(2)}, u32[]{:S(2)}) %collective-permute-start.4) | collective-permute-done | bytes 14432 | tf_op jit(solution)/shard_map/ppermute | solution.py:39
  37.0 2.8 %copy.26 = f32[20,10,18,1]{3,2,1,0:T(8,128)} copy(f32[20,10,18,1]{0,3,2,1:T(1,128)S(1)} %collective-permute-done.4) | data formatting | bytes 28800 | tf_op jit(solution)/shard_map/ppermute | solution.py:39
  39.7 7.1 %pad_maximum_fusion = f32[20,10,18,130]{3,2,1,0:T(8,128)S(1)} fusion(f32[20,10,18,1]{3,2,1,0:T(8,128)} %copy.27, f32[20,10,1,128]{3,2,1,0:T(1,128)S(1)} %collective-permute-done.3, f32[20,1,16,128]{3,2,1,0:T(8,128)S(1)} %collective-permute-done.1, f32[1,8,16,128]{3,2,1,0:T(8,128)S(1)} %exponential_subtract_fusion, f32[19,8,16,128]{3,2,1,0:T(8,128)S(1)} %copy-done, ...), kind=kLoop, calls=%fused_computation | loop fusion | flops 3276000 | bytes 3744000 | tf_op jit(solution)/shard_map/concatenate | solution.py:41
  48.0 1.1 %multiply_bitcast_fusion.2 = (f32[1,8,16,128]{3,2,1,0:T(8,128)S(1)}, f32[8,16,128]{2,1,0:T(8,128)S(1)}, f32[8,16,128]{2,1,0:T(8,128)S(1)}) fusion(f32[8,16,128]{2,1,0:T(8,128)S(1)} %get-tuple-element.17, f32[8,16,128]{2,1,0:T(8,128)S(1)} %get-tuple-element.11, f32[8,16,128]{2,1,0:T(8,128)S(1)} %get-tuple-element.52, ...), kind=kLoop, calls=%fused_computation.447 | loop fusion | flops 7192576 | bytes 1966080 | tf_op jit(solution)/shard_map/transpose(jvp())/broadcast_in_dim | solution.py:64
  49.1 1.0 %multiply_bitcast_fusion = (f32[1,8,16,128]{3,2,1,0:T(8,128)S(1)}, f32[8,16,128]{2,1,0:T(8,128)S(1)}) fusion(f32[8,16,128]{2,1,0:T(8,128)S(1)} %get-tuple-element.17, f32[8,16,128]{2,1,0:T(8,128)S(1)} %get-tuple-element.9, f32[8,16,128]{2,1,0:T(8,128)S(1)} %get-tuple-element.55, f32[8,16,128]{2,1,0:T(8,128)S(1)} %get-tuple-element.52, ...), kind=kLoop, calls=%fused_computation.445 | loop fusion | flops 6520832 | bytes 1966080 | tf_op jit(solution)/shard_map/transpose(jvp())/broadcast_in_dim | solution.py:64
  50.2 1.0 %multiply_bitcast_fusion.1 = (f32[1,8,16,128]{3,2,1,0:T(8,128)S(1)}, f32[8,16,128]{2,1,0:T(8,128)S(1)}) fusion(f32[8,16,128]{2,1,0:T(8,128)S(1)} %get-tuple-element.17, f32[8,16,128]{2,1,0:T(8,128)S(1)} %get-tuple-element.10, f32[8,16,128]{2,1,0:T(8,128)S(1)} %get-tuple-element.55, f32[8,16,128]{2,1,0:T(8,128)S(1)} %get-tuple-element.52, ...), kind=kLoop, calls=%fused_computation.446 | loop fusion | flops 6569984 | bytes 1966080 | tf_op jit(solution)/shard_map/transpose(jvp())/broadcast_in_dim | solution.py:64
  52.3 1.6 %collective-permute-start.7 = (f32[3,1,16,128]{3,2,1,0:T(8,128)S(1)}, f32[3,1,16,128]{3,2,1,0:T(8,128)S(1)}, u32[]{:S(2)}, u32[]{:S(2)}) collective-permute-start(f32[3,1,16,128]{3,2,1,0:T(8,128)S(1)} %get-tuple-element.135), channel_id=1, source_target_pairs={{16,0},{0,16},{17,1},{1,17},{18,2},{2,18},{19,3},{3,19},{20,4},{4,... | collective-permute-start | bytes 73736 | tf_op jit(solution)/shard_map/ppermute | solution.py:40
  54.4 1.5 %add_bitcast_fusion = f32[1,8,16,128]{3,2,1,0:T(8,128)S(1)} fusion(f32[8,16,128]{2,1,0:T(8,128)S(1)} %get-tuple-element.16, f32[8,16,128]{2,1,0:T(8,128)S(1)} %get-tuple-element.14, f32[8,16,128]{2,1,0:T(8,128)S(1)} %get-tuple-element.12, f32[8,16,128]{2,1,0:T(8,128)S(1)} %get-tuple-element.17, f32[8,16,128]{2,1,0:T(8,128)S(1)} %get-tuple-element.11, ...), kind=kLoop, calls=%fused_computation.500 | loop fusion | flops 10141696 | bytes 2097152 | tf_op jit(solution)/shard_map/transpose(jvp())/broadcast_in_dim | solution.py:56
  56.2 1.5 %collective-permute-done.6 = f32[3,1,16,128]{3,2,1,0:T(8,128)S(1)} collective-permute-done((f32[3,1,16,128]{3,2,1,0:T(8,128)S(1)}, f32[3,1,16,128]{3,2,1,0:T(8,128)S(1)}, u32[]{:S(2)}, u32[]{:S(2)}) %collective-permute-start.6) | collective-permute-done | bytes 24608 | tf_op jit(solution)/shard_map/ppermute | solution.py:39
  59.3 1.8 %collective-permute-done.8 = f32[3,10,1,128]{3,2,1,0:T(1,128)S(1)} collective-permute-done((f32[3,10,1,128]{3,2,1,0:T(1,128)S(1)}, f32[3,10,1,128]{3,2,1,0:T(1,128)S(1)}, u32[]{:S(2)}, u32[]{:S(2)}) %collective-permute-start.8) | collective-permute-done | bytes 15392 | tf_op jit(solution)/shard_map/ppermute | solution.py:39
  61.7 1.7 %collective-permute-start.10 = (f32[3,10,18,1]{3,2,1,0:T(8,128)S(1)}, f32[3,10,18,1]{3,2,1,0:T(8,128)S(1)}, u32[]{:S(2)}, u32[]{:S(2)}) collective-permute-start(f32[3,10,18,1]{3,2,1,0:T(8,128)S(1)} %get-tuple-element.88), channel_id=1, source_target_pairs={{0,1},{1,2},{2,3},{3,0},{4,5},{5,6},{6,7},{7,4},{8,9},{9,10},{10,1... | collective-permute-start | bytes 6488 | tf_op jit(solution)/shard_map/ppermute | solution.py:39
  63.4 15.2 %collective-permute-done.11 = f32[3,10,18,1]{3,2,1,0:T(8,128)S(1)} collective-permute-done((f32[3,10,18,1]{3,2,1,0:T(8,128)S(1)}, f32[3,10,18,1]{3,2,1,0:T(8,128)S(1)}, u32[]{:S(2)}, u32[]{:S(2)}) %collective-permute-start.11) | collective-permute-done | bytes 2192 | tf_op jit(solution)/shard_map/ppermute | solution.py:40
  79.5 3.1 %add_add_fusion = f32[19,8,16,128]{3,2,1,0:T(8,128)} fusion(f32[1,8,16,128]{3,2,1,0:T(8,128)S(1)} %add_bitcast_fusion, f32[1,8,16,128]{3,2,1,0:T(8,128)S(1)} %bitcast.483, f32[1,8,16,128]{3,2,1,0:T(8,128)S(1)} %get-tuple-element.203, f32[1,8,16,128]{3,2,1,0:T(8,128)S(1)} %bitcast.484, f32[1,8,16,128]{3,2,1,0:T(8,128)S(1)} %get-tuple-element.204, ...), kind=kLoop, calls=%fused_computation.2 | loop fusion | flops 27082752 | bytes 4259840 | tf_op jit(solution)/shard_map/add | solution.py:134
  (44 shorter events, 7.9 us)
Async XLA Ops:
  0.0 1.8 %copy-start = (f32[19,8,16,128]{3,2,1,0:T(8,128)S(1)}, f32[19,8,16,128]{3,2,1,0:T(8,128)}, u32[]{:S(2)}) copy-start(f32[19,8,16,128]{3,2,1,0:T(8,128)} %param.3) | copy-start | bytes 3735556
  1.8 8.0 %collective-permute-start.1 = (f32[20,1,16,128]{3,2,1,0:T(8,128)S(1)}, f32[20,1,16,128]{3,2,1,0:T(8,128)S(1)}, u32[]{:S(2)}, u32[]{:S(2)}) collective-permute-start(f32[20,1,16,128]{3,2,1,0:T(8,128)S(1)} %get-tuple-element.84), channel_id=1, source_target_pairs={{16,0},{0,16},{17,1},{1,17},{18,2},{2,18},{19,3},{3,19},{20,4},{4,... | collective-permute-start | bytes 491528 | tf_op jit(solution)/shard_map/ppermute | solution.py:40
  4.8 7.7 %collective-permute-start = (f32[20,1,16,128]{3,2,1,0:T(8,128)S(1)}, f32[20,1,16,128]{3,2,1,0:T(8,128)S(1)}, u32[]{:S(2)}, u32[]{:S(2)}) collective-permute-start(f32[20,1,16,128]{3,2,1,0:T(8,128)S(1)} %get-tuple-element.83), channel_id=1, source_target_pairs={{0,16},{16,0},{1,17},{17,1},{2,18},{18,2},{3,19},{19,3},{4,20},{20... | collective-permute-start | bytes 491528 | tf_op jit(solution)/shard_map/ppermute | solution.py:39
  12.6 2.7 %collective-permute-start.3 = (f32[20,10,1,128]{3,2,1,0:T(1,128)S(1)}, f32[20,10,1,128]{3,2,1,0:T(1,128)S(1)}, u32[]{:S(2)}, u32[]{:S(2)}) collective-permute-start(f32[20,10,1,128]{3,2,1,0:T(1,128)S(1)} %get-tuple-element.82), channel_id=1, source_target_pairs={{4,0},{8,4},{12,8},{0,12},{5,1},{9,5},{13,9},{1,13},{6,2},{10,6},{... | collective-permute-start | bytes 307208 | tf_op jit(solution)/shard_map/ppermute | solution.py:40
  13.0 5.2 %collective-permute-start.2 = (f32[20,10,1,128]{3,2,1,0:T(1,128)S(1)}, f32[20,10,1,128]{3,2,1,0:T(1,128)S(1)}, u32[]{:S(2)}, u32[]{:S(2)}) collective-permute-start(f32[20,10,1,128]{3,2,1,0:T(1,128)S(1)} %get-tuple-element.81), channel_id=1, source_target_pairs={{0,4},{4,8},{8,12},{12,0},{1,5},{5,9},{9,13},{13,1},{2,6},{6,10},{... | collective-permute-start | bytes 307208 | tf_op jit(solution)/shard_map/ppermute | solution.py:39
  24.1 6.6 %collective-permute-start.5 = (f32[20,10,18,1]{0,3,2,1:T(1,128)S(1)}, f32[20,10,18,1]{0,3,2,1:T(1,128)S(1)}, u32[]{:S(2)}, u32[]{:S(2)}) collective-permute-start(f32[20,10,18,1]{0,3,2,1:T(1,128)S(1)} %copy.25), channel_id=1, source_target_pairs={{1,0},{2,1},{3,2},{0,3},{5,4},{6,5},{7,6},{4,7},{9,8},{10,9},{11,1... | collective-permute-start | bytes 43208 | tf_op jit(solution)/shard_map/ppermute | solution.py:40
  27.8 2.9 %copy-start.1 = (f32[19,8,16,128]{3,2,1,0:T(8,128)S(1)}, f32[19,8,16,128]{3,2,1,0:T(8,128)}, u32[]{:S(2)}) copy-start(f32[19,8,16,128]{3,2,1,0:T(8,128)} %param.2) | copy-start | bytes 3735556
  30.4 6.6 %collective-permute-start.4 = (f32[20,10,18,1]{0,3,2,1:T(1,128)S(1)}, f32[20,10,18,1]{0,3,2,1:T(1,128)S(1)}, u32[]{:S(2)}, u32[]{:S(2)}) collective-permute-start(f32[20,10,18,1]{0,3,2,1:T(1,128)S(1)} %copy.24), channel_id=1, source_target_pairs={{0,1},{1,2},{2,3},{3,0},{4,5},{5,6},{6,7},{7,4},{8,9},{9,10},{10,1... | collective-permute-start | bytes 43208 | tf_op jit(solution)/shard_map/ppermute | solution.py:39
  52.3 3.9 %collective-permute-start.7 = (f32[3,1,16,128]{3,2,1,0:T(8,128)S(1)}, f32[3,1,16,128]{3,2,1,0:T(8,128)S(1)}, u32[]{:S(2)}, u32[]{:S(2)}) collective-permute-start(f32[3,1,16,128]{3,2,1,0:T(8,128)S(1)} %get-tuple-element.135), channel_id=1, source_target_pairs={{16,0},{0,16},{17,1},{1,17},{18,2},{2,18},{19,3},{3,19},{20,4},{4,... | collective-permute-start | bytes 73736 | tf_op jit(solution)/shard_map/ppermute | solution.py:40
  53.9 3.8 %collective-permute-start.6 = (f32[3,1,16,128]{3,2,1,0:T(8,128)S(1)}, f32[3,1,16,128]{3,2,1,0:T(8,128)S(1)}, u32[]{:S(2)}, u32[]{:S(2)}) collective-permute-start(f32[3,1,16,128]{3,2,1,0:T(8,128)S(1)} %get-tuple-element.134), channel_id=1, source_target_pairs={{0,16},{16,0},{1,17},{17,1},{2,18},{18,2},{3,19},{19,3},{4,20},{20... | collective-permute-start | bytes 73736 | tf_op jit(solution)/shard_map/ppermute | solution.py:39
  57.8 1.5 %collective-permute-start.9 = (f32[3,10,1,128]{3,2,1,0:T(1,128)S(1)}, f32[3,10,1,128]{3,2,1,0:T(1,128)S(1)}, u32[]{:S(2)}, u32[]{:S(2)}) collective-permute-start(f32[3,10,1,128]{3,2,1,0:T(1,128)S(1)} %get-tuple-element.94), channel_id=1, source_target_pairs={{4,0},{8,4},{12,8},{0,12},{5,1},{9,5},{13,9},{1,13},{6,2},{10,6},{... | collective-permute-start | bytes 46088 | tf_op jit(solution)/shard_map/ppermute | solution.py:40
  57.8 3.2 %collective-permute-start.8 = (f32[3,10,1,128]{3,2,1,0:T(1,128)S(1)}, f32[3,10,1,128]{3,2,1,0:T(1,128)S(1)}, u32[]{:S(2)}, u32[]{:S(2)}) collective-permute-start(f32[3,10,1,128]{3,2,1,0:T(1,128)S(1)} %get-tuple-element.93), channel_id=1, source_target_pairs={{0,4},{4,8},{8,12},{12,0},{1,5},{5,9},{9,13},{13,1},{2,6},{6,10},{... | collective-permute-start | bytes 46088 | tf_op jit(solution)/shard_map/ppermute | solution.py:39
  61.3 17.3 %collective-permute-start.11 = (f32[3,10,18,1]{3,2,1,0:T(8,128)S(1)}, f32[3,10,18,1]{3,2,1,0:T(8,128)S(1)}, u32[]{:S(2)}, u32[]{:S(2)}) collective-permute-start(f32[3,10,18,1]{3,2,1,0:T(8,128)S(1)} %get-tuple-element.87), channel_id=1, source_target_pairs={{1,0},{2,1},{3,2},{0,3},{5,4},{6,5},{7,6},{4,7},{9,8},{10,9},{11,1... | collective-permute-start | bytes 6488 | tf_op jit(solution)/shard_map/ppermute | solution.py:40
  61.7 16.9 %collective-permute-start.10 = (f32[3,10,18,1]{3,2,1,0:T(8,128)S(1)}, f32[3,10,18,1]{3,2,1,0:T(8,128)S(1)}, u32[]{:S(2)}, u32[]{:S(2)}) collective-permute-start(f32[3,10,18,1]{3,2,1,0:T(8,128)S(1)} %get-tuple-element.88), channel_id=1, source_target_pairs={{0,1},{1,2},{2,3},{3,0},{4,5},{5,6},{6,7},{7,4},{8,9},{9,10},{10,1... | collective-permute-start | bytes 6488 | tf_op jit(solution)/shard_map/ppermute | solution.py:39
where the time goes:
time: 82.7 us; the launch traced here: 82.5 us
  waiting for transfers between devices  35.7 us (43%)
  other arithmetic  19.9 us (24%)
  local copies, waits for them, and re-layouts  14.5 us (18%)
  starting transfers between devices  12.3 us (15%)
    ppermute x6, waiting for transfers between devices, padded_2(): after = lax.ppermute(leading, axis, down)  23.5 us
    ppermute x6, waiting for transfers between devices, padded_2(): before = lax.ppermute(last, axis, up)  12.2 us
    ppermute x6, starting transfers between devices, padded_2(): after = lax.ppermute(leading, axis, down)  9.08 us
    concatenate x5, other arithmetic, padded_2(): value = jnp.concatenate([before, value, after], axis=dim)  8.01 us
    slice x3, local copies, waits for them, and re-layouts, padded_2(): last = lax.slice_in_dim(value, length - width, length, axis=dim)  5.62 us
    broadcast_in_dim x3, other arithmetic, collide(): moment = 0.5 * force_field[component]  3.21 us
    ppermute x6, starting transfers between devices, padded_2(): before = lax.ppermute(last, axis, up)  3.17 us
    add x1, other arithmetic, per_device(): return pop_bar + (potential_bar * decay_factor)[None]  3.06 us
  transfers between devices with their start and end apart: 12, of which 10 were waited for; matrix products, arithmetic and copies ran while one was open for 9% of the time, Pallas kernels for 0%

commit v1 on v0

v1 whole, which is shorter than its diff:
```python
import jax
import jax.numpy as jnp
from jax import lax
from jax.experimental import pallas as pl
from jax.experimental.pallas import tpu as pltpu
from jax.sharding import PartitionSpec as P

DIRECTIONS = (
    (0, 0, 0),
    (1, 0, 0),
    (-1, 0, 0),
    (0, 1, 0),
    (0, -1, 0),
    (0, 0, 1),
    (0, 0, -1),
    (1, 1, 0),
    (-1, -1, 0),
    (1, -1, 0),
    (-1, 1, 0),
    (1, 0, 1),
    (-1, 0, -1),
    (1, 0, -1),
    (-1, 0, 1),
    (0, 1, 1),
    (0, -1, -1),
    (0, 1, -1),
    (0, -1, 1),
)
W0, W1, W2 = 1.0 / 3.0, 1.0 / 18.0, 1.0 / 36.0
RELAX_TIME = 0.8
COUPLING = -5.5
INV_TAU = 1.0 / RELAX_TIME
KAPPA = 1.0 - 0.5 / RELAX_TIME

RHO, MOM, FIELDS = 19, 20, 23
ROWS = 24
F32 = jnp.float32
VM = pl.BlockSpec(memory_space=pltpu.VMEM)
HB = pl.BlockSpec(memory_space=pl.ANY)


def deep_fields(dim, side):
    return [i for i in range(19) if DIRECTIONS[i][dim] == side] + [RHO]


def side_fields(dim, side):
    return deep_fields(dim, side) + [i for i in range(19) if DIRECTIONS[i][dim] == 0] + [MOM, MOM + 1, MOM + 2]


def side_entries(dim, side):
    return [(f, d) for d in (0, 1) for f in (side_fields(dim, side) if d == 0 else deep_fields(dim, side))]


def lane_ids(rows):
    return lax.broadcasted_iota(jnp.int32, (rows, 128), 1)


def lroll(v, amount):
    amount = amount % 128
    return v if isinstance(amount, int) and amount == 0 else pltpu.roll(v, amount, 1)


def yroll(v, c):
    return v if c == 0 else pltpu.roll(v, (-c) % ROWS, 0)


def call(body, ins, outs, scratch=(), aliases=None, name=None, in_specs=None, out_specs=None):
    return pl.pallas_call(
        body,
        in_specs=in_specs or [VM] * len(ins),
        out_specs=out_specs or [VM] * len(outs),
        out_shape=[jax.ShapeDtypeStruct(s, F32) for s in outs],
        scratch_shapes=list(scratch),
        input_output_aliases=aliases or {},
        name=name,
        compiler_params=pltpu.CompilerParams(vmem_limit_bytes=20 * 2**20),
    )(*ins)


def load_kernel(pop_hbm, adj_hbm, ext, mini, zlow, zhigh, xmsg, pops, sems):
    nx = pop_hbm.shape[1]
    copies = []
    for f in range(19):
        c = pltpu.make_async_copy(pop_hbm.at[f], pops.at[f], sems.at[f])
        c.start()
        copies.append(c)
    for f in range(19):
        c = pltpu.make_async_copy(adj_hbm.at[f], ext.at[f, pl.ds(2, nx), pl.ds(0, 16), :], sems.at[19 + f])
        c.start()
        copies.append(c)
    for c in copies[:19]:
        c.wait()

    def moments(x, _):
        rho = pops[0, x]
        mom = [None] * 3
        for i in range(1, 19):
            p = pops[i, x]
            rho = rho + p
            for k in range(3):
                c = DIRECTIONS[i][k]
                if c:
                    mom[k] = (p if c > 0 else -p) if mom[k] is None else (mom[k] + p if c > 0 else mom[k] - p)
        ext[RHO, x + 2, pl.ds(0, 16), :] = rho
        for k in range(3):
            ext[MOM + k, x + 2, pl.ds(0, 16), :] = mom[k]
        return 0

    lax.fori_loop(0, nx, moments, 0)
    for c in copies[19:]:
        c.wait()
    lane = lane_ids(16)

    def edges(f, _):
        e = lroll(ext[f, 2, pl.ds(0, 16), :], 10)
        for x in range(1, nx):
            e = jnp.where(lane // 4 == x + 2, lroll(ext[f, x + 2, pl.ds(0, 16), :], 4 * x + 10), e)
        mini[f, pl.ds(0, 16), :] = jnp.where(lane < 64, e, lroll(e, 64))
        return 0

    lax.fori_loop(0, FIELDS, edges, 0)
    for side, msg in ((-1, zlow), (1, zhigh)):
        fields = side_fields(2, side)
        for t in range(msg.shape[0]):
            acc = None
            for j in range(8 * t, min(8 * t + 8, len(fields))):
                q = j % 8
                b, p = q // 2, q % 2
                if side < 0:
                    v = lroll(mini[fields[j], pl.ds(0, 16), :], 32 * b + 2 * p - 72)
                else:
                    v = lroll(mini[fields[j], pl.ds(0, 16), :], 32 * b + 2 * p - 10)
                acc = v if acc is None else jnp.where((lane // 32 == b) & ((lane % 4) // 2 == p), v, acc)
            msg[t] = acc
    for s, side in enumerate((-1, 1)):
        for e, (f, d) in enumerate(side_entries(0, side)):
            plane = (nx + 1 - d) if side < 0 else (2 + d)
            xmsg[s, e] = ext[f, plane, pl.ds(0, 16), :]


def zy_kernel(ext, mini_in, rlow, rhigh, mini, ylow, yhigh):
    lane = lane_ids(16)
    for f in range(FIELDS):
        mini[f, pl.ds(0, 16), :] = mini_in[f, pl.ds(0, 16), :]
    for side, msg in ((-1, rlow), (1, rhigh)):
        if side < 0:
            keep = (lane >= 8) & (lane < 40) & (lane % 4 < 2)
        else:
            keep = (lane >= 72) & (lane < 104) & (lane % 4 >= 2)
        for j, f in enumerate(side_fields(2, side)):
            q = j % 8
            b, p = q // 2, q % 2
            back = 8 - 32 * b - 2 * p if side < 0 else 74 - 32 * b - 2 * p
            mini[f, pl.ds(0, 16), :] = jnp.where(keep, lroll(msg[j // 8], back), mini[f, pl.ds(0, 16), :])
    for side, msg in ((-1, ylow), (1, yhigh)):
        entries = side_entries(1, side)
        for e, (f, d) in enumerate(entries):
            row = 15 - d if side < 0 else d
            msg[pl.ds(8 * e, 8), :] = ext[f, pl.ds(2, 8), row, :]
            msg[pl.ds(8 * len(entries) + e, 1), :] = mini[f, pl.ds(row, 1), :]


def yx_kernel(ext_in, mini_in, rlow, rhigh, ext, mini, xmsg):
    lane = lane_ids(ROWS)
    for side, msg in ((-1, rlow), (1, rhigh)):
        entries = side_entries(1, side)
        for e, (f, d) in enumerate(entries):
            row = 23 - d if side < 0 else 16 + d
            ext[f, pl.ds(2, 8), row, :] = msg[pl.ds(8 * e, 8), :]
            mini[f, pl.ds(row, 1), :] = msg[pl.ds(8 * len(entries) + e, 1), :]
    tile_row = lax.broadcasted_iota(jnp.int32, (8, 128), 0)
    for s, side in enumerate((-1, 1)):
        entries = side_entries(0, side)
        for e in range(0, len(entries), 2):
            pair = []
            for f, d in entries[e : e + 2]:
                plane = 9 - d if side < 0 else 2 + d
                pair.append(ext[f, plane, pl.ds(16, 8), :])
            xmsg[s, pl.ds(4 * e, 8), :] = jnp.where(tile_row < 4, pltpu.roll(pair[0], 2, 0), pltpu.roll(pair[1], 6, 0))
        fields = side_fields(0, side)
        for t in range(3):
            acc = None
            for j in range(8 * t, min(8 * t + 8, len(fields))):
                q = j % 8
                v = lroll(mini[fields[j]], 8 * q - (32 if side < 0 else 8))
                acc = v if acc is None else jnp.where((lane % 64) // 8 == q, v, acc)
            xmsg[s, pl.ds(4 * len(entries) + ROWS * t, ROWS), :] = acc


def cell(b, rho, mom, psi, g):
    pairs = {}
    for i in range(1, 19, 2):
        pairs[i] = (b[i] + b[i + 1], b[i] - b[i + 1])
    s = {i: v[0] for i, v in pairs.items()}
    d = {i: v[1] for i, v in pairs.items()}
    sxy, sxz, syz = s[7] + s[9], s[11] + s[13], s[15] + s[17]
    a0 = W0 * b[0] + W1 * (s[1] + s[3] + s[5]) + W2 * (sxy + sxz + syz)
    a1 = (
        (3 * W1) * d[1] + (3 * W2) * ((d[7] + d[9]) + (d[11] + d[13])),
        (3 * W1) * d[3] + (3 * W2) * ((d[7] - d[9]) + (d[15] + d[17])),
        (3 * W1) * d[5] + (3 * W2) * ((d[11] - d[13]) + (d[15] - d[17])),
    )
    a03 = 3.0 * a0
    bxx = (9 * W1) * s[1] + (9 * W2) * (sxy + sxz) - a03
    byy = (9 * W1) * s[3] + (9 * W2) * (sxy + syz) - a03
    bzz = (9 * W1) * s[5] + (9 * W2) * (sxz + syz) - a03
    bxy = (9 * W2) * (s[7] - s[9])
    bxz = (9 * W2) * (s[11] - s[13])
    byz = (9 * W2) * (s[15] - s[17])
    force = [(-COUPLING * psi) * gk for gk in g]
    inv = 1.0 / rho
    u = [(m + 0.5 * fk) * inv for m, fk in zip(mom, force)]

    def apply(v):
        return (
            bxx * v[0] + bxy * v[1] + bxz * v[2],
            bxy * v[0] + byy * v[1] + byz * v[2],
            bxz * v[0] + byz * v[1] + bzz * v[2],
        )

    w = [p + q for p, q in zip(a1, apply(u))]
    bf = [(KAPPA * inv) * q for q in apply(force)]
    force_bar = [p + 0.5 * q for p, q in zip(w, bf)]
    return a0, a1, u, w, bf, force_bar


def dot(p, q):
    return p[0] * q[0] + p[1] * q[1] + p[2] * q[2]


def last_kernel(ext_in, mini_in, r1, r2, out_hbm, ext, mini, psi, zs, zd, flux, out, sems):
    nx = 8
    lane = lane_ids(ROWS)
    first, last = lane == 0, lane == 127
    for s, side in enumerate((-1, 1)):
        entries = side_entries(0, side)
        for e, (f, d) in enumerate(entries):
            plane = 1 - d if side < 0 else 10 + d
            ext[f, plane, pl.ds(0, 16), :] = r1[s, e]
            tile = r2[s, pl.ds(8 * (e // 2), 8), :]
            ext[f, plane, pl.ds(16, 8), :] = pltpu.roll(tile, 6 if e % 2 == 0 else 2, 0)
        keep = (lane % 64) // 8 == (0 if side < 0 else 5)
        for j, f in enumerate(side_fields(0, side)):
            q = j % 8
            v = r2[s, pl.ds(4 * len(entries) + ROWS * (j // 8), ROWS), :]
            mini[f] = jnp.where(keep, lroll(v, (0 if side < 0 else 40) - 8 * q), mini[f])

    def zsh(v, small, plane, c):
        if c > 0:
            return lroll(jnp.where(first, lroll(small, 62 - 4 * plane + 128), v), 127)
        return lroll(jnp.where(last, lroll(small, 126 - 4 * plane), v), 1)

    mpsi = 1.0 - jnp.exp(-mini[RHO])

    def msh(v, c):
        return lroll(yroll(v, c[1]), -4 * c[0] - c[2])

    def mgrad(v):
        ys = yroll(v, 1) + yroll(v, -1)
        zp, zm = lroll(v, -1), lroll(v, 1)
        xp, xm = lroll(v, -4), lroll(v, 4)
        qx = W1 * v + W2 * (ys + zp + zm)
        qy = W1 * v + W2 * (xp + xm + zp + zm)
        qz = W1 * v + W2 * (xp + xm + ys)
        return (
            lroll(qx, -4) - lroll(qx, 4),
            yroll(qy, 1) - yroll(qy, -1),
            lroll(qz, -1) - lroll(qz, 1),
        )

    mg = mgrad(mpsi)
    mb = [msh(mini[i], DIRECTIONS[i]) for i in range(19)]
    mfb = cell(mb, mini[RHO], [mini[MOM + k] for k in range(3)], mpsi, mg)[5]
    mflux = [mpsi * v for v in mfb]

    def potential(p, _):
        v = 1.0 - jnp.exp(-ext[RHO, p])
        psi[p] = v
        a, b = zsh(v, mpsi, p, 1), zsh(v, mpsi, p, -1)
        zs[p] = a + b
        zd[p] = a - b
        return 0

    lax.fori_loop(0, nx + 4, potential, 0)

    def collide(p, own):
        v, xp, xm = psi[p], psi[p + 1], psi[p - 1]
        qxp = W1 * xp + W2 * (yroll(xp, 1) + yroll(xp, -1) + zs[p + 1])
        qxm = W1 * xm + W2 * (yroll(xm, 1) + yroll(xm, -1) + zs[p - 1])
        qy = W1 * v + W2 * (xp + xm + zs[p])
        zz = zd[p]
        g = (
            qxp - qxm,
            yroll(qy, 1) - yroll(qy, -1),
            W1 * zz + W2 * (zd[p + 1] + zd[p - 1] + yroll(zz, 1) + yroll(zz, -1)),
        )
        b = []
        for i in range(19):
            cx, cy, cz = DIRECTIONS[i]
            a = ext[i, p + cx]
            if cz:
                a = zsh(a, mini[i], p + cx, cz)
            b.append(yroll(a, cy))
        a0, a1, u, w, bf, fb = cell(b, ext[RHO, p], [ext[MOM + k, p] for k in range(3)], v, g)
        for k in range(3):
            flux[k, p] = v * fb[k]
        if own:
            top = lambda a: a[:16]
            vv = [top(INV_TAU * wk + bk) for wk, bk in zip(w, bf)]
            uu = [top(a) for a in u]
            base = INV_TAU * (top(a0) + 0.5 * dot([top(p_ + q_) for p_, q_ in zip(a1, w)], uu)) - dot(vv, uu)
            base = base + (-COUPLING * (1.0 - top(v))) * top(dot(fb, g))
            x = p - 2
            for i in range(19):
                o = (1.0 - INV_TAU) * top(b[i]) + base
                for k in range(3):
                    if DIRECTIONS[i][k] > 0:
                        o = o + vv[k]
                    elif DIRECTIONS[i][k] < 0:
                        o = o - vv[k]
                out[i, x] = o

    collide(1, False)
    collide(nx + 2, False)

    def own_plane(p, _):
        collide(p, True)
        return 0

    lax.fori_loop(2, nx + 2, own_plane, 0)

    def z_of_flux(p, _):
        fx, fy, fz = flux[0, p], flux[1, p], flux[2, p]
        sx = zsh(fx, mflux[0], p, 1) + zsh(fx, mflux[0], p, -1)
        zs[p] = W1 * fx + W2 * (yroll(fx, 1) + yroll(fx, -1) + sx)
        zd[p] = zsh(fz, mflux[2], p, 1) - zsh(fz, mflux[2], p, -1)
        return 0

    lax.fori_loop(1, nx + 3, z_of_flux, 0)

    def finish(p, _):
        fy = flux[1, p]
        sy = zsh(fy, mflux[1], p, 1) + zsh(fy, mflux[1], p, -1)
        qy = W1 * fy + W2 * (flux[1, p + 1] + flux[1, p - 1] + sy)
        zz = zd[p]
        div = (
            (zs[p + 1] - zs[p - 1])
            + (yroll(qy, 1) - yroll(qy, -1))
            + (W1 * zz + W2 * (zd[p + 1] + zd[p - 1] + yroll(zz, 1) + yroll(zz, -1)))
        )
        term = ((COUPLING * (1.0 - psi[p])) * div)[:16]
        x = p - 2
        for i in range(19):
            out[i, x] = out[i, x] + term
        pltpu.make_async_copy(out.at[:, x], out_hbm.at[:, x], sems.at[x]).start()
        return 0

    lax.fori_loop(2, nx + 2, finish, 0)
    for x in range(nx):
        pltpu.make_async_copy(out.at[:, x], out_hbm.at[:, x], sems.at[x]).wait()


def swap(low, high, axis):
    n = lax.axis_size(axis)
    up = [(i, (i + 1) % n) for i in range(n)]
    return lax.ppermute(low, axis, up), lax.ppermute(high, axis, [(j, i) for i, j in up])


def swap_both(msg, axis):
    n = lax.axis_size(axis)
    if n == 2:
        return lax.ppermute(msg, axis, [(0, 1), (1, 0)])
    return jnp.stack(swap(msg[0], msg[1], axis))


def per_device(populations, adjoint_next):
    nx = populations.shape[1]
    ext_shape, mini_shape = (FIELDS, nx + 4, ROWS, 128), (FIELDS, ROWS, 128)
    ext, mini, zlow, zhigh, xmsg = call(
        load_kernel,
        (populations, adjoint_next),
        (ext_shape, mini_shape, (3, 16, 128), (3, 16, 128), (2, 24, 16, 128)),
        scratch=[pltpu.VMEM((19, nx, 16, 128), F32), pltpu.SemaphoreType.DMA((38,))],
        in_specs=[HB, HB],
        name="load",
    )
    zlow, zhigh = swap(zlow, zhigh, "gz")
    x1 = swap_both(xmsg, "gx")
    mini, ylow, yhigh = call(
        zy_kernel,
        (ext, mini, zlow, zhigh),
        (mini_shape, (24 * 9, 128), (24 * 9, 128)),
        name="zy",
    )
    ylow, yhigh = swap(ylow, yhigh, "gy")
    ext, mini, xmsg2 = call(
        yx_kernel,
        (ext, mini, ylow, yhigh),
        (ext_shape, mini_shape, (2, 24 * 4 + 3 * ROWS, 128)),
        aliases={0: 0, 1: 1},
        name="yx",
    )
    x2 = swap_both(xmsg2, "gx")
    scratch = [
        pltpu.VMEM((nx + 4, ROWS, 128), F32),
        pltpu.VMEM((nx + 4, ROWS, 128), F32),
        pltpu.VMEM((nx + 4, ROWS, 128), F32),
        pltpu.VMEM((3, nx + 4, ROWS, 128), F32),
        pltpu.VMEM((19, nx, 16, 128), F32),
        pltpu.SemaphoreType.DMA((nx,)),
    ]

    def last(ext_in, mini_in, r1, r2, out_hbm, ext_out, mini_out, *rest):
        last_kernel(ext_in, mini_in, r1, r2, out_hbm, ext_out, mini_out, *rest)

    out, _, _ = call(
        last,
        (ext, mini, x1, x2),
        (populations.shape, ext_shape, mini_shape),
        scratch=scratch,
        aliases={0: 1, 1: 2},
        out_specs=[HB, VM, VM],
        name="last",
    )
    return out


def solution(mesh):
    return jax.shard_map(
        per_device,
        mesh=mesh,
        in_specs=(P(None, "gx", "gy", "gz"), P(None, "gx", "gy", "gz")),
        out_specs=P(None, "gx", "gy", "gz"),
        check_vma=False,
    )
```

time: 82.7 us -> 37.2 us (0.45)
  waiting for transfers between devices: 35.7 us -> 11 us
  other arithmetic: 19.9 us -> 0 us
  Pallas kernels: 0 us -> 14.2 us
  local copies, waits for them, and re-layouts: 14.5 us -> 2.59 us
  starting transfers between devices: 12.3 us -> 9.22 us
    ppermute x12 -> x6, waiting for transfers between devices: 35.7 us -> 11 us  [the longest x2 6.36 us: swap_both(): return lax.ppermute(msg, axis, [(0, 1), (1, 0)])]
    pallas_call x0 -> x4, Pallas kernels: none -> 14.2 us  [call(): pl.pallas_call(body, in_specs=in_specs or [VM] * len(ins), out_specs=out_...]
    slice x5 -> x0, local copies, waits for them, and re-layouts: 8.33 us -> none  [the longest x3 5.62 us: padded_2(): last = lax.slice_in_dim(value, length - width, length, axis=dim)]
    concatenate x5 -> x0, other arithmetic: 8.01 us -> none  [padded_2(): value = jnp.concatenate([before, value, after], axis=dim)]
    broadcast_in_dim x18 -> x0, other arithmetic: 6.27 us -> none  [the longest x3 3.21 us: collide(): moment = 0.5 * force_field[component]]
    ppermute x2 -> x0, local copies, waits for them, and re-layouts: 5.54 us -> none  [the longest x1 2.78 us: padded_2(): after = lax.ppermute(leading, axis, down)]
    add x1 -> x0, other arithmetic: 3.06 us -> none  [per_device(): return pop_bar + (potential_bar * decay_factor)[None]]
    ppermute x12 -> x6, starting transfers between devices: 12.3 us -> 9.22 us  [the longest x2 3.98 us: swap(): lax.ppermute(high, axis, [(j, i) for i, j in up])]
  transfers between devices with their start and end apart: 12 -> 6, of which waited for: 10 -> 4; matrix products, arithmetic and copies ran while one was open for 9% -> 0% of each run, Pallas kernels for 0% -> 1%
where the time goes in v1:
time: 37.2 us; the launch traced here: 37 us
  Pallas kernels  14.2 us (38%)
  waiting for transfers between devices  11 us (30%)
  starting transfers between devices  9.22 us (25%)
  local copies, waits for them, and re-layouts  2.59 us (7%)
    pallas_call x4, Pallas kernels, call(): pl.pallas_call(body, in_specs=in_specs or [VM] * len(ins), out_specs=out_...  14.2 us
    ppermute x2, waiting for transfers between devices, swap_both(): return lax.ppermute(msg, axis, [(0, 1), (1, 0)])  6.36 us
    ppermute x2, waiting for transfers between devices, swap(): lax.ppermute(low, axis, up)  4.38 us
    ppermute x2, starting transfers between devices, swap(): lax.ppermute(high, axis, [(j, i) for i, j in up])  3.98 us
    ppermute x2, starting transfers between devices, swap_both(): return lax.ppermute(msg, axis, [(0, 1), (1, 0)])  3.6 us
    unnamed x4, local copies, waits for them, and re-layouts  2.59 us
    ppermute x2, starting transfers between devices, swap(): lax.ppermute(low, axis, up)  1.63 us
  transfers between devices with their start and end apart: 6, of which 4 were waited for; matrix products, arithmetic and copies ran while one was open for 0% of the time, Pallas kernels for 1%

profile of v1, /device:TPU:0, one launch (start us, length us, event | category | flops | bytes accessed | tf_op | source)
XLA Modules:
  0.0 37.0 jit_solution(17723393971285297241)
XLA Ops:
  0.0 0.0 copy-start
  0.0 1.3 %copy-done = f32[19,8,16,128]{3,2,1,0:T(8,128)S(1)} copy-done((f32[19,8,16,128]{3,2,1,0:T(8,128)S(1)}, f32[19,8,16,128]{3,2,1,0:T(8,128)}, u32[]{:S(2)}) %copy-start) | copy-done | bytes 1245208
  1.3 0.0 copy-start.1
  1.3 1.3 %copy-done.1 = f32[19,8,16,128]{3,2,1,0:T(8,128)S(1)} copy-done((f32[19,8,16,128]{3,2,1,0:T(8,128)S(1)}, f32[19,8,16,128]{3,2,1,0:T(8,128)}, u32[]{:S(2)}) %copy-start.1) | copy-done | bytes 1245208
  2.6 6.0 %load.1 = (f32[23,12,24,128]{3,2,1,0:T(8,128)S(1)}, f32[23,24,128]{2,1,0:T(8,128)S(1)}, f32[3,16,128]{2,1,0:T(8,128)S(1)}, f32[3,16,128]{2,1,0:T(8,128)S(1)}, f32[2,24,16,128]{3,2,1,0:T(8,128)S(1)}) custom-call(f32[19,8,16,128]{3,2,1,0:T(8,128)S(1)} %copy-done, f32[19,8,16,128]{3,2,1,0:T(8,128)S(1)} %copy-done.1), custom_call_target="tpu_custom_call" | custom-call | tf_op jit(solution)/shard_map/load/pallas_call | solution.py:68
  8.6 3.0 %collective-permute-start.4 = (f32[2,24,16,128]{3,2,1,0:T(8,128)S(1)}, f32[2,24,16,128]{3,2,1,0:T(8,128)S(1)}, u32[]{:S(2)}, u32[]{:S(2)}) collective-permute-start(f32[2,24,16,128]{3,2,1,0:T(8,128)S(1)} %get-tuple-element.26), channel_id=1, source_target_pairs={{0,16},{16,0},{1,17},{17,1},{2,18},{18,2},{3,19},{19,3},{4,20},{20... | collective-permute-start | bytes 1179656 | tf_op jit(solution)/shard_map/ppermute | solution.py:372
  11.6 1.6 %collective-permute-start = (f32[3,16,128]{2,1,0:T(8,128)S(1)}, f32[3,16,128]{2,1,0:T(8,128)S(1)}, u32[]{:S(2)}, u32[]{:S(2)}) collective-permute-start(f32[3,16,128]{2,1,0:T(8,128)S(1)} %get-tuple-element.19), channel_id=1, source_target_pairs={{0,1},{1,2},{2,3},{3,0},{4,5},{5,6},{6,7},{7,4},{8,9},{9,10},{10,1... | collective-permute-start | bytes 73736 | tf_op jit(solution)/shard_map/ppermute | solution.py:366
  13.2 2.2 %collective-permute-start.1 = (f32[3,16,128]{2,1,0:T(8,128)S(1)}, f32[3,16,128]{2,1,0:T(8,128)S(1)}, u32[]{:S(2)}, u32[]{:S(2)}) collective-permute-start(f32[3,16,128]{2,1,0:T(8,128)S(1)} %get-tuple-element.20), channel_id=1, source_target_pairs={{1,0},{2,1},{3,2},{0,3},{5,4},{6,5},{7,6},{4,7},{9,8},{10,9},{11,1... | collective-permute-start | bytes 73736 | tf_op jit(solution)/shard_map/ppermute | solution.py:366
  15.4 2.0 %collective-permute-done.rlow = f32[3,16,128]{2,1,0:T(8,128)S(1)} collective-permute-done((f32[3,16,128]{2,1,0:T(8,128)S(1)}, f32[3,16,128]{2,1,0:T(8,128)S(1)}, u32[]{:S(2)}, u32[]{:S(2)}) %collective-permute-start) | collective-permute-done | bytes 24608 | tf_op jit(solution)/shard_map/ppermute | solution.py:366
  17.4 0.0 collective-permute-done.1.rhigh
  17.4 0.2 zy.1
  17.6 0.1 collective-permute-start.2
  17.6 1.7 %collective-permute-start.3 = (f32[216,128]{1,0:T(8,128)S(1)}, f32[216,128]{1,0:T(8,128)S(1)}, u32[]{:S(2)}, u32[]{:S(2)}) collective-permute-start(f32[216,128]{1,0:T(8,128)S(1)} %get-tuple-element.23), channel_id=1, source_target_pairs={{4,0},{8,4},{12,8},{0,12},{5,1},{9,5},{13,9},{1,13},{6,2},{10,6},{... | collective-permute-start | bytes 331784 | tf_op jit(solution)/shard_map/ppermute | solution.py:366
  19.4 2.4 %collective-permute-done.2.rlow = f32[216,128]{1,0:T(8,128)S(1)} collective-permute-done((f32[216,128]{1,0:T(8,128)S(1)}, f32[216,128]{1,0:T(8,128)S(1)}, u32[]{:S(2)}, u32[]{:S(2)}) %collective-permute-start.2) | collective-permute-done | bytes 110624 | tf_op jit(solution)/shard_map/ppermute | solution.py:366
  21.8 0.2 collective-permute-done.3.rhigh
  22.0 0.2 yx.1
  22.2 0.6 %collective-permute-start.5 = (f32[2,168,128]{2,1,0:T(8,128)S(1)}, f32[2,168,128]{2,1,0:T(8,128)S(1)}, u32[]{:S(2)}, u32[]{:S(2)}) collective-permute-start(f32[2,168,128]{2,1,0:T(8,128)S(1)} %get-tuple-element.27), channel_id=1, source_target_pairs={{0,16},{16,0},{1,17},{17,1},{2,18},{18,2},{3,19},{19,3},{4,20},{20... | collective-permute-start | bytes 516104 | tf_op jit(solution)/shard_map/ppermute | solution.py:372
  22.8 6.4 %collective-permute-done.5.r2 = f32[2,168,128]{2,1,0:T(8,128)S(1)} collective-permute-done((f32[2,168,128]{2,1,0:T(8,128)S(1)}, f32[2,168,128]{2,1,0:T(8,128)S(1)}, u32[]{:S(2)}, u32[]{:S(2)}) %collective-permute-start.5) | collective-permute-done | bytes 172064 | tf_op jit(solution)/shard_map/ppermute | solution.py:372
  29.2 0.0 collective-permute-done.4.r1
  29.2 7.8 %last.1 = (f32[19,8,16,128]{3,2,1,0:T(8,128)}, f32[23,12,24,128]{3,2,1,0:T(8,128)S(1)}, f32[23,24,128]{2,1,0:T(8,128)S(1)}) custom-call(f32[23,12,24,128]{3,2,1,0:T(8,128)S(1)} %get-tuple-element.24.ext_in, f32[23,24,128]{2,1,0:T(8,128)S(1)} %get-tuple-element.25.mini_in, ...), custom_call_target="tpu_custom_call", output_to_operand_aliasing={{1}: (0, {}), {2}: (1, {})} | custom-call | tf_op jit(solution)/shard_map/last/pallas_call | solution.py:68
Async XLA Ops:
  0.0 1.3 %copy-start = (f32[19,8,16,128]{3,2,1,0:T(8,128)S(1)}, f32[19,8,16,128]{3,2,1,0:T(8,128)}, u32[]{:S(2)}) copy-start(f32[19,8,16,128]{3,2,1,0:T(8,128)} %pop_hbm.1) | copy-start | bytes 3735556
  1.3 1.3 %copy-start.1 = (f32[19,8,16,128]{3,2,1,0:T(8,128)S(1)}, f32[19,8,16,128]{3,2,1,0:T(8,128)}, u32[]{:S(2)}) copy-start(f32[19,8,16,128]{3,2,1,0:T(8,128)} %adj_hbm.1) | copy-start | bytes 3735556
  8.6 20.6 %collective-permute-start.4 = (f32[2,24,16,128]{3,2,1,0:T(8,128)S(1)}, f32[2,24,16,128]{3,2,1,0:T(8,128)S(1)}, u32[]{:S(2)}, u32[]{:S(2)}) collective-permute-start(f32[2,24,16,128]{3,2,1,0:T(8,128)S(1)} %get-tuple-element.26), channel_id=1, source_target_pairs={{0,16},{16,0},{1,17},{17,1},{2,18},{18,2},{3,19},{19,3},{4,20},{20... | collective-permute-start | bytes 1179656 | tf_op jit(solution)/shard_map/ppermute | solution.py:372
  11.6 5.8 %collective-permute-start = (f32[3,16,128]{2,1,0:T(8,128)S(1)}, f32[3,16,128]{2,1,0:T(8,128)S(1)}, u32[]{:S(2)}, u32[]{:S(2)}) collective-permute-start(f32[3,16,128]{2,1,0:T(8,128)S(1)} %get-tuple-element.19), channel_id=1, source_target_pairs={{0,1},{1,2},{2,3},{3,0},{4,5},{5,6},{6,7},{7,4},{8,9},{9,10},{10,1... | collective-permute-start | bytes 73736 | tf_op jit(solution)/shard_map/ppermute | solution.py:366
  13.2 4.2 %collective-permute-start.1 = (f32[3,16,128]{2,1,0:T(8,128)S(1)}, f32[3,16,128]{2,1,0:T(8,128)S(1)}, u32[]{:S(2)}, u32[]{:S(2)}) collective-permute-start(f32[3,16,128]{2,1,0:T(8,128)S(1)} %get-tuple-element.20), channel_id=1, source_target_pairs={{1,0},{2,1},{3,2},{0,3},{5,4},{6,5},{7,6},{4,7},{9,8},{10,9},{11,1... | collective-permute-start | bytes 73736 | tf_op jit(solution)/shard_map/ppermute | solution.py:366
  17.6 4.2 %collective-permute-start.2 = (f32[216,128]{1,0:T(8,128)S(1)}, f32[216,128]{1,0:T(8,128)S(1)}, u32[]{:S(2)}, u32[]{:S(2)}) collective-permute-start(f32[216,128]{1,0:T(8,128)S(1)} %get-tuple-element.22), channel_id=1, source_target_pairs={{0,4},{4,8},{8,12},{12,0},{1,5},{5,9},{9,13},{13,1},{2,6},{6,10},{... | collective-permute-start | bytes 331784 | tf_op jit(solution)/shard_map/ppermute | solution.py:366
  17.6 4.4 %collective-permute-start.3 = (f32[216,128]{1,0:T(8,128)S(1)}, f32[216,128]{1,0:T(8,128)S(1)}, u32[]{:S(2)}, u32[]{:S(2)}) collective-permute-start(f32[216,128]{1,0:T(8,128)S(1)} %get-tuple-element.23), channel_id=1, source_target_pairs={{4,0},{8,4},{12,8},{0,12},{5,1},{9,5},{13,9},{1,13},{6,2},{10,6},{... | collective-permute-start | bytes 331784 | tf_op jit(solution)/shard_map/ppermute | solution.py:366
  22.2 7.0 %collective-permute-start.5 = (f32[2,168,128]{2,1,0:T(8,128)S(1)}, f32[2,168,128]{2,1,0:T(8,128)S(1)}, u32[]{:S(2)}, u32[]{:S(2)}) collective-permute-start(f32[2,168,128]{2,1,0:T(8,128)S(1)} %get-tuple-element.27), channel_id=1, source_target_pairs={{0,16},{16,0},{1,17},{17,1},{2,18},{18,2},{3,19},{19,3},{4,20},{20... | collective-permute-start | bytes 516104 | tf_op jit(solution)/shard_map/ppermute | solution.py:372

commit v2 on v1

v2 whole, which is shorter than its diff:
```python
import jax
import jax.numpy as jnp
from jax import lax
from jax.experimental import pallas as pl
from jax.experimental.pallas import tpu as pltpu
from jax.sharding import PartitionSpec as P

DIRECTIONS = (
    (0, 0, 0),
    (1, 0, 0),
    (-1, 0, 0),
    (0, 1, 0),
    (0, -1, 0),
    (0, 0, 1),
    (0, 0, -1),
    (1, 1, 0),
    (-1, -1, 0),
    (1, -1, 0),
    (-1, 1, 0),
    (1, 0, 1),
    (-1, 0, -1),
    (1, 0, -1),
    (-1, 0, 1),
    (0, 1, 1),
    (0, -1, -1),
    (0, 1, -1),
    (0, -1, 1),
)
W0, W1, W2 = 1.0 / 3.0, 1.0 / 18.0, 1.0 / 36.0
RELAX_TIME = 0.8
COUPLING = -5.5
INV_TAU = 1.0 / RELAX_TIME
KAPPA = 1.0 - 0.5 / RELAX_TIME

RHO, MOM, FIELDS = 19, 20, 23
ROWS = 24
F32 = jnp.float32
VM = pl.BlockSpec(memory_space=pltpu.VMEM)
HB = pl.BlockSpec(memory_space=pltpu.HBM)


def deep_fields(dim, side):
    return [i for i in range(19) if DIRECTIONS[i][dim] == side] + [RHO]


def side_fields(dim, side):
    return deep_fields(dim, side) + [i for i in range(19) if DIRECTIONS[i][dim] == 0] + [MOM, MOM + 1, MOM + 2]


def side_entries(dim, side):
    return [(f, d) for d in (0, 1) for f in (side_fields(dim, side) if d == 0 else deep_fields(dim, side))]


def edge_entries(side):
    found = []
    for up in (-1, 1):
        for dx in (0, 1):
            for dy in (0, 1):
                row = 23 - dy if up < 0 else 16 + dy
                across = deep_fields(0, side) if dx else side_fields(0, side)
                along = deep_fields(1, up) if dy else side_fields(1, up)
                found += [(f, dx, row) for f in across if f in along]
    return found


EDGE_LINES = -(-len(edge_entries(1)) // 8) * 8


def is_odd(axis, rows):
    return jnp.full((rows, 128), lax.axis_index(axis) % 2, jnp.int32) == 1


def lane_ids(rows):
    return lax.broadcasted_iota(jnp.int32, (rows, 128), 1)


def lroll(v, amount):
    amount = amount % 128
    return v if isinstance(amount, int) and amount == 0 else pltpu.roll(v, amount, 1)


def yroll(v, c):
    return v if c == 0 else pltpu.roll(v, (-c) % ROWS, 0)


def call(body, ins, outs, scratch=(), aliases=None, name=None, in_specs=None, out_specs=None):
    return pl.pallas_call(
        body,
        in_specs=in_specs or [VM] * len(ins),
        out_specs=out_specs or [VM] * len(outs),
        out_shape=[jax.ShapeDtypeStruct(s, F32) for s in outs],
        scratch_shapes=list(scratch),
        input_output_aliases=aliases or {},
        name=name,
        compiler_params=pltpu.CompilerParams(vmem_limit_bytes=20 * 2**20),
    )(*ins)


def load_kernel(pop_hbm, adj_hbm, ext, mini, za, zb, pops, sems):
    nx = pop_hbm.shape[1]
    lane = lane_ids(16)
    group = lane // 4
    chunks = [(f, min(4, 19 - f)) for f in range(0, 19, 4)]
    copies = []
    for k, (f, n) in enumerate(chunks):
        own = ext.at[pl.ds(f, n), pl.ds(2, nx), pl.ds(0, 16), :]
        copies.append(pltpu.make_async_copy(adj_hbm.at[pl.ds(f, n)], own, sems.at[k]))
    for k, (f, n) in enumerate(chunks):
        copies.append(pltpu.make_async_copy(pop_hbm.at[pl.ds(f, n)], pops.at[pl.ds(f, n)], sems.at[5 + k]))
    for c in copies:
        c.start()

    def edges(f):
        e = lroll(ext[f, 2, pl.ds(0, 16), :], 10)
        for x in range(1, nx):
            e = jnp.where(group == x + 2, lroll(ext[f, x + 2, pl.ds(0, 16), :], 4 * x + 10), e)
        mini[f, pl.ds(0, 16), :] = e

    for k, (f, n) in enumerate(chunks):
        copies[k].wait()
        for i in range(n):
            edges(f + i)
    for c in copies[5:]:
        c.wait()

    def moments(x, _):
        rho = pops[0, x]
        mom = [None] * 3
        for i in range(1, 19):
            p = pops[i, x]
            rho = rho + p
            for k in range(3):
                c = DIRECTIONS[i][k]
                if c:
                    mom[k] = (p if c > 0 else -p) if mom[k] is None else (mom[k] + p if c > 0 else mom[k] - p)
        ext[RHO, x + 2, pl.ds(0, 16), :] = rho
        for k in range(3):
            ext[MOM + k, x + 2, pl.ds(0, 16), :] = mom[k]
        return 0

    lax.fori_loop(0, nx, moments, 0, unroll=2)
    for f in range(RHO, FIELDS):
        edges(f)
    odd = is_odd("gz", 16)
    for t in range(za.shape[0]):
        made = []
        for side in (-1, 1):
            fields = side_fields(2, side)
            acc = None
            for j in range(8 * t, min(8 * t + 8, len(fields))):
                q = j % 8
                b, p = q // 2, q % 2
                v = lroll(mini[fields[j], pl.ds(0, 16), :], 32 * b + 2 * p - (8 if side < 0 else 10))
                acc = v if acc is None else jnp.where((lane // 32 == b) & ((lane % 4) // 2 == p), v, acc)
            made.append(acc)
        za[t] = jnp.where(odd, made[0], made[1])
        zb[t] = jnp.where(odd, made[1], made[0])


def x_kernel(ext, xmsg):
    nx = ext.shape[1] - 4
    for s, side in enumerate((-1, 1)):
        for e, (f, d) in enumerate(side_entries(0, side)):
            plane = (nx + 1 - d) if side < 0 else (2 + d)
            xmsg[s, e] = lroll(ext[f, plane, pl.ds(0, 16), :], -DIRECTIONS[f][2] if f < 19 else 0)


def turn_kernel(ext_in, ext):
    nx = ext.shape[1] - 4
    moving = [i for i in range(19) if DIRECTIONS[i][2]]

    def plane(p, _):
        turned = [lroll(ext_in[i, p, pl.ds(0, 16), :], -DIRECTIONS[i][2]) for i in moving]
        for i, v in zip(moving, turned):
            ext[i, p, pl.ds(0, 16), :] = v
        return 0

    lax.fori_loop(2, nx + 2, plane, 0)


Z_PAIRS = ((5, 6), (11, 13), (14, 12), (15, 17), (18, 16))


def z_ends(above, below):
    return jnp.where(lane_ids(above.shape[0]) % 4 == 0, lroll(above, 62), below)


def close_pairs(p, pairs, ends, ext):
    lane = lane_ids(16)
    found = []
    for (up, down), e in zip(pairs, ends):
        g = lroll(e, 255 - 4 * p)
        found.append((up, jnp.where(lane == 127, g, ext[up, p, pl.ds(0, 16), :])))
        found.append((down, jnp.where(lane == 0, g, ext[down, p, pl.ds(0, 16), :])))
    return found


def zy_kernel(ext_in, mini_in, ra, rb, ext, mini, ya, yb, ends):
    nx = ext.shape[1] - 4
    lane = lane_ids(16)
    for f in range(FIELDS):
        e = mini_in[f, pl.ds(0, 16), :]
        if f == RHO or (f < 19 and DIRECTIONS[f][2] < 0):
            e = jnp.where(lane < 64, e, lroll(e, 64))
        mini[f, pl.ds(0, 16), :] = e
    odd = is_odd("gz", 16)
    for side in (-1, 1):
        msg = [jnp.where(odd, rb[t], ra[t]) if side < 0 else jnp.where(odd, ra[t], rb[t]) for t in range(ra.shape[0])]
        if side < 0:
            keep = (lane >= 8) & (lane < 40) & (lane % 4 < 2)
        else:
            keep = (lane >= 72) & (lane < 104) & (lane % 4 >= 2)
        for j, f in enumerate(side_fields(2, side)):
            q = j % 8
            b, p = q // 2, q % 2
            back = 8 - 32 * b - 2 * p if side < 0 else 74 - 32 * b - 2 * p
            mini[f, pl.ds(0, 16), :] = jnp.where(keep, lroll(msg[j // 8], back), mini[f, pl.ds(0, 16), :])
    for k, (up, down) in enumerate(Z_PAIRS):
        ends[k] = z_ends(mini[up, pl.ds(0, 16), :], mini[down, pl.ds(0, 16), :])

    def close(p, _):
        closed = close_pairs(p, Z_PAIRS, [ends[k] for k in range(len(Z_PAIRS))], ext_in)
        for f, v in closed:
            ext[f, p, pl.ds(0, 16), :] = v
        return 0

    lax.fori_loop(2, nx + 2, close, 0)
    odd = is_odd("gy", 8)
    low, high = side_entries(1, -1), side_entries(1, 1)
    for e in range(len(low)):
        v = ext[low[e][0], pl.ds(2, 8), 15 - low[e][1], :]
        w = ext[high[e][0], pl.ds(2, 8), high[e][1], :]
        ya[pl.ds(8 * e, 8), :] = jnp.where(odd, v, w)
        yb[pl.ds(8 * e, 8), :] = jnp.where(odd, w, v)
    odd = is_odd("gy", 1)
    for e in range(len(low)):
        v = mini[low[e][0], pl.ds(15 - low[e][1], 1), :]
        w = mini[high[e][0], pl.ds(high[e][1], 1), :]
        ya[pl.ds(8 * len(low) + e, 1), :] = jnp.where(odd, v, w)
        yb[pl.ds(8 * len(low) + e, 1), :] = jnp.where(odd, w, v)


def yx_kernel(ext_in, mini_in, ra, rb, ext, mini, xmsg):
    lane = lane_ids(ROWS)
    odd8, odd1 = is_odd("gy", 8), is_odd("gy", 1)
    for side in (-1, 1):
        first, second = (rb, ra) if side < 0 else (ra, rb)
        entries = side_entries(1, side)
        for e, (f, d) in enumerate(entries):
            row = 23 - d if side < 0 else 16 + d
            main, small = pl.ds(8 * e, 8), pl.ds(8 * len(entries) + e, 1)
            ext[f, pl.ds(2, 8), row, :] = jnp.where(odd8, first[main, :], second[main, :])
            mini[f, pl.ds(row, 1), :] = jnp.where(odd1, first[small, :], second[small, :])
    group = (lane % 64) // 4
    for s, side in enumerate((-1, 1)):
        for e, (f, dx, row) in enumerate(edge_entries(side)):
            plane = 9 - dx if side < 0 else 2 + dx
            xmsg[s, pl.ds(e, 1), :] = ext[f, plane, pl.ds(row, 1), :]
        entries = side_entries(0, side)
        for t in range(2):
            acc = None
            for e in range(16 * t, min(16 * t + 16, len(entries))):
                f, d = entries[e]
                v = lroll(mini[f], 4 * (e % 16) - 4 * (9 - d if side < 0 else 2 + d))
                acc = v if acc is None else jnp.where(group == e % 16, v, acc)
            xmsg[s, pl.ds(EDGE_LINES + ROWS * t, ROWS), :] = acc


def cell(b, rho, mom, psi, g):
    pairs = {}
    for i in range(1, 19, 2):
        pairs[i] = (b[i] + b[i + 1], b[i] - b[i + 1])
    s = {i: v[0] for i, v in pairs.items()}
    d = {i: v[1] for i, v in pairs.items()}
    sxy, sxz, syz = s[7] + s[9], s[11] + s[13], s[15] + s[17]
    a0 = W0 * b[0] + W1 * (s[1] + s[3] + s[5]) + W2 * (sxy + sxz + syz)
    a1 = (
        (3 * W1) * d[1] + (3 * W2) * ((d[7] + d[9]) + (d[11] + d[13])),
        (3 * W1) * d[3] + (3 * W2) * ((d[7] - d[9]) + (d[15] + d[17])),
        (3 * W1) * d[5] + (3 * W2) * ((d[11] - d[13]) + (d[15] - d[17])),
    )
    a03 = 3.0 * a0
    bxx = (9 * W1) * s[1] + (9 * W2) * (sxy + sxz) - a03
    byy = (9 * W1) * s[3] + (9 * W2) * (sxy + syz) - a03
    bzz = (9 * W1) * s[5] + (9 * W2) * (sxz + syz) - a03
    bxy = (9 * W2) * (s[7] - s[9])
    bxz = (9 * W2) * (s[11] - s[13])
    byz = (9 * W2) * (s[15] - s[17])
    force = [(-COUPLING * psi) * gk for gk in g]
    inv = 1.0 / rho
    u = [(m + 0.5 * fk) * inv for m, fk in zip(mom, force)]

    def apply(v):
        return (
            bxx * v[0] + bxy * v[1] + bxz * v[2],
            bxy * v[0] + byy * v[1] + byz * v[2],
            bxz * v[0] + byz * v[1] + bzz * v[2],
        )

    w = [p + q for p, q in zip(a1, apply(u))]
    bf = [(KAPPA * inv) * q for q in apply(force)]
    force_bar = [p + 0.5 * q for p, q in zip(w, bf)]
    return a0, a1, u, w, bf, force_bar


def dot(p, q):
    return p[0] * q[0] + p[1] * q[1] + p[2] * q[2]


def mini_adjoint(mini):
    def msh(v, c):
        return lroll(yroll(v, c[1]), -4 * c[0] - c[2])

    psi = 1.0 - jnp.exp(-mini[RHO])
    ys = yroll(psi, 1) + yroll(psi, -1)
    zsum = lroll(psi, -1) + lroll(psi, 1)
    xsum = lroll(psi, -4) + lroll(psi, 4)
    qx = W1 * psi + W2 * (ys + zsum)
    qy = W1 * psi + W2 * (xsum + zsum)
    qz = W1 * psi + W2 * (xsum + ys)
    g = (lroll(qx, -4) - lroll(qx, 4), yroll(qy, 1) - yroll(qy, -1), lroll(qz, -1) - lroll(qz, 1))
    b = [msh(mini[i], DIRECTIONS[i]) for i in range(19)]
    force_bar = cell(b, mini[RHO], [mini[MOM + k] for k in range(3)], psi, g)[5]
    fx, fy, fz = (psi * v for v in force_bar)
    across = W2 * ((lroll(fx, -4) - lroll(fx, 4)) + (yroll(fy, 1) - yroll(fy, -1)))
    along = W1 * fz + W2 * ((lroll(fz, -4) + lroll(fz, 4)) + (yroll(fz, 1) + yroll(fz, -1)))
    return z_ends(psi, psi), z_ends(across + along, across - along)


def zpair(above, below, ends, plane):
    lane = lane_ids(above.shape[0])
    g = lroll(ends, 255 - 4 * plane)
    return jnp.where(lane == 127, g, lroll(above, 127)), jnp.where(lane == 0, g, lroll(below, 1))


def potential(p, ext, ends, psi, zs, zd):
    v = 1.0 - jnp.exp(-ext[RHO, p])
    psi[p] = v
    a, b = zpair(v, v, ends, p)
    zs[p] = a + b
    zd[p] = a - b


def collide(p, ext, psi, zs, zd, flux, out):
    v, xp, xm = psi[p], psi[p + 1], psi[p - 1]
    qxp = W1 * xp + W2 * (yroll(xp, 1) + yroll(xp, -1) + zs[p + 1])
    qxm = W1 * xm + W2 * (yroll(xm, 1) + yroll(xm, -1) + zs[p - 1])
    qy = W1 * v + W2 * (xp + xm + zs[p])
    zz = zd[p]
    g = (
        qxp - qxm,
        yroll(qy, 1) - yroll(qy, -1),
        W1 * zz + W2 * (zd[p + 1] + zd[p - 1] + yroll(zz, 1) + yroll(zz, -1)),
    )
    b = [yroll(ext[i, p + DIRECTIONS[i][0]], DIRECTIONS[i][1]) for i in range(19)]
    a0, a1, u, w, bf, fb = cell(b, ext[RHO, p], [ext[MOM + k, p] for k in range(3)], v, g)
    for k in range(3):
        flux[k, p] = v * fb[k]

    def top(a):
        return a[:16]

    vv = [top(INV_TAU * wk + bk) for wk, bk in zip(w, bf)]
    uu = [top(a) for a in u]
    base = INV_TAU * (top(a0) + 0.5 * dot([top(r + q) for r, q in zip(a1, w)], uu)) - dot(vv, uu)
    base = base + (-COUPLING * (1.0 - top(v))) * top(dot(fb, g))
    for i in range(19):
        o = (1.0 - INV_TAU) * top(b[i]) + base
        for k in range(3):
            if DIRECTIONS[i][k] > 0:
                o = o + vv[k]
            elif DIRECTIONS[i][k] < 0:
                o = o - vv[k]
        out[i, p - 1] = o


def finish(p, psi, flux, ends, out):
    fx, fxm, fy = flux[0, p + 1], flux[0, p - 1], flux[1, p]
    fz = flux[2, p]
    xd = fx - fxm
    fyx = flux[1, p + 1] + flux[1, p - 1]
    dx = xd[:16]
    dy = (yroll(fy, 1) - yroll(fy, -1))[:16]
    here = W1 * (dx + dy) + W2 * (
        (yroll(xd, 1) + yroll(xd, -1))[:16] + (yroll(fyx, 1) - yroll(fyx, -1))[:16]
    )
    across = W2 * (dx + dy)
    along = W1 * fz[:16] + W2 * (flux[2, p + 1, pl.ds(0, 16), :] + flux[2, p - 1, pl.ds(0, 16), :] + (yroll(fz, 1) + yroll(fz, -1))[:16])
    a, b = zpair(across + along, across - along, ends[:16], p)
    term = (COUPLING * (1.0 - psi[p, pl.ds(0, 16), :])) * (here + (a + b))
    for i in range(19):
        out[i, p - 1] = out[i, p - 1] + term


def planes(count, of, step):
    def body(k, _):
        step(of(k))
        return 0

    lax.fori_loop(0, count, body, 0)


def send_plane(out, out_hbm, sems, p):
    return pltpu.make_async_copy(out.at[:, p - 1], out_hbm.at[:, p - 2], sems.at[p - 2])


def mid_kernel(ext, mini, out_hbm, psi, zs, zd, flux, out, sems):
    nx = ext.shape[1] - 4
    psi_ends, flux_ends = mini_adjoint(mini)
    for p in range(2, nx + 2):
        potential(p, ext, psi_ends, psi, zs, zd)
    planes(nx - 2, lambda k: k + 3, lambda p: collide(p, ext, psi, zs, zd, flux, out))

    def done(p):
        finish(p, psi, flux, flux_ends, out)
        send_plane(out, out_hbm, sems, p).start()

    planes(nx - 4, lambda k: k + 4, done)
    for p in range(4, nx):
        send_plane(out, out_hbm, sems, p).wait()


def last_kernel(ext_in, mini_in, r1, r2, psi_in, zs_in, zd_in, flux_in, out_in, hbm_in, ext, mini, psi, zs, zd, flux, out, out_hbm, sems):
    nx = ext.shape[1] - 4
    lane = lane_ids(ROWS)
    group = (lane % 64) // 4
    for s, side in enumerate((-1, 1)):
        entries = side_entries(0, side)
        for e, (f, d) in enumerate(entries):
            plane = 1 - d if side < 0 else nx + 2 + d
            ext[f, plane, pl.ds(0, 16), :] = r1[s, e]
            v = r2[s, pl.ds(EDGE_LINES + ROWS * (e // 16), ROWS), :]
            mini[f] = jnp.where(group == plane, lroll(v, 4 * plane - 4 * (e % 16)), mini[f])
        for e, (f, dx, row) in enumerate(edge_entries(side)):
            plane = 1 - dx if side < 0 else nx + 2 + dx
            ext[f, plane, pl.ds(row, 1), :] = r2[s, pl.ds(e, 1), :]
    ends = [z_ends(mini[up, pl.ds(0, 16), :], mini[down, pl.ds(0, 16), :]) for up, down in Z_PAIRS]
    for p in (0, 1, nx + 2, nx + 3):
        keep = [k for k, (f, _) in enumerate(Z_PAIRS) if DIRECTIONS[f][0] == (-1 if p < 2 else 1) or (p in (1, nx + 2) and DIRECTIONS[f][0] == 0)]
        for f, v in close_pairs(p, [Z_PAIRS[k] for k in keep], [ends[k] for k in keep], ext):
            ext[f, p, pl.ds(0, 16), :] = v
    psi_ends, flux_ends = mini_adjoint(mini)
    for p in (0, 1, nx + 2, nx + 3):
        potential(p, ext, psi_ends, psi, zs, zd)

    def outer(low, k):
        return low + k + jnp.where(k >= 2, nx - 2, 0)

    planes(4, lambda k: outer(1, k), lambda p: collide(p, ext, psi, zs, zd, flux, out))

    def done(p):
        finish(p, psi, flux, flux_ends, out)
        send_plane(out, out_hbm, sems, p).start()

    planes(4, lambda k: outer(2, k) - jnp.where(k >= 2, 2, 0), done)
    for p in (2, 3, nx, nx + 1):
        send_plane(out, out_hbm, sems, p).wait()


def swap(low, high, axis):
    n = lax.axis_size(axis)
    up = [(i, (i + 1) % n) for i in range(n)]
    return lax.ppermute(low, axis, up), lax.ppermute(high, axis, [(j, i) for i, j in up])


def exchange(a, b, axis):
    n = lax.axis_size(axis)
    swaps = [[], []]
    for i in range(n):
        j = (i + 1) % n
        swaps[1 - i % 2] += [(i, j), (j, i)]
    return lax.ppermute(a, axis, swaps[0]), lax.ppermute(b, axis, swaps[1])


def swap_both(msg, axis):
    n = lax.axis_size(axis)
    if n == 2:
        return lax.ppermute(msg, axis, [(0, 1), (1, 0)])
    return jnp.stack(swap(msg[0], msg[1], axis))


def per_device(populations, adjoint_next):
    nx = populations.shape[1]
    ext_shape, mini_shape, plane_shape = (FIELDS, nx + 4, ROWS, 128), (FIELDS, ROWS, 128), (nx + 4, ROWS, 128)
    ext, mini, za, zb = call(
        load_kernel,
        tuple(pltpu.with_memory_space_constraint(v, pltpu.HBM) for v in (populations, adjoint_next)),
        (ext_shape, mini_shape, (3, 16, 128), (3, 16, 128)),
        scratch=[pltpu.VMEM((19, nx, 16, 128), F32), pltpu.SemaphoreType.DMA((10,))],
        in_specs=[HB, HB],
        name="load",
    )
    (xmsg,) = call(x_kernel, (ext,), ((2, 24, 16, 128),), name="xpack")
    x1 = swap_both(xmsg, "gx")
    za, zb = exchange(za, zb, "gz")
    (ext,) = call(turn_kernel, (ext,), (ext_shape,), aliases={0: 0}, name="turn")
    ext, mini, ya, yb = call(
        zy_kernel,
        (ext, mini, za, zb),
        (ext_shape, mini_shape, (24 * 9, 128), (24 * 9, 128)),
        scratch=[pltpu.VMEM((len(Z_PAIRS), 16, 128), F32)],
        aliases={0: 0, 1: 1},
        name="zy",
    )
    ya, yb = exchange(ya, yb, "gy")
    ext, mini, xmsg2 = call(
        yx_kernel,
        (ext, mini, ya, yb),
        (ext_shape, mini_shape, (2, EDGE_LINES + 2 * ROWS, 128)),
        aliases={0: 0, 1: 1},
        name="yx",
    )
    x2 = swap_both(xmsg2, "gx")
    work = (plane_shape, plane_shape, plane_shape, (3, *plane_shape), (19, nx + 2, 16, 128))
    out, *parts = call(
        mid_kernel,
        (ext, mini),
        (populations.shape, *work),
        scratch=[pltpu.SemaphoreType.DMA((nx,))],
        out_specs=[HB] + [VM] * len(work),
        name="mid",
    )
    return call(
        last_kernel,
        (ext, mini, x1, x2, *parts, out),
        (ext_shape, mini_shape, *work, populations.shape),
        scratch=[pltpu.SemaphoreType.DMA((nx,))],
        aliases={0: 0, 1: 1, **{4 + i: 2 + i for i in range(len(work) + 1)}},
        in_specs=[VM] * (4 + len(work)) + [HB],
        out_specs=[VM] * (2 + len(work)) + [HB],
        name="last",
    )[-1]


def solution(mesh):
    return jax.shard_map(
        per_device,
        mesh=mesh,
        in_specs=(P(None, "gx", "gy", "gz"), P(None, "gx", "gy", "gz")),
        out_specs=P(None, "gx", "gy", "gz"),
        check_vma=False,
    )
```

time: 37.2 us -> 26.7 us (0.72)
  Pallas kernels: 14.2 us -> 8.6 us
  local copies, waits for them, and re-layouts: 2.59 us -> 0 us
  waiting for transfers between devices: 11 us -> 9.01 us
    pallas_call x4 -> x7, Pallas kernels: 14.2 us -> 8.6 us  [call(): pl.pallas_call(body, in_specs=in_specs or [VM] * len(ins), out_specs=out_...]
    ppermute x2, waiting for transfers between devices: 6.36 us -> 2.24 us  [swap_both(): return lax.ppermute(msg, axis, [(0, 1), (1, 0)])]
    unnamed x4 -> x0, local copies, waits for them, and re-layouts: 2.59 us -> none
    ppermute x4, waiting for transfers between devices: 4.61 us -> 6.77 us  [exchange(): return (lax.ppermute(a, axis, swaps[0]), lax.ppermute(b, axis, swaps[1]))]
  transfers between devices with their start and end apart: 6 -> 6, of which waited for: 4 -> 4; matrix products, arithmetic and copies ran while one was open for 0% -> 0% of each run, Pallas kernels for 1% -> 16%
where the time goes in v2:
time: 26.7 us; the launch traced here: 26.6 us
  waiting for transfers between devices  9.01 us (34%)
  starting transfers between devices  8.9 us (33%)
  Pallas kernels  8.6 us (32%)
    pallas_call x7, Pallas kernels, call(): pl.pallas_call(body, in_specs=in_specs or [VM] * len(ins), out_specs=out_...  8.6 us
    ppermute x4, waiting for transfers between devices, exchange(): return (lax.ppermute(a, axis, swaps[0]), lax.ppermute(b, axis, swaps[1]))  6.77 us
    ppermute x4, starting transfers between devices, exchange(): return (lax.ppermute(a, axis, swaps[0]), lax.ppermute(b, axis, swaps[1]))  5.3 us
    ppermute x2, starting transfers between devices, swap_both(): return lax.ppermute(msg, axis, [(0, 1), (1, 0)])  3.6 us
    ppermute x2, waiting for transfers between devices, swap_both(): return lax.ppermute(msg, axis, [(0, 1), (1, 0)])  2.24 us
  transfers between devices with their start and end apart: 6, of which 4 were waited for; matrix products, arithmetic and copies ran while one was open for 0% of the time, Pallas kernels for 16%

profile of v2, /device:TPU:0, one launch (start us, length us, event | category | flops | bytes accessed | tf_op | source)
XLA Modules:
  0.0 26.6 jit_solution(5964586467971417330)
XLA Ops:
  0.0 2.1 %load.1 = (f32[23,12,24,128]{3,2,1,0:T(8,128)S(1)}, f32[23,24,128]{2,1,0:T(8,128)S(1)}, f32[3,16,128]{2,1,0:T(8,128)S(1)}, f32[3,16,128]{2,1,0:T(8,128)S(1)}) custom-call(f32[19,8,16,128]{3,2,1,0:T(8,128)} %pop_hbm.1, f32[19,8,16,128]{3,2,1,0:T(8,128)} %adj_hbm.1), custom_call_target="tpu_custom_call" | custom-call | tf_op jit(solution)/shard_map/load/pallas_call | solution.py:87
  2.1 0.1 xpack.1
  2.2 3.0 %collective-permute-start.4 = (f32[2,24,16,128]{3,2,1,0:T(8,128)S(1)}, f32[2,24,16,128]{3,2,1,0:T(8,128)S(1)}, u32[]{:S(2)}, u32[]{:S(2)}) collective-permute-start(f32[2,24,16,128]{3,2,1,0:T(8,128)S(1)} %xpack.1), channel_id=1, source_target_pairs={{0,16},{16,0},{1,17},{17,1},{2,18},{18,2},{3,19},{19,3},{4,20},{20... | collective-permute-start | bytes 1179656 | tf_op jit(solution)/shard_map/ppermute | solution.py:478
  5.2 3.6 %collective-permute-start = (f32[3,16,128]{2,1,0:T(8,128)S(1)}, f32[3,16,128]{2,1,0:T(8,128)S(1)}, u32[]{:S(2)}, u32[]{:S(2)}) collective-permute-start(f32[3,16,128]{2,1,0:T(8,128)S(1)} %get-tuple-element.25), channel_id=1, source_target_pairs={{1,2},{2,1},{3,0},{0,3},{5,6},{6,5},{7,4},{4,7},{9,10},{10,9},{11,... | collective-permute-start | bytes 73736 | tf_op jit(solution)/shard_map/ppermute | solution.py:472
  8.8 0.0 collective-permute-start.1
  8.8 0.7 %turn.1.ext_in = f32[23,12,24,128]{3,2,1,0:T(8,128)S(1)} custom-call(f32[23,12,24,128]{3,2,1,0:T(8,128)S(1)} %get-tuple-element.23.ext_in.ext), custom_call_target="tpu_custom_call", output_to_operand_aliasing={{}: (0, {})} | custom-call | tf_op jit(solution)/shard_map/turn/pallas_call | solution.py:87
  9.5 1.3 %collective-permute-done.ra = f32[3,16,128]{2,1,0:T(8,128)S(1)} collective-permute-done((f32[3,16,128]{2,1,0:T(8,128)S(1)}, f32[3,16,128]{2,1,0:T(8,128)S(1)}, u32[]{:S(2)}, u32[]{:S(2)}) %collective-permute-start) | collective-permute-done | bytes 24608 | tf_op jit(solution)/shard_map/ppermute | solution.py:472
  10.8 1.8 %collective-permute-done.1.rb = f32[3,16,128]{2,1,0:T(8,128)S(1)} collective-permute-done((f32[3,16,128]{2,1,0:T(8,128)S(1)}, f32[3,16,128]{2,1,0:T(8,128)S(1)}, u32[]{:S(2)}, u32[]{:S(2)}) %collective-permute-start.1) | collective-permute-done | bytes 24608 | tf_op jit(solution)/shard_map/ppermute | solution.py:472
  12.6 1.0 %zy.1 = (f32[23,12,24,128]{3,2,1,0:T(8,128)S(1)}, f32[23,24,128]{2,1,0:T(8,128)S(1)}, f32[216,128]{1,0:T(8,128)S(1)}, f32[216,128]{1,0:T(8,128)S(1)}) custom-call(f32[23,12,24,128]{3,2,1,0:T(8,128)S(1)} %turn.1.ext_in, f32[23,24,128]{2,1,0:T(8,128)S(1)} %get-tuple-element.24.mini_in, ...), custom_call_target="tpu_custom_call", output_to_operand_aliasing={{0}: (0, {}), {1}: (1, {})} | custom-call | tf_op jit(solution)/shard_map/zy/pallas_call | solution.py:87
  13.6 0.1 collective-permute-start.2
  13.7 1.6 %collective-permute-start.3 = (f32[216,128]{1,0:T(8,128)S(1)}, f32[216,128]{1,0:T(8,128)S(1)}, u32[]{:S(2)}, u32[]{:S(2)}) collective-permute-start(f32[216,128]{1,0:T(8,128)S(1)} %get-tuple-element.30), channel_id=1, source_target_pairs={{0,4},{4,0},{8,12},{12,8},{1,5},{5,1},{9,13},{13,9},{2,6},{6,2},{1... | collective-permute-start | bytes 331784 | tf_op jit(solution)/shard_map/ppermute | solution.py:472
  15.3 3.6 %collective-permute-done.2.ra = f32[216,128]{1,0:T(8,128)S(1)} collective-permute-done((f32[216,128]{1,0:T(8,128)S(1)}, f32[216,128]{1,0:T(8,128)S(1)}, u32[]{:S(2)}, u32[]{:S(2)}) %collective-permute-start.2) | collective-permute-done | bytes 110624 | tf_op jit(solution)/shard_map/ppermute | solution.py:472
  19.0 0.0 collective-permute-done.3.rb
  19.0 0.3 %yx.1 = (f32[23,12,24,128]{3,2,1,0:T(8,128)S(1)}, f32[23,24,128]{2,1,0:T(8,128)S(1)}, f32[2,104,128]{2,1,0:T(8,128)S(1)}) custom-call(f32[23,12,24,128]{3,2,1,0:T(8,128)S(1)} %get-tuple-element.27.ext_in, f32[23,24,128]{2,1,0:T(8,128)S(1)} %get-tuple-element.28.mini_in, ...), custom_call_target="tpu_custom_call", output_to_operand_aliasing={{0}: (0, {}), {1}: (1, {})} | custom-call | tf_op jit(solution)/shard_map/yx/pallas_call | solution.py:87
  19.3 0.6 %collective-permute-start.5 = (f32[2,104,128]{2,1,0:T(8,128)S(1)}, f32[2,104,128]{2,1,0:T(8,128)S(1)}, u32[]{:S(2)}, u32[]{:S(2)}) collective-permute-start(f32[2,104,128]{2,1,0:T(8,128)S(1)} %get-tuple-element.33), channel_id=1, source_target_pairs={{0,16},{16,0},{1,17},{17,1},{2,18},{18,2},{3,19},{19,3},{4,20},{20... | collective-permute-start | bytes 319496 | tf_op jit(solution)/shard_map/ppermute | solution.py:478
  19.9 2.2 %mid.1 = (f32[19,8,16,128]{3,2,1,0:T(8,128)}, f32[12,24,128]{2,1,0:T(8,128)S(1)}, f32[12,24,128]{2,1,0:T(8,128)S(1)}, f32[12,24,128]{2,1,0:T(8,128)S(1)}, f32[3,...) custom-call(f32[23,12,24,128]{3,2,1,0:T(8,128)S(1)} %get-tuple-element.31.ext.ext_in, ...), custom_call_target="tpu_custom_call" | custom-call | tf_op jit(solution)/shard_map/mid/pallas_call | solution.py:87
  22.1 2.2 %collective-permute-done.5.r2 = f32[2,104,128]{2,1,0:T(8,128)S(1)} collective-permute-done((f32[2,104,128]{2,1,0:T(8,128)S(1)}, f32[2,104,128]{2,1,0:T(8,128)S(1)}, u32[]{:S(2)}, u32[]{:S(2)}) %collective-permute-start.5) | collective-permute-done | bytes 106528 | tf_op jit(solution)/shard_map/ppermute | solution.py:478
  24.3 0.0 collective-permute-done.4.r1
  24.3 2.2 %last.1 = (f32[23,12,24,128]{3,2,1,0:T(8,128)S(1)}, f32[23,24,128]{2,1,0:T(8,128)S(1)}, f32[12,24,128]{2,1,0:T(8,128)S(1)}, f32[12,24,128]{2,1,0:T(8,128)S(1)}, ...) custom-call(f32[23,12,24,128]{3,2,1,0:T(8,128)S(1)} %get-tuple-eleme, ...), custom_call_target="tpu_custom_call", output_to_operand_aliasing={{0}: (0, {}), {1}: (1, {}), {2}: (4, {}), {3}: (5, {}), {4}... | custom-call | tf_op jit(solution)/shard_map/last/pallas_call | solution.py:87
Async XLA Ops:
  2.2 22.2 %collective-permute-start.4 = (f32[2,24,16,128]{3,2,1,0:T(8,128)S(1)}, f32[2,24,16,128]{3,2,1,0:T(8,128)S(1)}, u32[]{:S(2)}, u32[]{:S(2)}) collective-permute-start(f32[2,24,16,128]{3,2,1,0:T(8,128)S(1)} %xpack.1), channel_id=1, source_target_pairs={{0,16},{16,0},{1,17},{17,1},{2,18},{18,2},{3,19},{19,3},{4,20},{20... | collective-permute-start | bytes 1179656 | tf_op jit(solution)/shard_map/ppermute | solution.py:478
  5.2 5.6 %collective-permute-start = (f32[3,16,128]{2,1,0:T(8,128)S(1)}, f32[3,16,128]{2,1,0:T(8,128)S(1)}, u32[]{:S(2)}, u32[]{:S(2)}) collective-permute-start(f32[3,16,128]{2,1,0:T(8,128)S(1)} %get-tuple-element.25), channel_id=1, source_target_pairs={{1,2},{2,1},{3,0},{0,3},{5,6},{6,5},{7,4},{4,7},{9,10},{10,9},{11,... | collective-permute-start | bytes 73736 | tf_op jit(solution)/shard_map/ppermute | solution.py:472
  8.8 3.8 %collective-permute-start.1 = (f32[3,16,128]{2,1,0:T(8,128)S(1)}, f32[3,16,128]{2,1,0:T(8,128)S(1)}, u32[]{:S(2)}, u32[]{:S(2)}) collective-permute-start(f32[3,16,128]{2,1,0:T(8,128)S(1)} %get-tuple-element.26), channel_id=1, source_target_pairs={{0,1},{1,0},{2,3},{3,2},{4,5},{5,4},{6,7},{7,6},{8,9},{9,8},{10,11... | collective-permute-start | bytes 73736 | tf_op jit(solution)/shard_map/ppermute | solution.py:472
  13.6 5.3 %collective-permute-start.2 = (f32[216,128]{1,0:T(8,128)S(1)}, f32[216,128]{1,0:T(8,128)S(1)}, u32[]{:S(2)}, u32[]{:S(2)}) collective-permute-start(f32[216,128]{1,0:T(8,128)S(1)} %get-tuple-element.29), channel_id=1, source_target_pairs={{4,8},{8,4},{12,0},{0,12},{5,9},{9,5},{13,1},{1,13},{6,10},{10,6},... | collective-permute-start | bytes 331784 | tf_op jit(solution)/shard_map/ppermute | solution.py:472
  13.7 5.3 %collective-permute-start.3 = (f32[216,128]{1,0:T(8,128)S(1)}, f32[216,128]{1,0:T(8,128)S(1)}, u32[]{:S(2)}, u32[]{:S(2)}) collective-permute-start(f32[216,128]{1,0:T(8,128)S(1)} %get-tuple-element.30), channel_id=1, source_target_pairs={{0,4},{4,0},{8,12},{12,8},{1,5},{5,1},{9,13},{13,9},{2,6},{6,2},{1... | collective-permute-start | bytes 331784 | tf_op jit(solution)/shard_map/ppermute | solution.py:472
  19.3 5.1 %collective-permute-start.5 = (f32[2,104,128]{2,1,0:T(8,128)S(1)}, f32[2,104,128]{2,1,0:T(8,128)S(1)}, u32[]{:S(2)}, u32[]{:S(2)}) collective-permute-start(f32[2,104,128]{2,1,0:T(8,128)S(1)} %get-tuple-element.33), channel_id=1, source_target_pairs={{0,16},{16,0},{1,17},{17,1},{2,18},{18,2},{3,19},{19,3},{4,20},{20... | collective-permute-start | bytes 319496 | tf_op jit(solution)/shard_map/ppermute | solution.py:478

commit v3 on v2

--- a/solution.py
+++ b/solution.py
@@ -35,6 +35,7 @@
 RHO, MOM, FIELDS = 19, 20, 23
 ROWS = 24
 F32 = jnp.float32
+COSTLY = pl.CostEstimate(flops=10**10, bytes_accessed=10**6, transcendentals=0)
 VM = pl.BlockSpec(memory_space=pltpu.VMEM)
 HB = pl.BlockSpec(memory_space=pltpu.HBM)
 
@@ -63,11 +64,55 @@
     return found
 
 
+def z_pieces(side):
+    deep = deep_fields(2, side)
+    shallow = side_fields(2, side)[len(deep) :]
+    found = [(f, u, 0) for u, f in enumerate(deep)]
+    return found + [(f, len(deep) + k // 2, 1 + k % 2) for k, f in enumerate(shallow)]
+
+
+def z_place(side, unit, kind):
+    block, pair = unit % 8 // 2, unit % 2
+    start = 32 * block + 2 * pair
+    if side < 0:
+        shift, slots = start - 8, {0: (0, 1), 1: (1,), 2: (0,)}[kind]
+        shift -= kind == 2
+    else:
+        shift, slots = start - 10, {0: (0, 1), 1: (0,), 2: (1,)}[kind]
+        shift += kind == 2
+    return block, shift, [2 * pair + k for k in slots]
+
+
+def x_pieces(side):
+    found, group = [], 0
+    for d in (0, 1):
+        fields = [f for f in (deep_fields(0, side) if d else side_fields(0, side))]
+        up = [f for f in fields if f < 19 and DIRECTIONS[f][2] > 0]
+        down = [f for f in fields if f < 19 and DIRECTIONS[f][2] < 0]
+        flat = [f for f in fields if f > RHO or (f < 19 and DIRECTIONS[f][2] == 0)]
+        for a, b in zip(up, down):
+            found += [(a, d, group, 0, (2,), (2, 3)), (b, d, group, 0, (0, 1), (1,))]
+            group += 1
+        for k, f in enumerate(flat):
+            found.append((f, d, group + k // 3, k % 3 - 1, (1,), (2,)))
+        group += -(-len(flat) // 3)
+        found.append((RHO, d, group, 0, (0, 1, 2), (1, 2, 3)))
+        group += 1
+    assert group <= 16
+    return found
+
+
+def slot_mask(lane, shift, low, high):
+    four = lane % 4
+    inside = [None, None]
+    for half, slots in enumerate((low, high)):
+        for k in slots:
+            hit = four == k + shift
+            inside[half] = hit if inside[half] is None else inside[half] | hit
+    return ((lane < 64) & inside[0]) | ((lane >= 64) & inside[1])
+
+
 EDGE_LINES = -(-len(edge_entries(1)) // 8) * 8
-
-
-def is_odd(axis, rows):
-    return jnp.full((rows, 128), lax.axis_index(axis) % 2, jnp.int32) == 1
 
 
 def lane_ids(rows):
@@ -83,7 +128,7 @@
     return v if c == 0 else pltpu.roll(v, (-c) % ROWS, 0)
 
 
-def call(body, ins, outs, scratch=(), aliases=None, name=None, in_specs=None, out_specs=None):
+def call(body, ins, outs, scratch=(), aliases=None, name=None, in_specs=None, out_specs=None, cost=None):
     return pl.pallas_call(
         body,
         in_specs=in_specs or [VM] * len(ins),
@@ -92,6 +137,7 @@
         scratch_shapes=list(scratch),
         input_output_aliases=aliases or {},
         name=name,
+        cost_estimate=cost,
         compiler_params=pltpu.CompilerParams(vmem_limit_bytes=20 * 2**20),
     )(*ins)
 
@@ -141,41 +187,37 @@
     lax.fori_loop(0, nx, moments, 0, unroll=2)
     for f in range(RHO, FIELDS):
         edges(f)
-    odd = is_odd("gz", 16)
-    for t in range(za.shape[0]):
-        made = []
-        for side in (-1, 1):
-            fields = side_fields(2, side)
-            acc = None
-            for j in range(8 * t, min(8 * t + 8, len(fields))):
-                q = j % 8
-                b, p = q // 2, q % 2
-                v = lroll(mini[fields[j], pl.ds(0, 16), :], 32 * b + 2 * p - (8 if side < 0 else 10))
-                acc = v if acc is None else jnp.where((lane // 32 == b) & ((lane % 4) // 2 == p), v, acc)
-            made.append(acc)
-        za[t] = jnp.where(odd, made[0], made[1])
-        zb[t] = jnp.where(odd, made[1], made[0])
-
-
-def x_kernel(ext, xmsg):
+    for side, msg in ((-1, za), (1, zb)):
+        tiles = [None, None]
+        for f, unit, kind in z_pieces(side):
+            block, shift, slots = z_place(side, unit, kind)
+            v = lroll(mini[f, pl.ds(0, 16), :], shift)
+            here = lane % 4 == slots[0]
+            for k in slots[1:]:
+                here = here | (lane % 4 == k)
+            t = unit // 8
+            tiles[t] = v if tiles[t] is None else jnp.where((lane // 32 == block) & here, v, tiles[t])
+        msg[pl.ds(0, 16), :] = tiles[0]
+        msg[pl.ds(16, 8), :] = jnp.where(lane[:8] < 64, tiles[1][:8], lroll(tiles[1][8:], 64))
+
+
+def z_part(f):
+    return DIRECTIONS[f][2] if f < 19 else 0
+
+
+def pack_kernel(ext, xmsg, ya, yb):
     nx = ext.shape[1] - 4
     for s, side in enumerate((-1, 1)):
         for e, (f, d) in enumerate(side_entries(0, side)):
             plane = (nx + 1 - d) if side < 0 else (2 + d)
-            xmsg[s, e] = lroll(ext[f, plane, pl.ds(0, 16), :], -DIRECTIONS[f][2] if f < 19 else 0)
-
-
-def turn_kernel(ext_in, ext):
-    nx = ext.shape[1] - 4
-    moving = [i for i in range(19) if DIRECTIONS[i][2]]
-
-    def plane(p, _):
-        turned = [lroll(ext_in[i, p, pl.ds(0, 16), :], -DIRECTIONS[i][2]) for i in moving]
-        for i, v in zip(moving, turned):
-            ext[i, p, pl.ds(0, 16), :] = v
-        return 0
-
-    lax.fori_loop(2, nx + 2, plane, 0)
+            xmsg[s, e] = lroll(ext[f, plane, pl.ds(0, 16), :], -z_part(f))
+    for side, msg in ((-1, ya), (1, yb)):
+        for e, (f, d) in enumerate(side_entries(1, side)):
+            msg[pl.ds(8 * e, 8), :] = ext[f, pl.ds(2, 8), 15 - d if side < 0 else d, :]
+    for side, msg in ((-1, ya), (1, yb)):
+        for e, (f, d) in enumerate(side_entries(1, side)):
+            if z_part(f):
+                msg[pl.ds(8 * e, 8), :] = lroll(msg[pl.ds(8 * e, 8), :], -z_part(f))
 
 
 Z_PAIRS = ((5, 6), (11, 13), (14, 12), (15, 17), (18, 16))
@@ -185,85 +227,80 @@
     return jnp.where(lane_ids(above.shape[0]) % 4 == 0, lroll(above, 62), below)
 
 
-def close_pairs(p, pairs, ends, ext):
-    lane = lane_ids(16)
+def close_pairs(p, pairs, ends, ext, rows):
+    lane = lane_ids(rows.size)
     found = []
     for (up, down), e in zip(pairs, ends):
         g = lroll(e, 255 - 4 * p)
-        found.append((up, jnp.where(lane == 127, g, ext[up, p, pl.ds(0, 16), :])))
-        found.append((down, jnp.where(lane == 0, g, ext[down, p, pl.ds(0, 16), :])))
+        found.append((up, jnp.where(lane == 127, g, ext[up, p, rows, :])))
+        found.append((down, jnp.where(lane == 0, g, ext[down, p, rows, :])))
     return found
 
 
-def zy_kernel(ext_in, mini_in, ra, rb, ext, mini, ya, yb, ends):
-    nx = ext.shape[1] - 4
+def zy_kernel(mini_in, ra, rb, ya_in, yb_in, mini, ya, yb):
     lane = lane_ids(16)
     for f in range(FIELDS):
         e = mini_in[f, pl.ds(0, 16), :]
-        if f == RHO or (f < 19 and DIRECTIONS[f][2] < 0):
+        if f == RHO or z_part(f) < 0:
             e = jnp.where(lane < 64, e, lroll(e, 64))
         mini[f, pl.ds(0, 16), :] = e
-    odd = is_odd("gz", 16)
-    for side in (-1, 1):
-        msg = [jnp.where(odd, rb[t], ra[t]) if side < 0 else jnp.where(odd, ra[t], rb[t]) for t in range(ra.shape[0])]
-        if side < 0:
-            keep = (lane >= 8) & (lane < 40) & (lane % 4 < 2)
-        else:
-            keep = (lane >= 72) & (lane < 104) & (lane % 4 >= 2)
-        for j, f in enumerate(side_fields(2, side)):
-            q = j % 8
-            b, p = q // 2, q % 2
-            back = 8 - 32 * b - 2 * p if side < 0 else 74 - 32 * b - 2 * p
-            mini[f, pl.ds(0, 16), :] = jnp.where(keep, lroll(msg[j // 8], back), mini[f, pl.ds(0, 16), :])
+    for side, msg in ((-1, ra), (1, rb)):
+        second = msg[pl.ds(16, 8), :]
+        tiles = (msg[pl.ds(0, 16), :], jnp.concatenate([second, lroll(second, 64)], axis=0))
+        start, slots = (8, (0, 1)) if side < 0 else (72, (2, 3))
+        near = slots[1] if side < 0 else slots[0]
+        inside = (lane >= start) & (lane < start + 32)
+        for f, unit, kind in z_pieces(side):
+            shift = z_place(side, unit, kind)[1]
+            keep = inside & ((lane % 4 // 2 == slots[0] // 2) if kind == 0 else (lane % 4 == near))
+            v = lroll(tiles[unit // 8], -shift + (0 if side < 0 else 64))
+            mini[f, pl.ds(0, 16), :] = jnp.where(keep, v, mini[f, pl.ds(0, 16), :])
+    for side, msg in ((-1, ya), (1, yb)):
+        entries = side_entries(1, side)
+        for e, (f, d) in enumerate(entries):
+            msg[pl.ds(8 * len(entries) + e, 1), :] = mini[f, pl.ds(15 - d if side < 0 else d, 1), :]
+
+
+def turn_kernel(ext_in, mini, ext, ends):
+    nx = ext.shape[1] - 4
+    lane = lane_ids(16)
+    rows = pl.ds(0, 16)
     for k, (up, down) in enumerate(Z_PAIRS):
-        ends[k] = z_ends(mini[up, pl.ds(0, 16), :], mini[down, pl.ds(0, 16), :])
-
-    def close(p, _):
-        closed = close_pairs(p, Z_PAIRS, [ends[k] for k in range(len(Z_PAIRS))], ext_in)
-        for f, v in closed:
-            ext[f, p, pl.ds(0, 16), :] = v
+        ends[k] = z_ends(mini[up, rows, :], mini[down, rows, :])
+
+    def turn(p, _):
+        found = []
+        for k, (up, down) in enumerate(Z_PAIRS):
+            g = lroll(ends[k], 255 - 4 * p)
+            found.append((up, jnp.where(lane == 127, g, lroll(ext_in[up, p, rows, :], 127))))
+            found.append((down, jnp.where(lane == 0, g, lroll(ext_in[down, p, rows, :], 1))))
+        for f, v in found:
+            ext[f, p, rows, :] = v
         return 0
 
-    lax.fori_loop(2, nx + 2, close, 0)
-    odd = is_odd("gy", 8)
-    low, high = side_entries(1, -1), side_entries(1, 1)
-    for e in range(len(low)):
-        v = ext[low[e][0], pl.ds(2, 8), 15 - low[e][1], :]
-        w = ext[high[e][0], pl.ds(2, 8), high[e][1], :]
-        ya[pl.ds(8 * e, 8), :] = jnp.where(odd, v, w)
-        yb[pl.ds(8 * e, 8), :] = jnp.where(odd, w, v)
-    odd = is_odd("gy", 1)
-    for e in range(len(low)):
-        v = mini[low[e][0], pl.ds(15 - low[e][1], 1), :]
-        w = mini[high[e][0], pl.ds(high[e][1], 1), :]
-        ya[pl.ds(8 * len(low) + e, 1), :] = jnp.where(odd, v, w)
-        yb[pl.ds(8 * len(low) + e, 1), :] = jnp.where(odd, w, v)
+    lax.fori_loop(2, nx + 2, turn, 0, unroll=2)
 
 
 def yx_kernel(ext_in, mini_in, ra, rb, ext, mini, xmsg):
     lane = lane_ids(ROWS)
-    odd8, odd1 = is_odd("gy", 8), is_odd("gy", 1)
-    for side in (-1, 1):
-        first, second = (rb, ra) if side < 0 else (ra, rb)
+    for side, msg in ((-1, ra), (1, rb)):
         entries = side_entries(1, side)
         for e, (f, d) in enumerate(entries):
             row = 23 - d if side < 0 else 16 + d
             main, small = pl.ds(8 * e, 8), pl.ds(8 * len(entries) + e, 1)
-            ext[f, pl.ds(2, 8), row, :] = jnp.where(odd8, first[main, :], second[main, :])
-            mini[f, pl.ds(row, 1), :] = jnp.where(odd1, first[small, :], second[small, :])
+            ext[f, pl.ds(2, 8), row, :] = msg[main, :]
+            mini[f, pl.ds(row, 1), :] = msg[small, :]
     group = (lane % 64) // 4
     for s, side in enumerate((-1, 1)):
         for e, (f, dx, row) in enumerate(edge_entries(side)):
             plane = 9 - dx if side < 0 else 2 + dx
             xmsg[s, pl.ds(e, 1), :] = ext[f, plane, pl.ds(row, 1), :]
-        entries = side_entries(0, side)
-        for t in range(2):
-            acc = None
-            for e in range(16 * t, min(16 * t + 16, len(entries))):
-                f, d = entries[e]
-                v = lroll(mini[f], 4 * (e % 16) - 4 * (9 - d if side < 0 else 2 + d))
-                acc = v if acc is None else jnp.where(group == e % 16, v, acc)
-            xmsg[s, pl.ds(EDGE_LINES + ROWS * t, ROWS), :] = acc
+        acc = None
+        for f, d, g, shift, low, high in x_pieces(side):
+            plane = 9 - d if side < 0 else 2 + d
+            v = lroll(mini[f], 4 * g - 4 * plane + shift)
+            acc = v if acc is None else jnp.where((group == g) & slot_mask(lane, shift, low, high), v, acc)
+        xmsg[s, pl.ds(EDGE_LINES, ROWS), :] = acc
 
 
 def cell(b, rho, mom, psi, g):
@@ -392,20 +429,30 @@
         out[i, p - 1] = out[i, p - 1] + term
 
 
-def planes(count, of, step):
+def planes(count, of, step, unroll=4):
     def body(k, _):
         step(of(k))
         return 0
 
-    lax.fori_loop(0, count, body, 0)
+    lax.fori_loop(0, count, body, 0, unroll=unroll)
 
 
 def send_plane(out, out_hbm, sems, p):
     return pltpu.make_async_copy(out.at[:, p - 1], out_hbm.at[:, p - 2], sems.at[p - 2])
 
 
-def mid_kernel(ext, mini, out_hbm, psi, zs, zd, flux, out, sems):
+def mid_kernel(ext_in, mini, ext, out_hbm, psi, zs, zd, flux, out, ends, sems):
     nx = ext.shape[1] - 4
+    rows = pl.ds(16, 8)
+    for k, (up, down) in enumerate(Z_PAIRS):
+        ends[k] = z_ends(mini[up, rows, :], mini[down, rows, :])
+
+    def close(p, _):
+        for f, v in close_pairs(p, Z_PAIRS, [ends[k] for k in range(len(Z_PAIRS))], ext_in, rows):
+            ext[f, p, rows, :] = v
+        return 0
+
+    lax.fori_loop(2, nx + 2, close, 0, unroll=4)
     psi_ends, flux_ends = mini_adjoint(mini)
     for p in range(2, nx + 2):
         potential(p, ext, psi_ends, psi, zs, zd)
@@ -429,16 +476,20 @@
         for e, (f, d) in enumerate(entries):
             plane = 1 - d if side < 0 else nx + 2 + d
             ext[f, plane, pl.ds(0, 16), :] = r1[s, e]
-            v = r2[s, pl.ds(EDGE_LINES + ROWS * (e // 16), ROWS), :]
-            mini[f] = jnp.where(group == plane, lroll(v, 4 * plane - 4 * (e % 16)), mini[f])
         for e, (f, dx, row) in enumerate(edge_entries(side)):
             plane = 1 - dx if side < 0 else nx + 2 + dx
             ext[f, plane, pl.ds(row, 1), :] = r2[s, pl.ds(e, 1), :]
-    ends = [z_ends(mini[up, pl.ds(0, 16), :], mini[down, pl.ds(0, 16), :]) for up, down in Z_PAIRS]
+        small = r2[s, pl.ds(EDGE_LINES, ROWS), :]
+        for f, d, g, shift, low, high in x_pieces(side):
+            plane = 1 - d if side < 0 else nx + 2 + d
+            keep = (group == plane) & slot_mask(lane, 0, low, high)
+            mini[f] = jnp.where(keep, lroll(small, 4 * plane - 4 * g - shift), mini[f])
+    rows = pl.ds(0, ROWS)
+    ends = [z_ends(mini[up], mini[down]) for up, down in Z_PAIRS]
     for p in (0, 1, nx + 2, nx + 3):
         keep = [k for k, (f, _) in enumerate(Z_PAIRS) if DIRECTIONS[f][0] == (-1 if p < 2 else 1) or (p in (1, nx + 2) and DIRECTIONS[f][0] == 0)]
-        for f, v in close_pairs(p, [Z_PAIRS[k] for k in keep], [ends[k] for k in keep], ext):
-            ext[f, p, pl.ds(0, 16), :] = v
+        for f, v in close_pairs(p, [Z_PAIRS[k] for k in keep], [ends[k] for k in keep], ext, rows):
+            ext[f, p] = v
     psi_ends, flux_ends = mini_adjoint(mini)
     for p in (0, 1, nx + 2, nx + 3):
         potential(p, ext, psi_ends, psi, zs, zd)
@@ -446,12 +497,11 @@
     def outer(low, k):
         return low + k + jnp.where(k >= 2, nx - 2, 0)
 
-    planes(4, lambda k: outer(1, k), lambda p: collide(p, ext, psi, zs, zd, flux, out))
-
     def done(p):
         finish(p, psi, flux, flux_ends, out)
         send_plane(out, out_hbm, sems, p).start()
 
+    planes(4, lambda k: outer(1, k), lambda p: collide(p, ext, psi, zs, zd, flux, out))
     planes(4, lambda k: outer(2, k) - jnp.where(k >= 2, 2, 0), done)
     for p in (2, 3, nx, nx + 1):
         send_plane(out, out_hbm, sems, p).wait()
@@ -461,15 +511,6 @@
     n = lax.axis_size(axis)
     up = [(i, (i + 1) % n) for i in range(n)]
     return lax.ppermute(low, axis, up), lax.ppermute(high, axis, [(j, i) for i, j in up])
-
-
-def exchange(a, b, axis):
-    n = lax.axis_size(axis)
-    swaps = [[], []]
-    for i in range(n):
-        j = (i + 1) % n
-        swaps[1 - i % 2] += [(i, j), (j, i)]
-    return lax.ppermute(a, axis, swaps[0]), lax.ppermute(b, axis, swaps[1])
 
 
 def swap_both(msg, axis):
@@ -485,39 +526,49 @@
     ext, mini, za, zb = call(
         load_kernel,
         tuple(pltpu.with_memory_space_constraint(v, pltpu.HBM) for v in (populations, adjoint_next)),
-        (ext_shape, mini_shape, (3, 16, 128), (3, 16, 128)),
+        (ext_shape, mini_shape, (24, 128), (24, 128)),
         scratch=[pltpu.VMEM((19, nx, 16, 128), F32), pltpu.SemaphoreType.DMA((10,))],
         in_specs=[HB, HB],
         name="load",
     )
-    (xmsg,) = call(x_kernel, (ext,), ((2, 24, 16, 128),), name="xpack")
+    xmsg, ya, yb = call(
+        pack_kernel, (ext,), ((2, 24, 16, 128), (24 * 9, 128), (24 * 9, 128)), name="pack", cost=COSTLY
+    )
     x1 = swap_both(xmsg, "gx")
-    za, zb = exchange(za, zb, "gz")
-    (ext,) = call(turn_kernel, (ext,), (ext_shape,), aliases={0: 0}, name="turn")
-    ext, mini, ya, yb = call(
+    za, zb = swap(za, zb, "gz")
+    mini, ya, yb = call(
         zy_kernel,
-        (ext, mini, za, zb),
-        (ext_shape, mini_shape, (24 * 9, 128), (24 * 9, 128)),
+        (mini, za, zb, ya, yb),
+        (mini_shape, ya.shape, yb.shape),
+        aliases={0: 0, 3: 1, 4: 2},
+        name="zy",
+    )
+    ya, yb = swap(ya, yb, "gy")
+    (ext,) = call(
+        turn_kernel,
+        (ext, mini),
+        (ext_shape,),
         scratch=[pltpu.VMEM((len(Z_PAIRS), 16, 128), F32)],
-        aliases={0: 0, 1: 1},
-        name="zy",
-    )
-    ya, yb = exchange(ya, yb, "gy")
+        aliases={0: 0},
+        name="turn",
+        cost=COSTLY,
+    )
     ext, mini, xmsg2 = call(
         yx_kernel,
         (ext, mini, ya, yb),
-        (ext_shape, mini_shape, (2, EDGE_LINES + 2 * ROWS, 128)),
+        (ext_shape, mini_shape, (2, EDGE_LINES + ROWS, 128)),
         aliases={0: 0, 1: 1},
         name="yx",
     )
     x2 = swap_both(xmsg2, "gx")
     work = (plane_shape, plane_shape, plane_shape, (3, *plane_shape), (19, nx + 2, 16, 128))
-    out, *parts = call(
+    ext, out, *parts = call(
         mid_kernel,
         (ext, mini),
-        (populations.shape, *work),
-        scratch=[pltpu.SemaphoreType.DMA((nx,))],
-        out_specs=[HB] + [VM] * len(work),
+        (ext_shape, populations.shape, *work),
+        scratch=[pltpu.VMEM((len(Z_PAIRS), 8, 128), F32), pltpu.SemaphoreType.DMA((nx,))],
+        aliases={0: 0},
+        out_specs=[VM, HB] + [VM] * len(work),
         name="mid",
     )
     return call(

time: 26.7 us -> 21.3 us (0.80)
  waiting for transfers between devices: 9.01 us -> 3.28 us
  starting transfers between devices: 8.9 us -> 10.2 us
  Pallas kernels: 8.6 us -> 7.68 us
    ppermute x4, waiting for transfers between devices: 6.77 us -> 1.8 us  [the longest x2 1.58 us: swap(): lax.ppermute(low, axis, up)]
    ppermute x4, starting transfers between devices: 5.3 us -> 6.96 us  [the longest x2 3.82 us: swap(): lax.ppermute(high, axis, [(j, i) for i, j in up])]
    pallas_call x7, Pallas kernels: 8.6 us -> 7.68 us  [call(): pl.pallas_call(body, in_specs=in_specs or [VM] * len(ins), out_specs=out_...]
    ppermute x2, waiting for transfers between devices: 2.24 us -> 1.47 us  [swap_both(): return lax.ppermute(msg, axis, [(0, 1), (1, 0)])]
    ppermute x2, starting transfers between devices: 3.6 us -> 3.19 us  [swap_both(): return lax.ppermute(msg, axis, [(0, 1), (1, 0)])]
  transfers between devices with their start and end apart: 6 -> 6, of which waited for: 4 -> 3; matrix products, arithmetic and copies ran while one was open for 0% -> 0% of each run, Pallas kernels for 16% -> 18%
where the time goes in v3:
time: 21.3 us; the launch traced here: 21.2 us
  starting transfers between devices  10.2 us (48%)
  Pallas kernels  7.68 us (36%)
  waiting for transfers between devices  3.28 us (15%)
    pallas_call x7, Pallas kernels, call(): pl.pallas_call(body, in_specs=in_specs or [VM] * len(ins), out_specs=out_...  7.68 us
    ppermute x2, starting transfers between devices, swap(): lax.ppermute(high, axis, [(j, i) for i, j in up])  3.82 us
    ppermute x2, starting transfers between devices, swap_both(): return lax.ppermute(msg, axis, [(0, 1), (1, 0)])  3.19 us
    ppermute x2, starting transfers between devices, swap(): lax.ppermute(low, axis, up)  3.13 us
    ppermute x2, waiting for transfers between devices, swap(): lax.ppermute(low, axis, up)  1.58 us
    ppermute x2, waiting for transfers between devices, swap_both(): return lax.ppermute(msg, axis, [(0, 1), (1, 0)])  1.47 us
  transfers between devices with their start and end apart: 6, of which 3 were waited for; matrix products, arithmetic and copies ran while one was open for 0% of the time, Pallas kernels for 18%

profile of v3, /device:TPU:0, one launch (start us, length us, event | category | flops | bytes accessed | tf_op | source)
XLA Modules:
  0.0 21.2 jit_solution(3509136558806051419)
XLA Ops:
  0.0 2.1 %load.1 = (f32[23,12,24,128]{3,2,1,0:T(8,128)S(1)}, f32[23,24,128]{2,1,0:T(8,128)S(1)}, f32[24,128]{1,0:T(8,128)S(1)}, f32[24,128]{1,0:T(8,128)S(1)}) custom-call(f32[19,8,16,128]{3,2,1,0:T(8,128)} %pop_hbm.1, f32[19,8,16,128]{3,2,1,0:T(8,128)} %adj_hbm.1), custom_call_target="tpu_custom_call" | custom-call | tf_op jit(solution)/shard_map/load/pallas_call | solution.py:132
  2.1 3.1 %collective-permute-start = (f32[24,128]{1,0:T(8,128)S(1)}, f32[24,128]{1,0:T(8,128)S(1)}, u32[]{:S(2)}, u32[]{:S(2)}) collective-permute-start(f32[24,128]{1,0:T(8,128)S(1)} %get-tuple-element.28), channel_id=1, source_target_pairs={{0,1},{1,2},{2,3},{3,0},{4,5},{5,6},{6,7},{7,4},{8,9},{9,10},{10,1... | collective-permute-start | bytes 36872 | tf_op jit(solution)/shard_map/ppermute | solution.py:513
  5.2 2.1 %collective-permute-start.1 = (f32[24,128]{1,0:T(8,128)S(1)}, f32[24,128]{1,0:T(8,128)S(1)}, u32[]{:S(2)}, u32[]{:S(2)}) collective-permute-start(f32[24,128]{1,0:T(8,128)S(1)} %get-tuple-element.29), channel_id=1, source_target_pairs={{1,0},{2,1},{3,2},{0,3},{5,4},{6,5},{7,6},{4,7},{9,8},{10,9},{11,1... | collective-permute-start | bytes 36872 | tf_op jit(solution)/shard_map/ppermute | solution.py:513
  7.3 0.2 pack.1
  7.5 1.7 %collective-permute-start.4 = (f32[2,24,16,128]{3,2,1,0:T(8,128)S(1)}, f32[2,24,16,128]{3,2,1,0:T(8,128)S(1)}, u32[]{:S(2)}, u32[]{:S(2)}) collective-permute-start(f32[2,24,16,128]{3,2,1,0:T(8,128)S(1)} %get-tuple-element.38), channel_id=1, source_target_pairs={{0,16},{16,0},{1,17},{17,1},{2,18},{18,2},{3,19},{19,3},{4,20},{20... | collective-permute-start | bytes 1179656 | tf_op jit(solution)/shard_map/ppermute | solution.py:519
  9.2 0.0 collective-permute-done.ra
  9.2 0.0 collective-permute-done.1.rb
  9.2 0.3 %zy.1 = (f32[23,24,128]{2,1,0:T(8,128)S(1)}, f32[216,128]{1,0:T(8,128)S(1)}, f32[216,128]{1,0:T(8,128)S(1)}) custom-call(f32[23,24,128]{2,1,0:T(8,128)S(1)} %get-tuple-element.27.mini_in, f32[24,128]{1,0:T(8,128)S(1)} %collective-permute-done.ra, ...), custom_call_target="tpu_custom_call", output_to_operand_aliasing={{0}: (0, {}), {1}: (3, {}), {2}: (4, {})} | custom-call | tf_op jit(solution)/shard_map/zy/pallas_call | solution.py:132
  9.4 0.1 collective-permute-start.2
  9.5 1.7 %collective-permute-start.3 = (f32[216,128]{1,0:T(8,128)S(1)}, f32[216,128]{1,0:T(8,128)S(1)}, u32[]{:S(2)}, u32[]{:S(2)}) collective-permute-start(f32[216,128]{1,0:T(8,128)S(1)} %get-tuple-element.34), channel_id=1, source_target_pairs={{4,0},{8,4},{12,8},{0,12},{5,1},{9,5},{13,9},{1,13},{6,2},{10,6},{... | collective-permute-start | bytes 331784 | tf_op jit(solution)/shard_map/ppermute | solution.py:513
  11.2 0.8 %turn.1.ext_in = f32[23,12,24,128]{3,2,1,0:T(8,128)S(1)} custom-call(f32[23,12,24,128]{3,2,1,0:T(8,128)S(1)} %get-tuple-element.26.ext.ext_in, f32[23,24,128]{2,1,0:T(8,128)S(1)} %get-tuple-element.32.mini.mini_in), custom_call_target="tpu_custom_call", output_to_operand_aliasing={{}: (0, {})} | custom-call | flops 10000000000 | bytes 1000000 | tf_op jit(solution)/shard_map/turn/pallas_call | solution.py:132
  12.1 1.6 %collective-permute-done.2.ra = f32[216,128]{1,0:T(8,128)S(1)} collective-permute-done((f32[216,128]{1,0:T(8,128)S(1)}, f32[216,128]{1,0:T(8,128)S(1)}, u32[]{:S(2)}, u32[]{:S(2)}) %collective-permute-start.2) | collective-permute-done | bytes 110624 | tf_op jit(solution)/shard_map/ppermute | solution.py:513
  13.6 0.2 %collective-permute-done.3.rb = f32[216,128]{1,0:T(8,128)S(1)} collective-permute-done((f32[216,128]{1,0:T(8,128)S(1)}, f32[216,128]{1,0:T(8,128)S(1)}, u32[]{:S(2)}, u32[]{:S(2)}) %collective-permute-start.3) | collective-permute-done | bytes 110624 | tf_op jit(solution)/shard_map/ppermute | solution.py:513
  13.9 0.3 %yx.1 = (f32[23,12,24,128]{3,2,1,0:T(8,128)S(1)}, f32[23,24,128]{2,1,0:T(8,128)S(1)}, f32[2,80,128]{2,1,0:T(8,128)S(1)}) custom-call(f32[23,12,24,128]{3,2,1,0:T(8,128)S(1)} %turn.1.ext_in, f32[23,24,128]{2,1,0:T(8,128)S(1)} %get-tuple-element.32.mini.mini_in, ...), custom_call_target="tpu_custom_call", output_to_operand_aliasing={{0}: (0, {}), {1}: (1, {})} | custom-call | tf_op jit(solution)/shard_map/yx/pallas_call | solution.py:132
  14.2 1.5 %collective-permute-start.5 = (f32[2,80,128]{2,1,0:T(8,128)S(1)}, f32[2,80,128]{2,1,0:T(8,128)S(1)}, u32[]{:S(2)}, u32[]{:S(2)}) collective-permute-start(f32[2,80,128]{2,1,0:T(8,128)S(1)} %get-tuple-element.39), channel_id=1, source_target_pairs={{0,16},{16,0},{1,17},{17,1},{2,18},{18,2},{3,19},{19,3},{4,20},{20... | collective-permute-start | bytes 245768 | tf_op jit(solution)/shard_map/ppermute | solution.py:519
  15.7 2.2 %mid.1 = (f32[23,12,24,128]{3,2,1,0:T(8,128)S(1)}, f32[19,8,16,128]{3,2,1,0:T(8,128)}, f32[12,24,128]{2,1,0:T(8,128)S(1)}, f32[12,24,128]{2,1,0:T(8,128)S(1)}, f...) custom-call(f32[23,12,24,128]{3,2,1,0:T(8,128)S(1)} %get-tuple-eleme, ...), custom_call_target="tpu_custom_call", output_to_operand_aliasing={{0}: (0, {})} | custom-call | tf_op jit(solution)/shard_map/mid/pallas_call | solution.py:132
  17.8 1.5 %collective-permute-done.5.r2 = f32[2,80,128]{2,1,0:T(8,128)S(1)} collective-permute-done((f32[2,80,128]{2,1,0:T(8,128)S(1)}, f32[2,80,128]{2,1,0:T(8,128)S(1)}, u32[]{:S(2)}, u32[]{:S(2)}) %collective-permute-start.5) | collective-permute-done | bytes 81952 | tf_op jit(solution)/shard_map/ppermute | solution.py:519
  19.3 0.0 collective-permute-done.4.r1
  19.3 1.8 %last.1 = (f32[23,12,24,128]{3,2,1,0:T(8,128)S(1)}, f32[23,24,128]{2,1,0:T(8,128)S(1)}, f32[12,24,128]{2,1,0:T(8,128)S(1)}, f32[12,24,128]{2,1,0:T(8,128)S(1)}, ...) custom-call(f32[23,12,24,128]{3,2,1,0:T(8,128)S(1)} %get-tuple-eleme, ...), custom_call_target="tpu_custom_call", output_to_operand_aliasing={{0}: (0, {}), {1}: (1, {}), {2}: (4, {}), {3}: (5, {}), {4}... | custom-call | tf_op jit(solution)/shard_map/last/pallas_call | solution.py:132
Async XLA Ops:
  2.1 7.1 %collective-permute-start = (f32[24,128]{1,0:T(8,128)S(1)}, f32[24,128]{1,0:T(8,128)S(1)}, u32[]{:S(2)}, u32[]{:S(2)}) collective-permute-start(f32[24,128]{1,0:T(8,128)S(1)} %get-tuple-element.28), channel_id=1, source_target_pairs={{0,1},{1,2},{2,3},{3,0},{4,5},{5,6},{6,7},{7,4},{8,9},{9,10},{10,1... | collective-permute-start | bytes 36872 | tf_op jit(solution)/shard_map/ppermute | solution.py:513
  5.2 4.0 %collective-permute-start.1 = (f32[24,128]{1,0:T(8,128)S(1)}, f32[24,128]{1,0:T(8,128)S(1)}, u32[]{:S(2)}, u32[]{:S(2)}) collective-permute-start(f32[24,128]{1,0:T(8,128)S(1)} %get-tuple-element.29), channel_id=1, source_target_pairs={{1,0},{2,1},{3,2},{0,3},{5,4},{6,5},{7,6},{4,7},{9,8},{10,9},{11,1... | collective-permute-start | bytes 36872 | tf_op jit(solution)/shard_map/ppermute | solution.py:513
  7.5 11.9 %collective-permute-start.4 = (f32[2,24,16,128]{3,2,1,0:T(8,128)S(1)}, f32[2,24,16,128]{3,2,1,0:T(8,128)S(1)}, u32[]{:S(2)}, u32[]{:S(2)}) collective-permute-start(f32[2,24,16,128]{3,2,1,0:T(8,128)S(1)} %get-tuple-element.38), channel_id=1, source_target_pairs={{0,16},{16,0},{1,17},{17,1},{2,18},{18,2},{3,19},{19,3},{4,20},{20... | collective-permute-start | bytes 1179656 | tf_op jit(solution)/shard_map/ppermute | solution.py:519
  9.4 4.2 %collective-permute-start.2 = (f32[216,128]{1,0:T(8,128)S(1)}, f32[216,128]{1,0:T(8,128)S(1)}, u32[]{:S(2)}, u32[]{:S(2)}) collective-permute-start(f32[216,128]{1,0:T(8,128)S(1)} %get-tuple-element.33), channel_id=1, source_target_pairs={{0,4},{4,8},{8,12},{12,0},{1,5},{5,9},{9,13},{13,1},{2,6},{6,10},{... | collective-permute-start | bytes 331784 | tf_op jit(solution)/shard_map/ppermute | solution.py:513
  9.5 4.4 %collective-permute-start.3 = (f32[216,128]{1,0:T(8,128)S(1)}, f32[216,128]{1,0:T(8,128)S(1)}, u32[]{:S(2)}, u32[]{:S(2)}) collective-permute-start(f32[216,128]{1,0:T(8,128)S(1)} %get-tuple-element.34), channel_id=1, source_target_pairs={{4,0},{8,4},{12,8},{0,12},{5,1},{9,5},{13,9},{1,13},{6,2},{10,6},{... | collective-permute-start | bytes 331784 | tf_op jit(solution)/shard_map/ppermute | solution.py:513
  14.2 5.1 %collective-permute-start.5 = (f32[2,80,128]{2,1,0:T(8,128)S(1)}, f32[2,80,128]{2,1,0:T(8,128)S(1)}, u32[]{:S(2)}, u32[]{:S(2)}) collective-permute-start(f32[2,80,128]{2,1,0:T(8,128)S(1)} %get-tuple-element.39), channel_id=1, source_target_pairs={{0,16},{16,0},{1,17},{17,1},{2,18},{18,2},{3,19},{19,3},{4,20},{20... | collective-permute-start | bytes 245768 | tf_op jit(solution)/shard_map/ppermute | solution.py:519

commit v4 on v3

--- a/solution.py
+++ b/solution.py
@@ -52,16 +52,14 @@
     return [(f, d) for d in (0, 1) for f in (side_fields(dim, side) if d == 0 else deep_fields(dim, side))]
 
 
-def edge_entries(side):
+def edge_entries(side, up):
     found = []
-    for up in (-1, 1):
-        for dx in (0, 1):
-            for dy in (0, 1):
-                row = 23 - dy if up < 0 else 16 + dy
-                across = deep_fields(0, side) if dx else side_fields(0, side)
-                along = deep_fields(1, up) if dy else side_fields(1, up)
-                found += [(f, dx, row) for f in across if f in along]
-    return found
+    for dx in (0, 1):
+        for dy in (0, 1):
+            across = deep_fields(0, side) if dx else side_fields(0, side)
+            along = deep_fields(1, up) if dy else side_fields(1, up)
+            found += [(f, dx, dy) for f in across if f in along]
+    return sorted(found, key=lambda entry: z_part(entry[0]))
 
 
 def z_pieces(side):
@@ -83,23 +81,31 @@
     return block, shift, [2 * pair + k for k in slots]
 
 
-def x_pieces(side):
+def x_units(side):
     found, group = [], 0
-    for d in (0, 1):
-        fields = [f for f in (deep_fields(0, side) if d else side_fields(0, side))]
-        up = [f for f in fields if f < 19 and DIRECTIONS[f][2] > 0]
-        down = [f for f in fields if f < 19 and DIRECTIONS[f][2] < 0]
-        flat = [f for f in fields if f > RHO or (f < 19 and DIRECTIONS[f][2] == 0)]
-        for a, b in zip(up, down):
-            found += [(a, d, group, 0, (2,), (2, 3)), (b, d, group, 0, (0, 1), (1,))]
-            group += 1
-        for k, f in enumerate(flat):
-            found.append((f, d, group + k // 3, k % 3 - 1, (1,), (2,)))
-        group += -(-len(flat) // 3)
-        found.append((RHO, d, group, 0, (0, 1, 2), (1, 2, 3)))
-        group += 1
+    deep = deep_fields(0, side)
+    for depths, fields in ((2, deep), (1, side_fields(0, side)[len(deep) :])):
+        up = [f for f in fields if z_part(f) > 0]
+        down = [f for f in fields if z_part(f) < 0]
+        flat = [f for f in fields if f != RHO and z_part(f) == 0]
+        sets = [[(0, ((a, (2,), (2, 3)), (b, (0, 1), (1,))))] for a, b in zip(up, down)]
+        for k in range(0, len(flat), 3):
+            sets.append([(n - 1, ((f, (1,), (2,)),)) for n, f in enumerate(flat[k : k + 3])])
+        if RHO in fields:
+            sets.append([(0, ((RHO, (0, 1, 2), (1, 2, 3)),))])
+        for units in sets:
+            groups = (group,) if depths == 1 else (group + 1, group) if side < 0 else (group, group + 1)
+            found += [(groups, shift, parts) for shift, parts in units]
+            group += depths
     assert group <= 16
     return found
+
+
+def any_group(group, groups):
+    hit = group == groups[0]
+    for g in groups[1:]:
+        hit = hit | (group == g)
+    return hit
 
 
 def slot_mask(lane, shift, low, high):
@@ -112,7 +118,12 @@
     return ((lane < 64) & inside[0]) | ((lane >= 64) & inside[1])
 
 
-EDGE_LINES = -(-len(edge_entries(1)) // 8) * 8
+def z_part(f):
+    return DIRECTIONS[f][2] if f < 19 else 0
+
+
+CORNER = len(edge_entries(1, 1))
+EDGE_LINES = -(-(2 * CORNER + 4) // 8) * 8
 
 
 def lane_ids(rows):
@@ -142,7 +153,7 @@
     )(*ins)
 
 
-def load_kernel(pop_hbm, adj_hbm, ext, mini, za, zb, pops, sems):
+def load_kernel(pop_hbm, adj_hbm, ext, mini, ya, yb, pops, sems):
     nx = pop_hbm.shape[1]
     lane = lane_ids(16)
     group = lane // 4
@@ -187,37 +198,78 @@
     lax.fori_loop(0, nx, moments, 0, unroll=2)
     for f in range(RHO, FIELDS):
         edges(f)
+    place = lax.broadcasted_iota(jnp.int32, (EDGE_LINES, 128), 0)
+    for up, msg in ((-1, ya), (1, yb)):
+        entries = side_entries(1, up)
+        for e, (f, d) in enumerate(entries):
+            msg[pl.ds(e, 1), :] = mini[f, pl.ds(15 - d if up < 0 else d, 1), :]
+        lines = [(side, *entry) for side in (-1, 1) for entry in edge_entries(side, up)]
+        for e, (side, f, dx, dy) in enumerate(lines):
+            plane = nx + 1 - dx if side < 0 else 2 + dx
+            msg[pl.ds(len(entries) + e, 1), :] = ext[f, plane, pl.ds(15 - dy if up < 0 else dy, 1), :]
+        v = msg[pl.ds(len(entries), EDGE_LINES), :]
+        turned = v
+        for step in (-1, 1):
+            here = None
+            for k in (0, 1):
+                hits = [e for e in range(CORNER) if z_part(lines[CORNER * k + e][1]) == step]
+                hit = (place >= CORNER * k + hits[0]) & (place <= CORNER * k + hits[-1])
+                here = hit if here is None else here | hit
+            turned = jnp.where(here, lroll(v, -step), turned)
+        msg[pl.ds(len(entries), EDGE_LINES), :] = turned
+
+
+def x_kernel(ext, xmsg):
+    nx = ext.shape[1] - 4
+    for s, side in enumerate((-1, 1)):
+        for e, (f, d) in enumerate(side_entries(0, side)):
+            plane = (nx + 1 - d) if side < 0 else (2 + d)
+            xmsg[s, e] = lroll(ext[f, plane, pl.ds(0, 16), :], -z_part(f))
+
+
+def yz_kernel(mini_in, ra, rb, mini, za, zb):
+    lane = lane_ids(ROWS)
+    for side, msg in ((-1, ra), (1, rb)):
+        entries = side_entries(1, side)
+        for e, (f, d) in enumerate(entries):
+            mini[f, pl.ds(23 - d if side < 0 else 16 + d, 1), :] = msg[pl.ds(e, 1), :]
     for side, msg in ((-1, za), (1, zb)):
         tiles = [None, None]
         for f, unit, kind in z_pieces(side):
             block, shift, slots = z_place(side, unit, kind)
-            v = lroll(mini[f, pl.ds(0, 16), :], shift)
+            v = lroll(mini[f], shift)
             here = lane % 4 == slots[0]
             for k in slots[1:]:
                 here = here | (lane % 4 == k)
             t = unit // 8
             tiles[t] = v if tiles[t] is None else jnp.where((lane // 32 == block) & here, v, tiles[t])
-        msg[pl.ds(0, 16), :] = tiles[0]
-        msg[pl.ds(16, 8), :] = jnp.where(lane[:8] < 64, tiles[1][:8], lroll(tiles[1][8:], 64))
-
-
-def z_part(f):
-    return DIRECTIONS[f][2] if f < 19 else 0
-
-
-def pack_kernel(ext, xmsg, ya, yb):
-    nx = ext.shape[1] - 4
-    for s, side in enumerate((-1, 1)):
-        for e, (f, d) in enumerate(side_entries(0, side)):
-            plane = (nx + 1 - d) if side < 0 else (2 + d)
-            xmsg[s, e] = lroll(ext[f, plane, pl.ds(0, 16), :], -z_part(f))
+        msg[pl.ds(0, ROWS), :] = tiles[0]
+        msg[pl.ds(ROWS, 8), :] = jnp.where(lane[:8] < 64, tiles[1][:8], lroll(tiles[1][8:16], 64))
+        msg[pl.ds(ROWS + 8, 8), :] = tiles[1][16:]
+
+
+def y_entries(side):
+    found = []
+    for f, d in side_entries(1, side):
+        cx = DIRECTIONS[f][0] if f < 19 else 0
+        found.append((f, d, 3 + cx))
+    return sorted(found, key=lambda entry: z_part(entry[0]))
+
+
+def y_kernel(ext, mini, ya, yb):
     for side, msg in ((-1, ya), (1, yb)):
-        for e, (f, d) in enumerate(side_entries(1, side)):
-            msg[pl.ds(8 * e, 8), :] = ext[f, pl.ds(2, 8), 15 - d if side < 0 else d, :]
-    for side, msg in ((-1, ya), (1, yb)):
-        for e, (f, d) in enumerate(side_entries(1, side)):
-            if z_part(f):
-                msg[pl.ds(8 * e, 8), :] = lroll(msg[pl.ds(8 * e, 8), :], -z_part(f))
+        entries = y_entries(side)
+        six = ext.shape[1] - 6
+        msg[pl.ds(six * len(entries), 8), :] = jnp.zeros((8, 128), F32)
+        for e, (f, d, first) in enumerate(entries):
+            msg[pl.ds(six * e, six), :] = ext[f, pl.ds(first, six), 15 - d if side < 0 else d, :]
+        for step in (-1, 1):
+            hits = [e for e, (f, _, _) in enumerate(entries) if z_part(f) == step]
+            start, stop = six * hits[0], six * (hits[-1] + 1)
+            low, high = start // 8 * 8, -(-stop // 8) * 8
+            v = msg[pl.ds(low, high - low), :]
+            place = low + lax.broadcasted_iota(jnp.int32, v.shape, 0)
+            msg[pl.ds(low, high - low), :] = jnp.where((place >= start) & (place < stop), lroll(v, -step), v)
 
 
 Z_PAIRS = ((5, 6), (11, 13), (14, 12), (15, 17), (18, 16))
@@ -237,16 +289,16 @@
     return found
 
 
-def zy_kernel(mini_in, ra, rb, ya_in, yb_in, mini, ya, yb):
-    lane = lane_ids(16)
+def zx_kernel(mini_in, ra, rb, ya, yb, mini, xmsg):
+    lane = lane_ids(ROWS)
     for f in range(FIELDS):
-        e = mini_in[f, pl.ds(0, 16), :]
+        e = mini_in[f]
         if f == RHO or z_part(f) < 0:
             e = jnp.where(lane < 64, e, lroll(e, 64))
-        mini[f, pl.ds(0, 16), :] = e
+        mini[f] = e
     for side, msg in ((-1, ra), (1, rb)):
-        second = msg[pl.ds(16, 8), :]
-        tiles = (msg[pl.ds(0, 16), :], jnp.concatenate([second, lroll(second, 64)], axis=0))
+        second = msg[pl.ds(ROWS, 8), :]
+        tiles = (msg[pl.ds(0, ROWS), :], jnp.concatenate([second, lroll(second, 64), msg[pl.ds(ROWS + 8, 8), :]], axis=0))
         start, slots = (8, (0, 1)) if side < 0 else (72, (2, 3))
         near = slots[1] if side < 0 else slots[0]
         inside = (lane >= start) & (lane < start + 32)
@@ -254,14 +306,30 @@
             shift = z_place(side, unit, kind)[1]
             keep = inside & ((lane % 4 // 2 == slots[0] // 2) if kind == 0 else (lane % 4 == near))
             v = lroll(tiles[unit // 8], -shift + (0 if side < 0 else 64))
-            mini[f, pl.ds(0, 16), :] = jnp.where(keep, v, mini[f, pl.ds(0, 16), :])
-    for side, msg in ((-1, ya), (1, yb)):
-        entries = side_entries(1, side)
-        for e, (f, d) in enumerate(entries):
-            msg[pl.ds(8 * len(entries) + e, 1), :] = mini[f, pl.ds(15 - d if side < 0 else d, 1), :]
-
-
-def turn_kernel(ext_in, mini, ext, ends):
+            mini[f] = jnp.where(keep, v, mini[f])
+    group = (lane % 64) // 4
+    for s, side in enumerate((-1, 1)):
+        acc = None
+        for groups, shift, parts in x_units(side):
+            v = mini[parts[0][0]]
+            for f, low, high in parts[1:]:
+                v = jnp.where(slot_mask(lane, 0, low, high), mini[f], v)
+            v = lroll(v, 4 * groups[0] - 4 * (9 if side < 0 else 2) + shift)
+            if acc is None:
+                acc = v
+            else:
+                here = any_group(group, groups)
+                if parts[0][1:] == ((1,), (2,)):
+                    here = here & slot_mask(lane, shift, (1,), (2,))
+                acc = jnp.where(here, v, acc)
+        xmsg[s, pl.ds(EDGE_LINES - 8, 8), :] = pltpu.roll(acc[16:], 6, 0)
+        xmsg[s, pl.ds(EDGE_LINES, 16), :] = acc[:16]
+        for k, msg in enumerate((ya, yb)):
+            start = len(side_entries(1, 1)) + CORNER * s
+            xmsg[s, pl.ds(CORNER * k, CORNER), :] = msg[pl.ds(start, CORNER), :]
+
+
+def turn_kernel(ext_in, mini, ext, psi_ends, flux_ends, psi, zs, zd, ends):
     nx = ext.shape[1] - 4
     lane = lane_ids(16)
     rows = pl.ds(0, 16)
@@ -279,28 +347,9 @@
         return 0
 
     lax.fori_loop(2, nx + 2, turn, 0, unroll=2)
-
-
-def yx_kernel(ext_in, mini_in, ra, rb, ext, mini, xmsg):
-    lane = lane_ids(ROWS)
-    for side, msg in ((-1, ra), (1, rb)):
-        entries = side_entries(1, side)
-        for e, (f, d) in enumerate(entries):
-            row = 23 - d if side < 0 else 16 + d
-            main, small = pl.ds(8 * e, 8), pl.ds(8 * len(entries) + e, 1)
-            ext[f, pl.ds(2, 8), row, :] = msg[main, :]
-            mini[f, pl.ds(row, 1), :] = msg[small, :]
-    group = (lane % 64) // 4
-    for s, side in enumerate((-1, 1)):
-        for e, (f, dx, row) in enumerate(edge_entries(side)):
-            plane = 9 - dx if side < 0 else 2 + dx
-            xmsg[s, pl.ds(e, 1), :] = ext[f, plane, pl.ds(row, 1), :]
-        acc = None
-        for f, d, g, shift, low, high in x_pieces(side):
-            plane = 9 - d if side < 0 else 2 + d
-            v = lroll(mini[f], 4 * g - 4 * plane + shift)
-            acc = v if acc is None else jnp.where((group == g) & slot_mask(lane, shift, low, high), v, acc)
-        xmsg[s, pl.ds(EDGE_LINES, ROWS), :] = acc
+    psi_ends[...], flux_ends[...] = mini_adjoint(mini)
+    for p in range(2, nx + 2):
+        potential(p, ext, psi_ends, psi, zs, zd, rows)
 
 
 def cell(b, rho, mom, psi, g):
@@ -370,12 +419,12 @@
     return jnp.where(lane == 127, g, lroll(above, 127)), jnp.where(lane == 0, g, lroll(below, 1))
 
 
-def potential(p, ext, ends, psi, zs, zd):
-    v = 1.0 - jnp.exp(-ext[RHO, p])
-    psi[p] = v
-    a, b = zpair(v, v, ends, p)
-    zs[p] = a + b
-    zd[p] = a - b
+def potential(p, ext, ends, psi, zs, zd, rows):
+    v = 1.0 - jnp.exp(-ext[RHO, p, rows, :])
+    psi[p, rows, :] = v
+    a, b = zpair(v, v, ends[rows, :], p)
+    zs[p, rows, :] = a + b
+    zd[p, rows, :] = a - b
 
 
 def collide(p, ext, psi, zs, zd, flux, out):
@@ -423,7 +472,7 @@
     )
     across = W2 * (dx + dy)
     along = W1 * fz[:16] + W2 * (flux[2, p + 1, pl.ds(0, 16), :] + flux[2, p - 1, pl.ds(0, 16), :] + (yroll(fz, 1) + yroll(fz, -1))[:16])
-    a, b = zpair(across + along, across - along, ends[:16], p)
+    a, b = zpair(across + along, across - along, ends[pl.ds(0, 16), :], p)
     term = (COUPLING * (1.0 - psi[p, pl.ds(0, 16), :])) * (here + (a + b))
     for i in range(19):
         out[i, p - 1] = out[i, p - 1] + term
@@ -441,21 +490,27 @@
     return pltpu.make_async_copy(out.at[:, p - 1], out_hbm.at[:, p - 2], sems.at[p - 2])
 
 
-def mid_kernel(ext_in, mini, ext, out_hbm, psi, zs, zd, flux, out, ends, sems):
+def mid_kernel(ext_in, mini, sa, sb, ra, rb, psi_ends, flux_ends, psi_in, zs_in, zd_in, ext, out_hbm, psi, zs, zd, flux, out, ends, sems):
     nx = ext.shape[1] - 4
     rows = pl.ds(16, 8)
+    for up, small, large in ((-1, sa, ra), (1, sb, rb)):
+        for e, (f, d, first) in enumerate(y_entries(up)):
+            ext[f, pl.ds(first, nx - 2), 23 - d if up < 0 else 16 + d, :] = large[pl.ds((nx - 2) * e, nx - 2), :]
+        lines = [(side, *entry) for side in (-1, 1) for entry in edge_entries(side, up)]
+        for e, (side, f, dx, dy) in enumerate(lines):
+            plane, row = nx + 1 - dx if side < 0 else 2 + dx, 23 - dy if up < 0 else 16 + dy
+            ext[f, plane, pl.ds(row, 1), :] = small[pl.ds(len(side_entries(1, up)) + e, 1), :]
     for k, (up, down) in enumerate(Z_PAIRS):
         ends[k] = z_ends(mini[up, rows, :], mini[down, rows, :])
 
     def close(p, _):
-        for f, v in close_pairs(p, Z_PAIRS, [ends[k] for k in range(len(Z_PAIRS))], ext_in, rows):
+        for f, v in close_pairs(p, Z_PAIRS, [ends[k] for k in range(len(Z_PAIRS))], ext, rows):
             ext[f, p, rows, :] = v
         return 0
 
     lax.fori_loop(2, nx + 2, close, 0, unroll=4)
-    psi_ends, flux_ends = mini_adjoint(mini)
     for p in range(2, nx + 2):
-        potential(p, ext, psi_ends, psi, zs, zd)
+        potential(p, ext, psi_ends, psi, zs, zd, rows)
     planes(nx - 2, lambda k: k + 3, lambda p: collide(p, ext, psi, zs, zd, flux, out))
 
     def done(p):
@@ -467,32 +522,37 @@
         send_plane(out, out_hbm, sems, p).wait()
 
 
-def last_kernel(ext_in, mini_in, r1, r2, psi_in, zs_in, zd_in, flux_in, out_in, hbm_in, ext, mini, psi, zs, zd, flux, out, out_hbm, sems):
+def fill_kernel(ext_in, r1, ext):
+    nx = ext.shape[1] - 4
+    for s, side in enumerate((-1, 1)):
+        for e, (f, d) in enumerate(side_entries(0, side)):
+            ext[f, 1 - d if side < 0 else nx + 2 + d, pl.ds(0, 16), :] = r1[s, e]
+
+
+def last_kernel(ext_in, mini_in, r2, psi_in, zs_in, zd_in, flux_in, out_in, hbm_in, ext, mini, psi, zs, zd, flux, out, out_hbm, psi_ends, flux_ends, sems):
     nx = ext.shape[1] - 4
     lane = lane_ids(ROWS)
     group = (lane % 64) // 4
     for s, side in enumerate((-1, 1)):
-        entries = side_entries(0, side)
-        for e, (f, d) in enumerate(entries):
-            plane = 1 - d if side < 0 else nx + 2 + d
-            ext[f, plane, pl.ds(0, 16), :] = r1[s, e]
-        for e, (f, dx, row) in enumerate(edge_entries(side)):
-            plane = 1 - dx if side < 0 else nx + 2 + dx
+        lines = [(up, *entry) for up in (-1, 1) for entry in edge_entries(side, up)]
+        for e, (up, f, dx, dy) in enumerate(lines):
+            plane, row = 1 - dx if side < 0 else nx + 2 + dx, 23 - dy if up < 0 else 16 + dy
             ext[f, plane, pl.ds(row, 1), :] = r2[s, pl.ds(e, 1), :]
-        small = r2[s, pl.ds(EDGE_LINES, ROWS), :]
-        for f, d, g, shift, low, high in x_pieces(side):
-            plane = 1 - d if side < 0 else nx + 2 + d
-            keep = (group == plane) & slot_mask(lane, 0, low, high)
-            mini[f] = jnp.where(keep, lroll(small, 4 * plane - 4 * g - shift), mini[f])
-    rows = pl.ds(0, ROWS)
+        small = jnp.concatenate([r2[s, pl.ds(EDGE_LINES, 16), :], pltpu.roll(r2[s, pl.ds(EDGE_LINES - 8, 8), :], 2, 0)], axis=0)
+        for groups, shift, parts in x_units(side):
+            near = 1 if side < 0 else nx + 2
+            here = any_group(group, (near, near + side)[: len(groups)])
+            v = lroll(small, 4 * near - 4 * groups[0] - shift)
+            for f, low, high in parts:
+                mini[f] = jnp.where(here & slot_mask(lane, 0, low, high), v, mini[f])
     ends = [z_ends(mini[up], mini[down]) for up, down in Z_PAIRS]
     for p in (0, 1, nx + 2, nx + 3):
         keep = [k for k, (f, _) in enumerate(Z_PAIRS) if DIRECTIONS[f][0] == (-1 if p < 2 else 1) or (p in (1, nx + 2) and DIRECTIONS[f][0] == 0)]
-        for f, v in close_pairs(p, [Z_PAIRS[k] for k in keep], [ends[k] for k in keep], ext, rows):
+        for f, v in close_pairs(p, [Z_PAIRS[k] for k in keep], [ends[k] for k in keep], ext, pl.ds(0, ROWS)):
             ext[f, p] = v
-    psi_ends, flux_ends = mini_adjoint(mini)
+    psi_ends[...], flux_ends[...] = mini_adjoint(mini)
     for p in (0, 1, nx + 2, nx + 3):
-        potential(p, ext, psi_ends, psi, zs, zd)
+        potential(p, ext, psi_ends, psi, zs, zd, pl.ds(0, ROWS))
 
     def outer(low, k):
         return low + k + jnp.where(k >= 2, nx - 2, 0)
@@ -523,62 +583,63 @@
 def per_device(populations, adjoint_next):
     nx = populations.shape[1]
     ext_shape, mini_shape, plane_shape = (FIELDS, nx + 4, ROWS, 128), (FIELDS, ROWS, 128), (nx + 4, ROWS, 128)
-    ext, mini, za, zb = call(
+    small_y = (len(side_entries(1, 1)) + EDGE_LINES, 128)
+    ext, mini, ya, yb = call(
         load_kernel,
         tuple(pltpu.with_memory_space_constraint(v, pltpu.HBM) for v in (populations, adjoint_next)),
-        (ext_shape, mini_shape, (24, 128), (24, 128)),
+        (ext_shape, mini_shape, small_y, small_y),
         scratch=[pltpu.VMEM((19, nx, 16, 128), F32), pltpu.SemaphoreType.DMA((10,))],
         in_specs=[HB, HB],
         name="load",
     )
-    xmsg, ya, yb = call(
-        pack_kernel, (ext,), ((2, 24, 16, 128), (24 * 9, 128), (24 * 9, 128)), name="pack", cost=COSTLY
-    )
+    (xmsg,) = call(x_kernel, (ext,), ((2, 24, 16, 128),), name="xpack", cost=COSTLY)
     x1 = swap_both(xmsg, "gx")
+    ya, yb = swap(ya, yb, "gy")
+    mini, za, zb = call(
+        yz_kernel,
+        (mini, ya, yb),
+        (mini_shape, (ROWS + 16, 128), (ROWS + 16, 128)),
+        aliases={0: 0},
+        name="yz",
+    )
+    y2a, y2b = call(y_kernel, (ext, mini), ((24 * (nx - 2) + 8, 128), (24 * (nx - 2) + 8, 128)), name="ypack", cost=COSTLY)
+    y2a, y2b = swap(y2a, y2b, "gy")
     za, zb = swap(za, zb, "gz")
-    mini, ya, yb = call(
-        zy_kernel,
+    mini, xmsg2 = call(
+        zx_kernel,
         (mini, za, zb, ya, yb),
-        (mini_shape, ya.shape, yb.shape),
-        aliases={0: 0, 3: 1, 4: 2},
-        name="zy",
-    )
-    ya, yb = swap(ya, yb, "gy")
-    (ext,) = call(
+        (mini_shape, (2, EDGE_LINES + 16, 128)),
+        aliases={0: 0},
+        name="zx",
+    )
+    tile, out_shape = (ROWS, 128), (19, nx + 2, 16, 128)
+    ext, psi_ends, flux_ends, psi, zs, zd = call(
         turn_kernel,
         (ext, mini),
-        (ext_shape,),
+        (ext_shape, tile, tile, plane_shape, plane_shape, plane_shape),
         scratch=[pltpu.VMEM((len(Z_PAIRS), 16, 128), F32)],
         aliases={0: 0},
         name="turn",
-        cost=COSTLY,
-    )
-    ext, mini, xmsg2 = call(
-        yx_kernel,
-        (ext, mini, ya, yb),
-        (ext_shape, mini_shape, (2, EDGE_LINES + ROWS, 128)),
-        aliases={0: 0, 1: 1},
-        name="yx",
     )
     x2 = swap_both(xmsg2, "gx")
-    work = (plane_shape, plane_shape, plane_shape, (3, *plane_shape), (19, nx + 2, 16, 128))
-    ext, out, *parts = call(
+    ext, out, psi, zs, zd, flux, part = call(
         mid_kernel,
-        (ext, mini),
-        (ext_shape, populations.shape, *work),
+        (ext, mini, ya, yb, y2a, y2b, psi_ends, flux_ends, psi, zs, zd),
+        (ext_shape, populations.shape, plane_shape, plane_shape, plane_shape, (3, *plane_shape), out_shape),
         scratch=[pltpu.VMEM((len(Z_PAIRS), 8, 128), F32), pltpu.SemaphoreType.DMA((nx,))],
-        aliases={0: 0},
-        out_specs=[VM, HB] + [VM] * len(work),
+        aliases={0: 0, 8: 2, 9: 3, 10: 4},
+        out_specs=[VM, HB] + [VM] * 5,
         name="mid",
     )
+    (ext,) = call(fill_kernel, (ext, x1), (ext_shape,), aliases={0: 0}, name="fill")
     return call(
         last_kernel,
-        (ext, mini, x1, x2, *parts, out),
-        (ext_shape, mini_shape, *work, populations.shape),
-        scratch=[pltpu.SemaphoreType.DMA((nx,))],
-        aliases={0: 0, 1: 1, **{4 + i: 2 + i for i in range(len(work) + 1)}},
-        in_specs=[VM] * (4 + len(work)) + [HB],
-        out_specs=[VM] * (2 + len(work)) + [HB],
+        (ext, mini, x2, psi, zs, zd, flux, part, out),
+        (ext_shape, mini_shape, plane_shape, plane_shape, plane_shape, (3, *plane_shape), out_shape, populations.shape),
+        scratch=[pltpu.VMEM(tile, F32), pltpu.VMEM(tile, F32), pltpu.SemaphoreType.DMA((nx,))],
+        aliases={0: 0, 1: 1, 3: 2, 4: 3, 5: 4, 6: 5, 7: 6, 8: 7},
+        in_specs=[VM] * 8 + [HB],
+        out_specs=[VM] * 7 + [HB],
         name="last",
     )[-1]
 

time: 21.3 us -> 21 us (0.986)
  the two profiles are of different devices: /device:TPU:0 before, /device:TPU:1 now
where the time goes in v4:
time: 21 us; the launch traced here: 20.8 us
  starting transfers between devices  8.94 us (43%)
  Pallas kernels  7.91 us (38%)
  waiting for transfers between devices  3.89 us (19%)
    pallas_call x9, Pallas kernels, call(): pl.pallas_call(body, in_specs=in_specs or [VM] * len(ins), out_specs=out_...  7.91 us
    ppermute x3, starting transfers between devices, swap(): lax.ppermute(low, axis, up)  4.4 us
    ppermute x3, waiting for transfers between devices, swap(): lax.ppermute(high, axis, [(j, i) for i, j in up])  3.49 us
    ppermute x2, starting transfers between devices, swap_both(): return lax.ppermute(msg, axis, [(0, 1), (1, 0)])  2.27 us
    ppermute x3, starting transfers between devices, swap(): lax.ppermute(high, axis, [(j, i) for i, j in up])  2.27 us
  transfers between devices with their start and end apart: 8, of which 3 were waited for; matrix products, arithmetic and copies ran while one was open for 0% of the time, Pallas kernels for 20%

profile of v4, /device:TPU:1, one launch (start us, length us, event | category | flops | bytes accessed | tf_op | source)
XLA Modules:
  0.0 20.8 jit_solution(16157806987641687265)
XLA Ops:
  0.0 2.0 %load.1 = (f32[23,12,24,128]{3,2,1,0:T(8,128)S(1)}, f32[23,24,128]{2,1,0:T(8,128)S(1)}, f32[80,128]{1,0:T(8,128)S(1)}, f32[80,128]{1,0:T(8,128)S(1)}) custom-call(f32[19,8,16,128]{3,2,1,0:T(8,128)} %pop_hbm.1, f32[19,8,16,128]{3,2,1,0:T(8,128)} %adj_hbm.1), custom_call_target="tpu_custom_call" | custom-call | tf_op jit(solution)/shard_map/load/pallas_call | solution.py:143
  2.0 2.7 %collective-permute-start = (f32[80,128]{1,0:T(8,128)S(1)}, f32[80,128]{1,0:T(8,128)S(1)}, u32[]{:S(2)}, u32[]{:S(2)}) collective-permute-start(f32[80,128]{1,0:T(8,128)S(1)} %get-tuple-element.32), channel_id=1, source_target_pairs={{0,4},{4,8},{8,12},{12,0},{1,5},{5,9},{9,13},{13,1},{2,6},{6,10},{... | collective-permute-start | bytes 122888 | tf_op jit(solution)/shard_map/ppermute | solution.py:573
  4.7 0.0 collective-permute-start.1
  4.7 0.1 xpack.1
  4.8 1.3 %collective-permute-start.6 = (f32[2,24,16,128]{3,2,1,0:T(8,128)S(1)}, f32[2,24,16,128]{3,2,1,0:T(8,128)S(1)}, u32[]{:S(2)}, u32[]{:S(2)}) collective-permute-start(f32[2,24,16,128]{3,2,1,0:T(8,128)S(1)} %xpack.1), channel_id=1, source_target_pairs={{0,16},{16,0},{1,17},{17,1},{2,18},{18,2},{3,19},{19,3},{4,20},{20... | collective-permute-start | bytes 1179656 | tf_op jit(solution)/shard_map/ppermute | solution.py:579
  6.1 0.0 collective-permute-done.ra.ya.sa
  6.1 2.3 %collective-permute-done.1.rb.yb.sb = f32[80,128]{1,0:T(8,128)S(1)} collective-permute-done((f32[80,128]{1,0:T(8,128)S(1)}, f32[80,128]{1,0:T(8,128)S(1)}, u32[]{:S(2)}, u32[]{:S(2)}) %collective-permute-start.1) | collective-permute-done | bytes 40992 | tf_op jit(solution)/shard_map/ppermute | solution.py:573
  8.4 0.2 %yz.1 = (f32[23,24,128]{2,1,0:T(8,128)S(1)}, f32[40,128]{1,0:T(8,128)S(1)}, f32[40,128]{1,0:T(8,128)S(1)}) custom-call(f32[23,24,128]{2,1,0:T(8,128)S(1)} %get-tuple-element.31.mini_in, f32[80,128]{1,0:T(8,128)S(1)} %collective-permute-done.ra.ya.sa, f32[80,128]{1,0:T(8,128)S(1)} %collective-permute-done.1.rb.yb.sb), custom_call_target="tpu_custom_call", output_to_operand_aliasing={{0}: (0, {})} | custom-call | tf_op jit(solution)/shard_map/yz/pallas_call | solution.py:143
  8.6 1.1 %collective-permute-start.2 = (f32[40,128]{1,0:T(8,128)S(1)}, f32[40,128]{1,0:T(8,128)S(1)}, u32[]{:S(2)}, u32[]{:S(2)}) collective-permute-start(f32[40,128]{1,0:T(8,128)S(1)} %get-tuple-element.35), channel_id=1, source_target_pairs={{0,1},{1,2},{2,3},{3,0},{4,5},{5,6},{6,7},{7,4},{8,9},{9,10},{10,1... | collective-permute-start | bytes 61448 | tf_op jit(solution)/shard_map/ppermute | solution.py:573
  9.7 2.3 %collective-permute-start.3 = (f32[40,128]{1,0:T(8,128)S(1)}, f32[40,128]{1,0:T(8,128)S(1)}, u32[]{:S(2)}, u32[]{:S(2)}) collective-permute-start(f32[40,128]{1,0:T(8,128)S(1)} %get-tuple-element.36), channel_id=1, source_target_pairs={{1,0},{2,1},{3,2},{0,3},{5,4},{6,5},{7,6},{4,7},{9,8},{10,9},{11,1... | collective-permute-start | bytes 61448 | tf_op jit(solution)/shard_map/ppermute | solution.py:573
  12.0 0.2 ypack.1
  12.1 0.7 %collective-permute-start.4 = (f32[152,128]{1,0:T(8,128)S(1)}, f32[152,128]{1,0:T(8,128)S(1)}, u32[]{:S(2)}, u32[]{:S(2)}) collective-permute-start(f32[152,128]{1,0:T(8,128)S(1)} %get-tuple-element.39), channel_id=1, source_target_pairs={{0,4},{4,8},{8,12},{12,0},{1,5},{5,9},{9,13},{13,1},{2,6},{6,10},{... | collective-permute-start | bytes 233480 | tf_op jit(solution)/shard_map/ppermute | solution.py:573
  12.8 0.0 collective-permute-start.5
  12.8 0.4 %collective-permute-done.2.ra = f32[40,128]{1,0:T(8,128)S(1)} collective-permute-done((f32[40,128]{1,0:T(8,128)S(1)}, f32[40,128]{1,0:T(8,128)S(1)}, u32[]{:S(2)}, u32[]{:S(2)}) %collective-permute-start.2) | collective-permute-done | bytes 20512 | tf_op jit(solution)/shard_map/ppermute | solution.py:573
  13.2 0.0 collective-permute-done.3.rb
  13.2 0.4 %zx.1 = (f32[23,24,128]{2,1,0:T(8,128)S(1)}, f32[2,72,128]{2,1,0:T(8,128)S(1)}) custom-call(f32[23,24,128]{2,1,0:T(8,128)S(1)} %get-tuple-element.34.mini_in.mini, f32[40,128]{1,0:T(8,128)S(1)} %collective-permute-done.2.ra, f32[40,128]{1,0:T(8,128)S(1)} %collective-permute-done.3.rb, ...), custom_call_target="tpu_custom_call", output_to_operand_aliasing={{0}: (0, {})} | custom-call | tf_op jit(solution)/shard_map/zx/pallas_call | solution.py:143
  13.6 1.0 %collective-permute-start.7 = (f32[2,72,128]{2,1,0:T(8,128)S(1)}, f32[2,72,128]{2,1,0:T(8,128)S(1)}, u32[]{:S(2)}, u32[]{:S(2)}) collective-permute-start(f32[2,72,128]{2,1,0:T(8,128)S(1)} %get-tuple-element.47), channel_id=1, source_target_pairs={{0,16},{16,0},{1,17},{17,1},{2,18},{18,2},{3,19},{19,3},{4,20},{20... | collective-permute-start | bytes 221192 | tf_op jit(solution)/shard_map/ppermute | solution.py:579
  14.6 1.2 %turn.1 = (f32[23,12,24,128]{3,2,1,0:T(8,128)S(1)}, f32[24,128]{1,0:T(8,128)S(1)}, f32[24,128]{1,0:T(8,128)S(1)}, f32[12,24,128]{2,1,0:T(8,128)S(1)}, f32[12,24,...) custom-call(f32[23,12,24,128]{3,2,1,0:T(8,128)S(1)} %get-tuple-element.30.ext_in.ext, ...), custom_call_target="tpu_custom_call", output_to_operand_aliasing={{0}: (0, {})} | custom-call | tf_op jit(solution)/shard_map/turn/pallas_call | solution.py:143
  15.7 0.0 collective-permute-done.4.ra
  15.8 1.2 %collective-permute-done.5.rb = f32[152,128]{1,0:T(8,128)S(1)} collective-permute-done((f32[152,128]{1,0:T(8,128)S(1)}, f32[152,128]{1,0:T(8,128)S(1)}, u32[]{:S(2)}, u32[]{:S(2)}) %collective-permute-start.5) | collective-permute-done | bytes 77856 | tf_op jit(solution)/shard_map/ppermute | solution.py:573
  16.9 2.0 %mid.1 = (f32[23,12,24,128]{3,2,1,0:T(8,128)S(1)}, f32[19,8,16,128]{3,2,1,0:T(8,128)}, f32[12,24,128]{2,1,0:T(8,128)S(1)}, f32[12,24,128]{2,1,0:T(8,128)S(1)}, f...) custom-call(f32[23,12,24,128]{3,2,1,0:T(8,128)S(1)} %get-tuple-eleme, ...), custom_call_target="tpu_custom_call", output_to_operand_aliasing={{0}: (0, {}), {2}: (8, {}), {3}: (9, {}), {4}: (10, {})} | custom-call | tf_op jit(solution)/shard_map/mid/pallas_call | solution.py:143
  18.9 0.0 collective-permute-done.6.r1
  19.0 0.0 collective-permute-done.7.r2
  19.0 1.8 %last.1 = (f32[23,12,24,128]{3,2,1,0:T(8,128)S(1)}, f32[23,24,128]{2,1,0:T(8,128)S(1)}, f32[12,24,128]{2,1,0:T(8,128)S(1)}, f32[12,24,128]{2,1,0:T(8,128)S(1)}, ...) custom-call(f32[23,12,24,128]{3,2,1,0:T(8,128)S(1)} %fill.1.ext_in, ...), custom_call_target="tpu_custom_call", output_to_operand_aliasing={{0}: (0, {}), {1}: (1, {}), {2}: (3, {}), {3}: (4, {}), {4}... | custom-call | tf_op jit(solution)/shard_map/last/pallas_call | solution.py:143
  (1 shorter events, 0.0 us)
Async XLA Ops:
  2.0 4.1 %collective-permute-start = (f32[80,128]{1,0:T(8,128)S(1)}, f32[80,128]{1,0:T(8,128)S(1)}, u32[]{:S(2)}, u32[]{:S(2)}) collective-permute-start(f32[80,128]{1,0:T(8,128)S(1)} %get-tuple-element.32), channel_id=1, source_target_pairs={{0,4},{4,8},{8,12},{12,0},{1,5},{5,9},{9,13},{13,1},{2,6},{6,10},{... | collective-permute-start | bytes 122888 | tf_op jit(solution)/shard_map/ppermute | solution.py:573
  4.7 3.7 %collective-permute-start.1 = (f32[80,128]{1,0:T(8,128)S(1)}, f32[80,128]{1,0:T(8,128)S(1)}, u32[]{:S(2)}, u32[]{:S(2)}) collective-permute-start(f32[80,128]{1,0:T(8,128)S(1)} %get-tuple-element.33), channel_id=1, source_target_pairs={{4,0},{8,4},{12,8},{0,12},{5,1},{9,5},{13,9},{1,13},{6,2},{10,6},{... | collective-permute-start | bytes 122888 | tf_op jit(solution)/shard_map/ppermute | solution.py:573
  4.8 14.1 %collective-permute-start.6 = (f32[2,24,16,128]{3,2,1,0:T(8,128)S(1)}, f32[2,24,16,128]{3,2,1,0:T(8,128)S(1)}, u32[]{:S(2)}, u32[]{:S(2)}) collective-permute-start(f32[2,24,16,128]{3,2,1,0:T(8,128)S(1)} %xpack.1), channel_id=1, source_target_pairs={{0,16},{16,0},{1,17},{17,1},{2,18},{18,2},{3,19},{19,3},{4,20},{20... | collective-permute-start | bytes 1179656 | tf_op jit(solution)/shard_map/ppermute | solution.py:579
  8.6 4.5 %collective-permute-start.2 = (f32[40,128]{1,0:T(8,128)S(1)}, f32[40,128]{1,0:T(8,128)S(1)}, u32[]{:S(2)}, u32[]{:S(2)}) collective-permute-start(f32[40,128]{1,0:T(8,128)S(1)} %get-tuple-element.35), channel_id=1, source_target_pairs={{0,1},{1,2},{2,3},{3,0},{4,5},{5,6},{6,7},{7,4},{8,9},{9,10},{10,1... | collective-permute-start | bytes 61448 | tf_op jit(solution)/shard_map/ppermute | solution.py:573
  9.7 3.5 %collective-permute-start.3 = (f32[40,128]{1,0:T(8,128)S(1)}, f32[40,128]{1,0:T(8,128)S(1)}, u32[]{:S(2)}, u32[]{:S(2)}) collective-permute-start(f32[40,128]{1,0:T(8,128)S(1)} %get-tuple-element.36), channel_id=1, source_target_pairs={{1,0},{2,1},{3,2},{0,3},{5,4},{6,5},{7,6},{4,7},{9,8},{10,9},{11,1... | collective-permute-start | bytes 61448 | tf_op jit(solution)/shard_map/ppermute | solution.py:573
  12.1 3.6 %collective-permute-start.4 = (f32[152,128]{1,0:T(8,128)S(1)}, f32[152,128]{1,0:T(8,128)S(1)}, u32[]{:S(2)}, u32[]{:S(2)}) collective-permute-start(f32[152,128]{1,0:T(8,128)S(1)} %get-tuple-element.39), channel_id=1, source_target_pairs={{0,4},{4,8},{8,12},{12,0},{1,5},{5,9},{9,13},{13,1},{2,6},{6,10},{... | collective-permute-start | bytes 233480 | tf_op jit(solution)/shard_map/ppermute | solution.py:573
  12.8 4.1 %collective-permute-start.5 = (f32[152,128]{1,0:T(8,128)S(1)}, f32[152,128]{1,0:T(8,128)S(1)}, u32[]{:S(2)}, u32[]{:S(2)}) collective-permute-start(f32[152,128]{1,0:T(8,128)S(1)} %get-tuple-element.40), channel_id=1, source_target_pairs={{4,0},{8,4},{12,8},{0,12},{5,1},{9,5},{13,9},{1,13},{6,2},{10,6},{... | collective-permute-start | bytes 233480 | tf_op jit(solution)/shard_map/ppermute | solution.py:573
  13.6 5.4 %collective-permute-start.7 = (f32[2,72,128]{2,1,0:T(8,128)S(1)}, f32[2,72,128]{2,1,0:T(8,128)S(1)}, u32[]{:S(2)}, u32[]{:S(2)}) collective-permute-start(f32[2,72,128]{2,1,0:T(8,128)S(1)} %get-tuple-element.47), channel_id=1, source_target_pairs={{0,16},{16,0},{1,17},{17,1},{2,18},{18,2},{3,19},{19,3},{4,20},{20... | collective-permute-start | bytes 221192 | tf_op jit(solution)/shard_map/ppermute | solution.py:579

commit v5 on v4

--- a/solution.py
+++ b/solution.py
@@ -126,6 +126,11 @@
 EDGE_LINES = -(-(2 * CORNER + 4) // 8) * 8
 
 
+def by_parity(axis, v, w):
+    odd = jnp.full(v.shape, lax.axis_index(axis) % 2, jnp.int32) == 1
+    return jnp.where(odd, v, w), jnp.where(odd, w, v)
+
+
 def lane_ids(rows):
     return lax.broadcasted_iota(jnp.int32, (rows, 128), 1)
 
@@ -217,6 +222,37 @@
                 here = hit if here is None else here | hit
             turned = jnp.where(here, lroll(v, -step), turned)
         msg[pl.ds(len(entries), EDGE_LINES), :] = turned
+    ya[...], yb[...] = by_parity("gy", ya[...], yb[...])
+
+
+def y_entries(side):
+    found = []
+    for f, d in side_entries(1, side):
+        cx = DIRECTIONS[f][0] if f < 19 else 0
+        found.append((f, d, 3 + cx))
+    return sorted(found, key=lambda entry: z_part(entry[0]))
+
+
+def y_lines(ext, low, high):
+    for side, msg in ((-1, low), (1, high)):
+        entries = y_entries(side)
+        six = ext.shape[1] - 6
+        msg[pl.ds(six * len(entries), 8), :] = jnp.zeros((8, 128), F32)
+        for e, (f, d, first) in enumerate(entries):
+            msg[pl.ds(six * e, six), :] = ext[f, pl.ds(first, six), 15 - d if side < 0 else d, :]
+        for step in (-1, 1):
+            hits = [e for e, (f, _, _) in enumerate(entries) if z_part(f) == step]
+            start, stop = six * hits[0], six * (hits[-1] + 1)
+            bottom, top = start // 8 * 8, -(-stop // 8) * 8
+            v = msg[pl.ds(bottom, top - bottom), :]
+            place = bottom + lax.broadcasted_iota(jnp.int32, v.shape, 0)
+            msg[pl.ds(bottom, top - bottom), :] = jnp.where((place >= start) & (place < stop), lroll(v, -step), v)
+
+
+def pair_kernel(ext, small, msg, low, high):
+    y_lines(ext, low, high)
+    msg[pl.ds(0, small.shape[0]), :] = small[...]
+    msg[pl.ds(small.shape[0], low.shape[0]), :] = by_parity("gy", low[...], high[...])[1]
 
 
 def x_kernel(ext, xmsg):
@@ -227,9 +263,10 @@
             xmsg[s, e] = lroll(ext[f, plane, pl.ds(0, 16), :], -z_part(f))
 
 
-def yz_kernel(mini_in, ra, rb, mini, za, zb):
+def yz_kernel(mini_in, ra, rb, mini, za, zb, low, high):
     lane = lane_ids(ROWS)
-    for side, msg in ((-1, ra), (1, rb)):
+    low[...], high[...] = by_parity("gy", rb[pl.ds(0, low.shape[0]), :], ra[...])
+    for side, msg in ((-1, low), (1, high)):
         entries = side_entries(1, side)
         for e, (f, d) in enumerate(entries):
             mini[f, pl.ds(23 - d if side < 0 else 16 + d, 1), :] = msg[pl.ds(e, 1), :]
@@ -248,28 +285,9 @@
         msg[pl.ds(ROWS + 8, 8), :] = tiles[1][16:]
 
 
-def y_entries(side):
-    found = []
-    for f, d in side_entries(1, side):
-        cx = DIRECTIONS[f][0] if f < 19 else 0
-        found.append((f, d, 3 + cx))
-    return sorted(found, key=lambda entry: z_part(entry[0]))
-
-
-def y_kernel(ext, mini, ya, yb):
-    for side, msg in ((-1, ya), (1, yb)):
-        entries = y_entries(side)
-        six = ext.shape[1] - 6
-        msg[pl.ds(six * len(entries), 8), :] = jnp.zeros((8, 128), F32)
-        for e, (f, d, first) in enumerate(entries):
-            msg[pl.ds(six * e, six), :] = ext[f, pl.ds(first, six), 15 - d if side < 0 else d, :]
-        for step in (-1, 1):
-            hits = [e for e, (f, _, _) in enumerate(entries) if z_part(f) == step]
-            start, stop = six * hits[0], six * (hits[-1] + 1)
-            low, high = start // 8 * 8, -(-stop // 8) * 8
-            v = msg[pl.ds(low, high - low), :]
-            place = low + lax.broadcasted_iota(jnp.int32, v.shape, 0)
-            msg[pl.ds(low, high - low), :] = jnp.where((place >= start) & (place < stop), lroll(v, -step), v)
+def y_kernel(ext, mini, msg, low, high):
+    y_lines(ext, low, high)
+    msg[...] = by_parity("gy", low[...], high[...])[0]
 
 
 Z_PAIRS = ((5, 6), (11, 13), (14, 12), (15, 17), (18, 16))
@@ -486,14 +504,15 @@
     lax.fori_loop(0, count, body, 0, unroll=unroll)
 
 
-def send_plane(out, out_hbm, sems, p):
-    return pltpu.make_async_copy(out.at[:, p - 1], out_hbm.at[:, p - 2], sems.at[p - 2])
-
-
-def mid_kernel(ext_in, mini, sa, sb, ra, rb, psi_ends, flux_ends, psi_in, zs_in, zd_in, ext, out_hbm, psi, zs, zd, flux, out, ends, sems):
+def send_planes(out, out_hbm, sem, first, count):
+    return pltpu.make_async_copy(out.at[:, pl.ds(first - 1, count)], out_hbm.at[:, pl.ds(first - 2, count)], sem)
+
+
+def mid_kernel(ext_in, mini, sa, sb, r2, rb, psi_ends, flux_ends, psi_in, zs_in, zd_in, ext, psi, zs, zd, flux, out, ends, low, high):
     nx = ext.shape[1] - 4
     rows = pl.ds(16, 8)
-    for up, small, large in ((-1, sa, ra), (1, sb, rb)):
+    low[...], high[...] = by_parity("gy", rb[pl.ds(sa.shape[0], low.shape[0]), :], r2[...])
+    for up, small, large in ((-1, sa, low), (1, sb, high)):
         for e, (f, d, first) in enumerate(y_entries(up)):
             ext[f, pl.ds(first, nx - 2), 23 - d if up < 0 else 16 + d, :] = large[pl.ds((nx - 2) * e, nx - 2), :]
         lines = [(side, *entry) for side in (-1, 1) for entry in edge_entries(side, up)]
@@ -513,13 +532,7 @@
         potential(p, ext, psi_ends, psi, zs, zd, rows)
     planes(nx - 2, lambda k: k + 3, lambda p: collide(p, ext, psi, zs, zd, flux, out))
 
-    def done(p):
-        finish(p, psi, flux, flux_ends, out)
-        send_plane(out, out_hbm, sems, p).start()
-
-    planes(nx - 4, lambda k: k + 4, done)
-    for p in range(4, nx):
-        send_plane(out, out_hbm, sems, p).wait()
+    planes(nx - 4, lambda k: k + 4, lambda p: finish(p, psi, flux, flux_ends, out))
 
 
 def fill_kernel(ext_in, r1, ext):
@@ -529,8 +542,12 @@
             ext[f, 1 - d if side < 0 else nx + 2 + d, pl.ds(0, 16), :] = r1[s, e]
 
 
-def last_kernel(ext_in, mini_in, r2, psi_in, zs_in, zd_in, flux_in, out_in, hbm_in, ext, mini, psi, zs, zd, flux, out, out_hbm, psi_ends, flux_ends, sems):
+def last_kernel(ext_in, mini_in, r2, psi_in, zs_in, zd_in, flux_in, out_in, ext, mini, psi, zs, zd, flux, out, out_hbm, psi_ends, flux_ends, sems):
     nx = ext.shape[1] - 4
+    copies = [
+        send_planes(out, out_hbm, sems.at[k], first, count) for k, (first, count) in enumerate(((4, nx - 4), (2, 2), (nx, 2)))
+    ]
+    copies[0].start()
     lane = lane_ids(ROWS)
     group = (lane % 64) // 4
     for s, side in enumerate((-1, 1)):
@@ -557,20 +574,26 @@
     def outer(low, k):
         return low + k + jnp.where(k >= 2, nx - 2, 0)
 
-    def done(p):
-        finish(p, psi, flux, flux_ends, out)
-        send_plane(out, out_hbm, sems, p).start()
-
     planes(4, lambda k: outer(1, k), lambda p: collide(p, ext, psi, zs, zd, flux, out))
-    planes(4, lambda k: outer(2, k) - jnp.where(k >= 2, 2, 0), done)
-    for p in (2, 3, nx, nx + 1):
-        send_plane(out, out_hbm, sems, p).wait()
+    planes(4, lambda k: outer(2, k) - jnp.where(k >= 2, 2, 0), lambda p: finish(p, psi, flux, flux_ends, out))
+    for copy in copies[1:]:
+        copy.start()
+    for copy in copies:
+        copy.wait()
 
 
 def swap(low, high, axis):
     n = lax.axis_size(axis)
     up = [(i, (i + 1) % n) for i in range(n)]
     return lax.ppermute(low, axis, up), lax.ppermute(high, axis, [(j, i) for i, j in up])
+
+
+def ppermute_pairs(msg, axis, first):
+    n = lax.axis_size(axis)
+    found = []
+    for i in range(first, n + first, 2):
+        found += [(i % n, (i + 1) % n), ((i + 1) % n, i % n)]
+    return lax.ppermute(msg, axis, found)
 
 
 def swap_both(msg, axis):
@@ -592,18 +615,23 @@
         in_specs=[HB, HB],
         name="load",
     )
+    large_y = (24 * (nx - 2) + 8, 128)
+    two_large = [pltpu.VMEM(large_y, F32), pltpu.VMEM(large_y, F32)]
+    (yb,) = call(
+        pair_kernel, (ext, yb), ((small_y[0] + large_y[0], 128),), scratch=two_large, name="pair", cost=COSTLY
+    )
     (xmsg,) = call(x_kernel, (ext,), ((2, 24, 16, 128),), name="xpack", cost=COSTLY)
     x1 = swap_both(xmsg, "gx")
-    ya, yb = swap(ya, yb, "gy")
-    mini, za, zb = call(
+    ya, y2b = ppermute_pairs(ya, "gy", 1), ppermute_pairs(yb, "gy", 0)
+    mini, za, zb, ya, yb = call(
         yz_kernel,
-        (mini, ya, yb),
-        (mini_shape, (ROWS + 16, 128), (ROWS + 16, 128)),
+        (mini, ya, y2b),
+        (mini_shape, (ROWS + 16, 128), (ROWS + 16, 128), small_y, small_y),
         aliases={0: 0},
         name="yz",
     )
-    y2a, y2b = call(y_kernel, (ext, mini), ((24 * (nx - 2) + 8, 128), (24 * (nx - 2) + 8, 128)), name="ypack", cost=COSTLY)
-    y2a, y2b = swap(y2a, y2b, "gy")
+    (y2a,) = call(y_kernel, (ext, mini), (large_y,), scratch=two_large, name="ypack", cost=COSTLY)
+    y2a = ppermute_pairs(y2a, "gy", 1)
     za, zb = swap(za, zb, "gz")
     mini, xmsg2 = call(
         zx_kernel,
@@ -622,23 +650,21 @@
         name="turn",
     )
     x2 = swap_both(xmsg2, "gx")
-    ext, out, psi, zs, zd, flux, part = call(
+    ext, psi, zs, zd, flux, part = call(
         mid_kernel,
         (ext, mini, ya, yb, y2a, y2b, psi_ends, flux_ends, psi, zs, zd),
-        (ext_shape, populations.shape, plane_shape, plane_shape, plane_shape, (3, *plane_shape), out_shape),
-        scratch=[pltpu.VMEM((len(Z_PAIRS), 8, 128), F32), pltpu.SemaphoreType.DMA((nx,))],
-        aliases={0: 0, 8: 2, 9: 3, 10: 4},
-        out_specs=[VM, HB] + [VM] * 5,
+        (ext_shape, plane_shape, plane_shape, plane_shape, (3, *plane_shape), out_shape),
+        scratch=[pltpu.VMEM(v, F32) for v in ((len(Z_PAIRS), 8, 128), large_y, large_y)],
+        aliases={0: 0, 8: 1, 9: 2, 10: 3},
         name="mid",
     )
     (ext,) = call(fill_kernel, (ext, x1), (ext_shape,), aliases={0: 0}, name="fill")
     return call(
         last_kernel,
-        (ext, mini, x2, psi, zs, zd, flux, part, out),
+        (ext, mini, x2, psi, zs, zd, flux, part),
         (ext_shape, mini_shape, plane_shape, plane_shape, plane_shape, (3, *plane_shape), out_shape, populations.shape),
-        scratch=[pltpu.VMEM(tile, F32), pltpu.VMEM(tile, F32), pltpu.SemaphoreType.DMA((nx,))],
-        aliases={0: 0, 1: 1, 3: 2, 4: 3, 5: 4, 6: 5, 7: 6, 8: 7},
-        in_specs=[VM] * 8 + [HB],
+        scratch=[pltpu.VMEM(tile, F32), pltpu.VMEM(tile, F32), pltpu.SemaphoreType.DMA((3,))],
+        aliases={0: 0, 1: 1, 3: 2, 4: 3, 5: 4, 6: 5, 7: 6},
         out_specs=[VM] * 7 + [HB],
         name="last",
     )[-1]

time: 21 us -> 20.2 us (0.962)
  the two profiles are of different devices: /device:TPU:1 before, /device:TPU:0 now
where the time goes in v5:
time: 20.2 us; the launch traced here: 20 us
  starting transfers between devices  11.4 us (56%)
  Pallas kernels  7.26 us (36%)
  waiting for transfers between devices  1.31 us (6%)
    pallas_call x10, Pallas kernels, call(): pl.pallas_call(body, in_specs=in_specs or [VM] * len(ins), out_specs=out_...  7.26 us
    ppermute x3, starting transfers between devices, ppermute_pairs(): return lax.ppermute(msg, axis, found)  4.29 us
    ppermute x2, starting transfers between devices, swap_both(): return lax.ppermute(msg, axis, [(0, 1), (1, 0)])  3.12 us
    ppermute x1, starting transfers between devices, swap(): lax.ppermute(high, axis, [(j, i) for i, j in up])  2.09 us
    ppermute x1, starting transfers between devices, swap(): lax.ppermute(low, axis, up)  1.87 us
    ppermute x2, waiting for transfers between devices, swap_both(): return lax.ppermute(msg, axis, [(0, 1), (1, 0)])  0.65 us
    ppermute x1, waiting for transfers between devices, swap(): lax.ppermute(low, axis, up)  0.56 us
  transfers between devices with their start and end apart: 7, of which 3 were waited for; matrix products, arithmetic and copies ran while one was open for 0% of the time, Pallas kernels for 17%

profile of v5, /device:TPU:0, one launch (start us, length us, event | category | flops | bytes accessed | tf_op | source)
XLA Modules:
  0.0 20.0 jit_solution(1760928526962400918)
XLA Ops:
  0.0 2.0 %load.1 = (f32[23,12,24,128]{3,2,1,0:T(8,128)S(1)}, f32[23,24,128]{2,1,0:T(8,128)S(1)}, f32[80,128]{1,0:T(8,128)S(1)}, f32[80,128]{1,0:T(8,128)S(1)}) custom-call(f32[19,8,16,128]{3,2,1,0:T(8,128)} %pop_hbm.1, f32[19,8,16,128]{3,2,1,0:T(8,128)} %adj_hbm.1), custom_call_target="tpu_custom_call" | custom-call | tf_op jit(solution)/shard_map/load/pallas_call | solution.py:148
  2.0 2.5 %collective-permute-start = (f32[80,128]{1,0:T(8,128)S(1)}, f32[80,128]{1,0:T(8,128)S(1)}, u32[]{:S(2)}, u32[]{:S(2)}) collective-permute-start(f32[80,128]{1,0:T(8,128)S(1)} %get-tuple-element.31), channel_id=1, source_target_pairs={{4,8},{8,4},{12,0},{0,12},{5,9},{9,5},{13,1},{1,13},{6,10},{10,6},... | collective-permute-start | bytes 122888 | tf_op jit(solution)/shard_map/ppermute | solution.py:596
  4.5 0.2 pair.1
  4.7 0.7 %collective-permute-start.1 = (f32[232,128]{1,0:T(8,128)S(1)}, f32[232,128]{1,0:T(8,128)S(1)}, u32[]{:S(2)}, u32[]{:S(2)}) collective-permute-start(f32[232,128]{1,0:T(8,128)S(1)} %pair.1), channel_id=1, source_target_pairs={{0,4},{4,0},{8,12},{12,8},{1,5},{5,1},{9,13},{13,9},{2,6},{6,2},{1... | collective-permute-start | bytes 356360 | tf_op jit(solution)/shard_map/ppermute | solution.py:596
  5.4 0.1 xpack.1
  5.5 1.6 %collective-permute-start.5 = (f32[2,24,16,128]{3,2,1,0:T(8,128)S(1)}, f32[2,24,16,128]{3,2,1,0:T(8,128)S(1)}, u32[]{:S(2)}, u32[]{:S(2)}) collective-permute-start(f32[2,24,16,128]{3,2,1,0:T(8,128)S(1)} %xpack.1), channel_id=1, source_target_pairs={{0,16},{16,0},{1,17},{17,1},{2,18},{18,2},{3,19},{19,3},{4,20},{20... | collective-permute-start | bytes 1179656 | tf_op jit(solution)/shard_map/ppermute | solution.py:602
  7.1 0.0 collective-permute-done.ra
  7.1 0.0 collective-permute-done.1.rb
  7.1 0.2 %yz.1 = (f32[23,24,128]{2,1,0:T(8,128)S(1)}, f32[40,128]{1,0:T(8,128)S(1)}, f32[40,128]{1,0:T(8,128)S(1)}, f32[80,128]{1,0:T(8,128)S(1)}, f32[80,128]{1,0:T(8,128)S(1)}) custom-call(f32[23,24,128]{2,1,0:T(8,128)S(1)} %get-tuple-element.30.mini_in, f32[80,128]{1,0:T(8,128)S(1)} %collective-permute-done.ra, ...), custom_call_target="tpu_custom_call", output_to_operand_aliasing={{0}: (0, {})} | custom-call | tf_op jit(solution)/shard_map/yz/pallas_call | solution.py:148
  7.3 1.9 %collective-permute-start.2 = (f32[40,128]{1,0:T(8,128)S(1)}, f32[40,128]{1,0:T(8,128)S(1)}, u32[]{:S(2)}, u32[]{:S(2)}) collective-permute-start(f32[40,128]{1,0:T(8,128)S(1)} %get-tuple-element.34), channel_id=1, source_target_pairs={{0,1},{1,2},{2,3},{3,0},{4,5},{5,6},{6,7},{7,4},{8,9},{9,10},{10,1... | collective-permute-start | bytes 61448 | tf_op jit(solution)/shard_map/ppermute | solution.py:588
  9.2 2.1 %collective-permute-start.3 = (f32[40,128]{1,0:T(8,128)S(1)}, f32[40,128]{1,0:T(8,128)S(1)}, u32[]{:S(2)}, u32[]{:S(2)}) collective-permute-start(f32[40,128]{1,0:T(8,128)S(1)} %get-tuple-element.35), channel_id=1, source_target_pairs={{1,0},{2,1},{3,2},{0,3},{5,4},{6,5},{7,6},{4,7},{9,8},{10,9},{11,1... | collective-permute-start | bytes 61448 | tf_op jit(solution)/shard_map/ppermute | solution.py:588
  11.3 0.2 ypack.1
  11.5 1.1 %collective-permute-start.4 = (f32[152,128]{1,0:T(8,128)S(1)}, f32[152,128]{1,0:T(8,128)S(1)}, u32[]{:S(2)}, u32[]{:S(2)}) collective-permute-start(f32[152,128]{1,0:T(8,128)S(1)} %ypack.1), channel_id=1, source_target_pairs={{4,8},{8,4},{12,0},{0,12},{5,9},{9,5},{13,1},{1,13},{6,10},{10,6},... | collective-permute-start | bytes 233480 | tf_op jit(solution)/shard_map/ppermute | solution.py:596
  12.6 0.6 %collective-permute-done.2.ra = f32[40,128]{1,0:T(8,128)S(1)} collective-permute-done((f32[40,128]{1,0:T(8,128)S(1)}, f32[40,128]{1,0:T(8,128)S(1)}, u32[]{:S(2)}, u32[]{:S(2)}) %collective-permute-start.2) | collective-permute-done | bytes 20512 | tf_op jit(solution)/shard_map/ppermute | solution.py:588
  13.1 0.1 collective-permute-done.3.rb
  13.2 0.4 %zx.1 = (f32[23,24,128]{2,1,0:T(8,128)S(1)}, f32[2,72,128]{2,1,0:T(8,128)S(1)}) custom-call(f32[23,24,128]{2,1,0:T(8,128)S(1)} %get-tuple-element.33.mini_in.mini, f32[40,128]{1,0:T(8,128)S(1)} %collective-permute-done.2.ra, f32[40,128]{1,0:T(8,128)S(1)} %collective-permute-done.3.rb, ...), custom_call_target="tpu_custom_call", output_to_operand_aliasing={{0}: (0, {})} | custom-call | tf_op jit(solution)/shard_map/zx/pallas_call | solution.py:148
  13.6 1.6 %collective-permute-start.6 = (f32[2,72,128]{2,1,0:T(8,128)S(1)}, f32[2,72,128]{2,1,0:T(8,128)S(1)}, u32[]{:S(2)}, u32[]{:S(2)}) collective-permute-start(f32[2,72,128]{2,1,0:T(8,128)S(1)} %get-tuple-element.46), channel_id=1, source_target_pairs={{0,16},{16,0},{1,17},{17,1},{2,18},{18,2},{3,19},{19,3},{4,20},{20... | collective-permute-start | bytes 221192 | tf_op jit(solution)/shard_map/ppermute | solution.py:602
  15.2 1.2 %turn.1 = (f32[23,12,24,128]{3,2,1,0:T(8,128)S(1)}, f32[24,128]{1,0:T(8,128)S(1)}, f32[24,128]{1,0:T(8,128)S(1)}, f32[12,24,128]{2,1,0:T(8,128)S(1)}, f32[12,24,...) custom-call(f32[23,12,24,128]{3,2,1,0:T(8,128)S(1)} %get-tuple-element.29.ext.ext_in, ...), custom_call_target="tpu_custom_call", output_to_operand_aliasing={{0}: (0, {})} | custom-call | tf_op jit(solution)/shard_map/turn/pallas_call | solution.py:148
  16.3 0.0 collective-permute-done.4.r2
  16.3 1.2 %mid.1 = (f32[23,12,24,128]{3,2,1,0:T(8,128)S(1)}, f32[12,24,128]{2,1,0:T(8,128)S(1)}, f32[12,24,128]{2,1,0:T(8,128)S(1)}, f32[12,24,128]{2,1,0:T(8,128)S(1)}, f...) custom-call(f32[23,12,24,128]{3,2,1,0:T(8,128)S(1)} %get-tuple-eleme, ...), custom_call_target="tpu_custom_call", output_to_operand_aliasing={{0}: (0, {}), {1}: (8, {}), {2}: (9, {}), {3}: (10, {})} | custom-call | tf_op jit(solution)/shard_map/mid/pallas_call | solution.py:148
  17.5 0.0 collective-permute-done.5.r1
  17.5 0.6 %collective-permute-done.6.r2 = f32[2,72,128]{2,1,0:T(8,128)S(1)} collective-permute-done((f32[2,72,128]{2,1,0:T(8,128)S(1)}, f32[2,72,128]{2,1,0:T(8,128)S(1)}, u32[]{:S(2)}, u32[]{:S(2)}) %collective-permute-start.6) | collective-permute-done | bytes 73760 | tf_op jit(solution)/shard_map/ppermute | solution.py:602
  18.2 1.8 %last.1 = (f32[23,12,24,128]{3,2,1,0:T(8,128)S(1)}, f32[23,24,128]{2,1,0:T(8,128)S(1)}, f32[12,24,128]{2,1,0:T(8,128)S(1)}, f32[12,24,128]{2,1,0:T(8,128)S(1)}, ...) custom-call(f32[23,12,24,128]{3,2,1,0:T(8,128)S(1)} %fill.1.ext_in, ...), custom_call_target="tpu_custom_call", output_to_operand_aliasing={{0}: (0, {}), {1}: (1, {}), {2}: (3, {}), {3}: (4, {}), {4}... | custom-call | tf_op jit(solution)/shard_map/last/pallas_call | solution.py:148
  (1 shorter events, 0.0 us)
Async XLA Ops:
  2.0 5.1 %collective-permute-start = (f32[80,128]{1,0:T(8,128)S(1)}, f32[80,128]{1,0:T(8,128)S(1)}, u32[]{:S(2)}, u32[]{:S(2)}) collective-permute-start(f32[80,128]{1,0:T(8,128)S(1)} %get-tuple-element.31), channel_id=1, source_target_pairs={{4,8},{8,4},{12,0},{0,12},{5,9},{9,5},{13,1},{1,13},{6,10},{10,6},... | collective-permute-start | bytes 122888 | tf_op jit(solution)/shard_map/ppermute | solution.py:596
  4.7 2.4 %collective-permute-start.1 = (f32[232,128]{1,0:T(8,128)S(1)}, f32[232,128]{1,0:T(8,128)S(1)}, u32[]{:S(2)}, u32[]{:S(2)}) collective-permute-start(f32[232,128]{1,0:T(8,128)S(1)} %pair.1), channel_id=1, source_target_pairs={{0,4},{4,0},{8,12},{12,8},{1,5},{5,1},{9,13},{13,9},{2,6},{6,2},{1... | collective-permute-start | bytes 356360 | tf_op jit(solution)/shard_map/ppermute | solution.py:596
  5.5 12.0 %collective-permute-start.5 = (f32[2,24,16,128]{3,2,1,0:T(8,128)S(1)}, f32[2,24,16,128]{3,2,1,0:T(8,128)S(1)}, u32[]{:S(2)}, u32[]{:S(2)}) collective-permute-start(f32[2,24,16,128]{3,2,1,0:T(8,128)S(1)} %xpack.1), channel_id=1, source_target_pairs={{0,16},{16,0},{1,17},{17,1},{2,18},{18,2},{3,19},{19,3},{4,20},{20... | collective-permute-start | bytes 1179656 | tf_op jit(solution)/shard_map/ppermute | solution.py:602
  7.3 5.8 %collective-permute-start.2 = (f32[40,128]{1,0:T(8,128)S(1)}, f32[40,128]{1,0:T(8,128)S(1)}, u32[]{:S(2)}, u32[]{:S(2)}) collective-permute-start(f32[40,128]{1,0:T(8,128)S(1)} %get-tuple-element.34), channel_id=1, source_target_pairs={{0,1},{1,2},{2,3},{3,0},{4,5},{5,6},{6,7},{7,4},{8,9},{9,10},{10,1... | collective-permute-start | bytes 61448 | tf_op jit(solution)/shard_map/ppermute | solution.py:588
  9.2 4.0 %collective-permute-start.3 = (f32[40,128]{1,0:T(8,128)S(1)}, f32[40,128]{1,0:T(8,128)S(1)}, u32[]{:S(2)}, u32[]{:S(2)}) collective-permute-start(f32[40,128]{1,0:T(8,128)S(1)} %get-tuple-element.35), channel_id=1, source_target_pairs={{1,0},{2,1},{3,2},{0,3},{5,4},{6,5},{7,6},{4,7},{9,8},{10,9},{11,1... | collective-permute-start | bytes 61448 | tf_op jit(solution)/shard_map/ppermute | solution.py:588
  11.5 4.9 %collective-permute-start.4 = (f32[152,128]{1,0:T(8,128)S(1)}, f32[152,128]{1,0:T(8,128)S(1)}, u32[]{:S(2)}, u32[]{:S(2)}) collective-permute-start(f32[152,128]{1,0:T(8,128)S(1)} %ypack.1), channel_id=1, source_target_pairs={{4,8},{8,4},{12,0},{0,12},{5,9},{9,5},{13,1},{1,13},{6,10},{10,6},... | collective-permute-start | bytes 233480 | tf_op jit(solution)/shard_map/ppermute | solution.py:596
  13.6 4.6 %collective-permute-start.6 = (f32[2,72,128]{2,1,0:T(8,128)S(1)}, f32[2,72,128]{2,1,0:T(8,128)S(1)}, u32[]{:S(2)}, u32[]{:S(2)}) collective-permute-start(f32[2,72,128]{2,1,0:T(8,128)S(1)} %get-tuple-element.46), channel_id=1, source_target_pairs={{0,16},{16,0},{1,17},{17,1},{2,18},{18,2},{3,19},{19,3},{4,20},{20... | collective-permute-start | bytes 221192 | tf_op jit(solution)/shard_map/ppermute | solution.py:602

commit v6 on v5

--- a/solution.py
+++ b/solution.py
@@ -158,7 +158,7 @@
     )(*ins)
 
 
-def load_kernel(pop_hbm, adj_hbm, ext, mini, ya, yb, pops, sems):
+def load_kernel(pop_hbm, adj_hbm, ext, mini, ya, yb, pops, columns, sems):
     nx = pop_hbm.shape[1]
     lane = lane_ids(16)
     group = lane // 4
@@ -207,12 +207,14 @@
     for up, msg in ((-1, ya), (1, yb)):
         entries = side_entries(1, up)
         for e, (f, d) in enumerate(entries):
-            msg[pl.ds(e, 1), :] = mini[f, pl.ds(15 - d if up < 0 else d, 1), :]
+            columns[pl.ds(e, 1), :] = mini[f, pl.ds(15 - d if up < 0 else d, 1), :]
+        v = jnp.where(lane[:8] < 40, columns[pl.ds(0, 8), :], lroll(columns[pl.ds(8, 8), :], 32))
+        msg[pl.ds(0, 8), :] = jnp.where(lane[:8] < 72, v, lroll(columns[pl.ds(16, 8), :], 64))
         lines = [(side, *entry) for side in (-1, 1) for entry in edge_entries(side, up)]
         for e, (side, f, dx, dy) in enumerate(lines):
             plane = nx + 1 - dx if side < 0 else 2 + dx
-            msg[pl.ds(len(entries) + e, 1), :] = ext[f, plane, pl.ds(15 - dy if up < 0 else dy, 1), :]
-        v = msg[pl.ds(len(entries), EDGE_LINES), :]
+            msg[pl.ds(8 + e, 1), :] = ext[f, plane, pl.ds(15 - dy if up < 0 else dy, 1), :]
+        v = msg[pl.ds(8, EDGE_LINES), :]
         turned = v
         for step in (-1, 1):
             here = None
@@ -221,7 +223,7 @@
                 hit = (place >= CORNER * k + hits[0]) & (place <= CORNER * k + hits[-1])
                 here = hit if here is None else here | hit
             turned = jnp.where(here, lroll(v, -step), turned)
-        msg[pl.ds(len(entries), EDGE_LINES), :] = turned
+        msg[pl.ds(8, EDGE_LINES), :] = turned
     ya[...], yb[...] = by_parity("gy", ya[...], yb[...])
 
 
@@ -233,13 +235,14 @@
     return sorted(found, key=lambda entry: z_part(entry[0]))
 
 
-def y_lines(ext, low, high):
-    for side, msg in ((-1, low), (1, high)):
+def y_lines(ext, msg, on_odd, on_even):
+    six = ext.shape[1] - 6
+
+    def fill(side):
         entries = y_entries(side)
-        six = ext.shape[1] - 6
-        msg[pl.ds(six * len(entries), 8), :] = jnp.zeros((8, 128), F32)
         for e, (f, d, first) in enumerate(entries):
             msg[pl.ds(six * e, six), :] = ext[f, pl.ds(first, six), 15 - d if side < 0 else d, :]
+        msg[pl.ds(six * len(entries), 8), :] = jnp.zeros((8, 128), F32)
         for step in (-1, 1):
             hits = [e for e, (f, _, _) in enumerate(entries) if z_part(f) == step]
             start, stop = six * hits[0], six * (hits[-1] + 1)
@@ -248,11 +251,14 @@
             place = bottom + lax.broadcasted_iota(jnp.int32, v.shape, 0)
             msg[pl.ds(bottom, top - bottom), :] = jnp.where((place >= start) & (place < stop), lroll(v, -step), v)
 
-
-def pair_kernel(ext, small, msg, low, high):
-    y_lines(ext, low, high)
+    odd = lax.axis_index("gy") % 2
+    pl.when(odd == 1)(lambda: fill(on_odd))
+    pl.when(odd == 0)(lambda: fill(on_even))
+
+
+def pair_kernel(ext, small, msg):
     msg[pl.ds(0, small.shape[0]), :] = small[...]
-    msg[pl.ds(small.shape[0], low.shape[0]), :] = by_parity("gy", low[...], high[...])[1]
+    y_lines(ext, msg.at[pl.ds(small.shape[0], msg.shape[0] - small.shape[0]), :], 1, -1)
 
 
 def x_kernel(ext, xmsg):
@@ -263,13 +269,16 @@
             xmsg[s, e] = lroll(ext[f, plane, pl.ds(0, 16), :], -z_part(f))
 
 
-def yz_kernel(mini_in, ra, rb, mini, za, zb, low, high):
+def yz_kernel(mini_in, ra, rb, mini, za, zb, low, high, columns):
     lane = lane_ids(ROWS)
     low[...], high[...] = by_parity("gy", rb[pl.ds(0, low.shape[0]), :], ra[...])
     for side, msg in ((-1, low), (1, high)):
         entries = side_entries(1, side)
+        for k in range(3):
+            columns[pl.ds(8 * k, 8), :] = lroll(msg[pl.ds(0, 8), :], -32 * k)
         for e, (f, d) in enumerate(entries):
-            mini[f, pl.ds(23 - d if side < 0 else 16 + d, 1), :] = msg[pl.ds(e, 1), :]
+            mini[f, pl.ds(23 - d if side < 0 else 16 + d, 1), :] = columns[pl.ds(e, 1), :]
+    tile_row = lax.broadcasted_iota(jnp.int32, (8, 128), 0)
     for side, msg in ((-1, za), (1, zb)):
         tiles = [None, None]
         for f, unit, kind in z_pieces(side):
@@ -280,14 +289,13 @@
                 here = here | (lane % 4 == k)
             t = unit // 8
             tiles[t] = v if tiles[t] is None else jnp.where((lane // 32 == block) & here, v, tiles[t])
-        msg[pl.ds(0, ROWS), :] = tiles[0]
+        msg[pl.ds(0, 16), :] = tiles[0][:16]
+        msg[pl.ds(16, 8), :] = jnp.where((tile_row >= 2) & (tile_row < 6), pltpu.roll(tiles[1][16:], 4, 0), tiles[0][16:])
         msg[pl.ds(ROWS, 8), :] = jnp.where(lane[:8] < 64, tiles[1][:8], lroll(tiles[1][8:16], 64))
-        msg[pl.ds(ROWS + 8, 8), :] = tiles[1][16:]
-
-
-def y_kernel(ext, mini, msg, low, high):
-    y_lines(ext, low, high)
-    msg[...] = by_parity("gy", low[...], high[...])[0]
+
+
+def y_kernel(ext, mini, msg):
+    y_lines(ext, msg, -1, 1)
 
 
 Z_PAIRS = ((5, 6), (11, 13), (14, 12), (15, 17), (18, 16))
@@ -316,7 +324,7 @@
         mini[f] = e
     for side, msg in ((-1, ra), (1, rb)):
         second = msg[pl.ds(ROWS, 8), :]
-        tiles = (msg[pl.ds(0, ROWS), :], jnp.concatenate([second, lroll(second, 64), msg[pl.ds(ROWS + 8, 8), :]], axis=0))
+        tiles = (msg[pl.ds(0, ROWS), :], jnp.concatenate([second, lroll(second, 64), pltpu.roll(msg[pl.ds(16, 8), :], 4, 0)], axis=0))
         start, slots = (8, (0, 1)) if side < 0 else (72, (2, 3))
         near = slots[1] if side < 0 else slots[0]
         inside = (lane >= start) & (lane < start + 32)
@@ -343,7 +351,7 @@
         xmsg[s, pl.ds(EDGE_LINES - 8, 8), :] = pltpu.roll(acc[16:], 6, 0)
         xmsg[s, pl.ds(EDGE_LINES, 16), :] = acc[:16]
         for k, msg in enumerate((ya, yb)):
-            start = len(side_entries(1, 1)) + CORNER * s
+            start = 8 + CORNER * s
             xmsg[s, pl.ds(CORNER * k, CORNER), :] = msg[pl.ds(start, CORNER), :]
 
 
@@ -518,7 +526,7 @@
         lines = [(side, *entry) for side in (-1, 1) for entry in edge_entries(side, up)]
         for e, (side, f, dx, dy) in enumerate(lines):
             plane, row = nx + 1 - dx if side < 0 else 2 + dx, 23 - dy if up < 0 else 16 + dy
-            ext[f, plane, pl.ds(row, 1), :] = small[pl.ds(len(side_entries(1, up)) + e, 1), :]
+            ext[f, plane, pl.ds(row, 1), :] = small[pl.ds(8 + e, 1), :]
     for k, (up, down) in enumerate(Z_PAIRS):
         ends[k] = z_ends(mini[up, rows, :], mini[down, rows, :])
 
@@ -606,19 +614,18 @@
 def per_device(populations, adjoint_next):
     nx = populations.shape[1]
     ext_shape, mini_shape, plane_shape = (FIELDS, nx + 4, ROWS, 128), (FIELDS, ROWS, 128), (nx + 4, ROWS, 128)
-    small_y = (len(side_entries(1, 1)) + EDGE_LINES, 128)
+    small_y = (8 + EDGE_LINES, 128)
     ext, mini, ya, yb = call(
         load_kernel,
         tuple(pltpu.with_memory_space_constraint(v, pltpu.HBM) for v in (populations, adjoint_next)),
         (ext_shape, mini_shape, small_y, small_y),
-        scratch=[pltpu.VMEM((19, nx, 16, 128), F32), pltpu.SemaphoreType.DMA((10,))],
+        scratch=[pltpu.VMEM((19, nx, 16, 128), F32), pltpu.VMEM((24, 128), F32), pltpu.SemaphoreType.DMA((10,))],
         in_specs=[HB, HB],
         name="load",
     )
     large_y = (24 * (nx - 2) + 8, 128)
-    two_large = [pltpu.VMEM(large_y, F32), pltpu.VMEM(large_y, F32)]
     (yb,) = call(
-        pair_kernel, (ext, yb), ((small_y[0] + large_y[0], 128),), scratch=two_large, name="pair", cost=COSTLY
+        pair_kernel, (ext, yb), ((small_y[0] + large_y[0], 128),), name="pair", cost=COSTLY
     )
     (xmsg,) = call(x_kernel, (ext,), ((2, 24, 16, 128),), name="xpack", cost=COSTLY)
     x1 = swap_both(xmsg, "gx")
@@ -626,11 +633,12 @@
     mini, za, zb, ya, yb = call(
         yz_kernel,
         (mini, ya, y2b),
-        (mini_shape, (ROWS + 16, 128), (ROWS + 16, 128), small_y, small_y),
+        (mini_shape, (ROWS + 8, 128), (ROWS + 8, 128), small_y, small_y),
+        scratch=[pltpu.VMEM((24, 128), F32)],
         aliases={0: 0},
         name="yz",
     )
-    (y2a,) = call(y_kernel, (ext, mini), (large_y,), scratch=two_large, name="ypack", cost=COSTLY)
+    (y2a,) = call(y_kernel, (ext, mini), (large_y,), name="ypack", cost=COSTLY)
     y2a = ppermute_pairs(y2a, "gy", 1)
     za, zb = swap(za, zb, "gz")
     mini, xmsg2 = call(

time: 20.2 us -> 20.1 us (level)
  transfers between devices with their start and end apart: 7 -> 7, of which waited for: 3 -> 2; matrix products, arithmetic and copies ran while one was open for 0% -> 0% of each run, Pallas kernels for 17% -> 17%
where the time goes in v6:
time: 20.1 us; the launch traced here: 20 us
  starting transfers between devices  11.3 us (56%)
  Pallas kernels  7.2 us (36%)
  waiting for transfers between devices  1.46 us (7%)
    pallas_call x10, Pallas kernels, call(): pl.pallas_call(body, in_specs=in_specs or [VM] * len(ins), out_specs=out_...  7.2 us
    ppermute x3, starting transfers between devices, ppermute_pairs(): return lax.ppermute(msg, axis, found)  4.23 us
    ppermute x2, starting transfers between devices, swap_both(): return lax.ppermute(msg, axis, [(0, 1), (1, 0)])  3.16 us
    ppermute x1, starting transfers between devices, swap(): lax.ppermute(high, axis, [(j, i) for i, j in up])  2.1 us
    ppermute x1, starting transfers between devices, swap(): lax.ppermute(low, axis, up)  1.78 us
    ppermute x2, waiting for transfers between devices, swap_both(): return lax.ppermute(msg, axis, [(0, 1), (1, 0)])  0.8 us
    ppermute x1, waiting for transfers between devices, swap(): lax.ppermute(low, axis, up)  0.65 us
  transfers between devices with their start and end apart: 7, of which 2 were waited for; matrix products, arithmetic and copies ran while one was open for 0% of the time, Pallas kernels for 17%

profile of v6, /device:TPU:0, one launch (start us, length us, event | category | flops | bytes accessed | tf_op | source)
XLA Modules:
  0.0 20.0 jit_solution(7986301007706767809)
XLA Ops:
  0.0 2.1 %load.1 = (f32[23,12,24,128]{3,2,1,0:T(8,128)S(1)}, f32[23,24,128]{2,1,0:T(8,128)S(1)}, f32[64,128]{1,0:T(8,128)S(1)}, f32[64,128]{1,0:T(8,128)S(1)}) custom-call(f32[19,8,16,128]{3,2,1,0:T(8,128)} %pop_hbm.1, f32[19,8,16,128]{3,2,1,0:T(8,128)} %adj_hbm.1), custom_call_target="tpu_custom_call" | custom-call | tf_op jit(solution)/shard_map/load/pallas_call | solution.py:148
  2.1 2.5 %collective-permute-start = (f32[64,128]{1,0:T(8,128)S(1)}, f32[64,128]{1,0:T(8,128)S(1)}, u32[]{:S(2)}, u32[]{:S(2)}) collective-permute-start(f32[64,128]{1,0:T(8,128)S(1)} %get-tuple-element.31), channel_id=1, source_target_pairs={{4,8},{8,4},{12,0},{0,12},{5,9},{9,5},{13,1},{1,13},{6,10},{10,6},... | collective-permute-start | bytes 98312 | tf_op jit(solution)/shard_map/ppermute | solution.py:604
  4.5 0.1 pair.1
  4.7 0.7 %collective-permute-start.1 = (f32[216,128]{1,0:T(8,128)S(1)}, f32[216,128]{1,0:T(8,128)S(1)}, u32[]{:S(2)}, u32[]{:S(2)}) collective-permute-start(f32[216,128]{1,0:T(8,128)S(1)} %pair.1), channel_id=1, source_target_pairs={{0,4},{4,0},{8,12},{12,8},{1,5},{5,1},{9,13},{13,9},{2,6},{6,2},{1... | collective-permute-start | bytes 331784 | tf_op jit(solution)/shard_map/ppermute | solution.py:604
  5.4 0.1 xpack.1
  5.5 1.6 %collective-permute-start.5 = (f32[2,24,16,128]{3,2,1,0:T(8,128)S(1)}, f32[2,24,16,128]{3,2,1,0:T(8,128)S(1)}, u32[]{:S(2)}, u32[]{:S(2)}) collective-permute-start(f32[2,24,16,128]{3,2,1,0:T(8,128)S(1)} %xpack.1), channel_id=1, source_target_pairs={{0,16},{16,0},{1,17},{17,1},{2,18},{18,2},{3,19},{19,3},{4,20},{20... | collective-permute-start | bytes 1179656 | tf_op jit(solution)/shard_map/ppermute | solution.py:610
  7.1 0.0 collective-permute-done.ra
  7.1 0.0 collective-permute-done.1.rb
  7.1 0.2 %yz.1 = (f32[23,24,128]{2,1,0:T(8,128)S(1)}, f32[32,128]{1,0:T(8,128)S(1)}, f32[32,128]{1,0:T(8,128)S(1)}, f32[64,128]{1,0:T(8,128)S(1)}, f32[64,128]{1,0:T(8,128)S(1)}) custom-call(f32[23,24,128]{2,1,0:T(8,128)S(1)} %get-tuple-element.30.mini_in, f32[64,128]{1,0:T(8,128)S(1)} %collective-permute-done.ra, ...), custom_call_target="tpu_custom_call", output_to_operand_aliasing={{0}: (0, {})} | custom-call | tf_op jit(solution)/shard_map/yz/pallas_call | solution.py:148
  7.3 1.8 %collective-permute-start.2 = (f32[32,128]{1,0:T(8,128)S(1)}, f32[32,128]{1,0:T(8,128)S(1)}, u32[]{:S(2)}, u32[]{:S(2)}) collective-permute-start(f32[32,128]{1,0:T(8,128)S(1)} %get-tuple-element.34), channel_id=1, source_target_pairs={{0,1},{1,2},{2,3},{3,0},{4,5},{5,6},{6,7},{7,4},{8,9},{9,10},{10,1... | collective-permute-start | bytes 49160 | tf_op jit(solution)/shard_map/ppermute | solution.py:596
  9.1 2.1 %collective-permute-start.3 = (f32[32,128]{1,0:T(8,128)S(1)}, f32[32,128]{1,0:T(8,128)S(1)}, u32[]{:S(2)}, u32[]{:S(2)}) collective-permute-start(f32[32,128]{1,0:T(8,128)S(1)} %get-tuple-element.35), channel_id=1, source_target_pairs={{1,0},{2,1},{3,2},{0,3},{5,4},{6,5},{7,6},{4,7},{9,8},{10,9},{11,1... | collective-permute-start | bytes 49160 | tf_op jit(solution)/shard_map/ppermute | solution.py:596
  11.2 0.1 ypack.1
  11.3 1.0 %collective-permute-start.4 = (f32[152,128]{1,0:T(8,128)S(1)}, f32[152,128]{1,0:T(8,128)S(1)}, u32[]{:S(2)}, u32[]{:S(2)}) collective-permute-start(f32[152,128]{1,0:T(8,128)S(1)} %ypack.1), channel_id=1, source_target_pairs={{4,8},{8,4},{12,0},{0,12},{5,9},{9,5},{13,1},{1,13},{6,10},{10,6},... | collective-permute-start | bytes 233480 | tf_op jit(solution)/shard_map/ppermute | solution.py:604
  12.3 0.6 %collective-permute-done.2.ra = f32[32,128]{1,0:T(8,128)S(1)} collective-permute-done((f32[32,128]{1,0:T(8,128)S(1)}, f32[32,128]{1,0:T(8,128)S(1)}, u32[]{:S(2)}, u32[]{:S(2)}) %collective-permute-start.2) | collective-permute-done | bytes 16416 | tf_op jit(solution)/shard_map/ppermute | solution.py:596
  13.0 0.0 collective-permute-done.3.rb
  13.0 0.4 %zx.1 = (f32[23,24,128]{2,1,0:T(8,128)S(1)}, f32[2,72,128]{2,1,0:T(8,128)S(1)}) custom-call(f32[23,24,128]{2,1,0:T(8,128)S(1)} %get-tuple-element.33.mini_in.mini, f32[32,128]{1,0:T(8,128)S(1)} %collective-permute-done.2.ra, f32[32,128]{1,0:T(8,128)S(1)} %collective-permute-done.3.rb, ...), custom_call_target="tpu_custom_call", output_to_operand_aliasing={{0}: (0, {})} | custom-call | tf_op jit(solution)/shard_map/zx/pallas_call | solution.py:148
  13.4 1.6 %collective-permute-start.6 = (f32[2,72,128]{2,1,0:T(8,128)S(1)}, f32[2,72,128]{2,1,0:T(8,128)S(1)}, u32[]{:S(2)}, u32[]{:S(2)}) collective-permute-start(f32[2,72,128]{2,1,0:T(8,128)S(1)} %get-tuple-element.46), channel_id=1, source_target_pairs={{0,16},{16,0},{1,17},{17,1},{2,18},{18,2},{3,19},{19,3},{4,20},{20... | collective-permute-start | bytes 221192 | tf_op jit(solution)/shard_map/ppermute | solution.py:610
  15.0 1.2 %turn.1 = (f32[23,12,24,128]{3,2,1,0:T(8,128)S(1)}, f32[24,128]{1,0:T(8,128)S(1)}, f32[24,128]{1,0:T(8,128)S(1)}, f32[12,24,128]{2,1,0:T(8,128)S(1)}, f32[12,24,...) custom-call(f32[23,12,24,128]{3,2,1,0:T(8,128)S(1)} %get-tuple-element.29.ext.ext_in, ...), custom_call_target="tpu_custom_call", output_to_operand_aliasing={{0}: (0, {})} | custom-call | tf_op jit(solution)/shard_map/turn/pallas_call | solution.py:148
  16.2 0.0 collective-permute-done.4.r2
  16.2 1.2 %mid.1 = (f32[23,12,24,128]{3,2,1,0:T(8,128)S(1)}, f32[12,24,128]{2,1,0:T(8,128)S(1)}, f32[12,24,128]{2,1,0:T(8,128)S(1)}, f32[12,24,128]{2,1,0:T(8,128)S(1)}, f...) custom-call(f32[23,12,24,128]{3,2,1,0:T(8,128)S(1)} %get-tuple-eleme, ...), custom_call_target="tpu_custom_call", output_to_operand_aliasing={{0}: (0, {}), {1}: (8, {}), {2}: (9, {}), {3}: (10, {})} | custom-call | tf_op jit(solution)/shard_map/mid/pallas_call | solution.py:148
  17.3 0.0 collective-permute-done.5.r1
  17.4 0.8 %collective-permute-done.6.r2 = f32[2,72,128]{2,1,0:T(8,128)S(1)} collective-permute-done((f32[2,72,128]{2,1,0:T(8,128)S(1)}, f32[2,72,128]{2,1,0:T(8,128)S(1)}, u32[]{:S(2)}, u32[]{:S(2)}) %collective-permute-start.6) | collective-permute-done | bytes 73760 | tf_op jit(solution)/shard_map/ppermute | solution.py:610
  18.2 1.8 %last.1 = (f32[23,12,24,128]{3,2,1,0:T(8,128)S(1)}, f32[23,24,128]{2,1,0:T(8,128)S(1)}, f32[12,24,128]{2,1,0:T(8,128)S(1)}, f32[12,24,128]{2,1,0:T(8,128)S(1)}, ...) custom-call(f32[23,12,24,128]{3,2,1,0:T(8,128)S(1)} %fill.1.ext_in, ...), custom_call_target="tpu_custom_call", output_to_operand_aliasing={{0}: (0, {}), {1}: (1, {}), {2}: (3, {}), {3}: (4, {}), {4}... | custom-call | tf_op jit(solution)/shard_map/last/pallas_call | solution.py:148
  (1 shorter events, 0.0 us)
Async XLA Ops:
  2.1 5.0 %collective-permute-start = (f32[64,128]{1,0:T(8,128)S(1)}, f32[64,128]{1,0:T(8,128)S(1)}, u32[]{:S(2)}, u32[]{:S(2)}) collective-permute-start(f32[64,128]{1,0:T(8,128)S(1)} %get-tuple-element.31), channel_id=1, source_target_pairs={{4,8},{8,4},{12,0},{0,12},{5,9},{9,5},{13,1},{1,13},{6,10},{10,6},... | collective-permute-start | bytes 98312 | tf_op jit(solution)/shard_map/ppermute | solution.py:604
  4.7 2.4 %collective-permute-start.1 = (f32[216,128]{1,0:T(8,128)S(1)}, f32[216,128]{1,0:T(8,128)S(1)}, u32[]{:S(2)}, u32[]{:S(2)}) collective-permute-start(f32[216,128]{1,0:T(8,128)S(1)} %pair.1), channel_id=1, source_target_pairs={{0,4},{4,0},{8,12},{12,8},{1,5},{5,1},{9,13},{13,9},{2,6},{6,2},{1... | collective-permute-start | bytes 331784 | tf_op jit(solution)/shard_map/ppermute | solution.py:604
  5.5 11.8 %collective-permute-start.5 = (f32[2,24,16,128]{3,2,1,0:T(8,128)S(1)}, f32[2,24,16,128]{3,2,1,0:T(8,128)S(1)}, u32[]{:S(2)}, u32[]{:S(2)}) collective-permute-start(f32[2,24,16,128]{3,2,1,0:T(8,128)S(1)} %xpack.1), channel_id=1, source_target_pairs={{0,16},{16,0},{1,17},{17,1},{2,18},{18,2},{3,19},{19,3},{4,20},{20... | collective-permute-start | bytes 1179656 | tf_op jit(solution)/shard_map/ppermute | solution.py:610
  7.3 5.7 %collective-permute-start.2 = (f32[32,128]{1,0:T(8,128)S(1)}, f32[32,128]{1,0:T(8,128)S(1)}, u32[]{:S(2)}, u32[]{:S(2)}) collective-permute-start(f32[32,128]{1,0:T(8,128)S(1)} %get-tuple-element.34), channel_id=1, source_target_pairs={{0,1},{1,2},{2,3},{3,0},{4,5},{5,6},{6,7},{7,4},{8,9},{9,10},{10,1... | collective-permute-start | bytes 49160 | tf_op jit(solution)/shard_map/ppermute | solution.py:596
  9.1 3.9 %collective-permute-start.3 = (f32[32,128]{1,0:T(8,128)S(1)}, f32[32,128]{1,0:T(8,128)S(1)}, u32[]{:S(2)}, u32[]{:S(2)}) collective-permute-start(f32[32,128]{1,0:T(8,128)S(1)} %get-tuple-element.35), channel_id=1, source_target_pairs={{1,0},{2,1},{3,2},{0,3},{5,4},{6,5},{7,6},{4,7},{9,8},{10,9},{11,1... | collective-permute-start | bytes 49160 | tf_op jit(solution)/shard_map/ppermute | solution.py:596
  11.3 4.9 %collective-permute-start.4 = (f32[152,128]{1,0:T(8,128)S(1)}, f32[152,128]{1,0:T(8,128)S(1)}, u32[]{:S(2)}, u32[]{:S(2)}) collective-permute-start(f32[152,128]{1,0:T(8,128)S(1)} %ypack.1), channel_id=1, source_target_pairs={{4,8},{8,4},{12,0},{0,12},{5,9},{9,5},{13,1},{1,13},{6,10},{10,6},... | collective-permute-start | bytes 233480 | tf_op jit(solution)/shard_map/ppermute | solution.py:604
  13.4 4.8 %collective-permute-start.6 = (f32[2,72,128]{2,1,0:T(8,128)S(1)}, f32[2,72,128]{2,1,0:T(8,128)S(1)}, u32[]{:S(2)}, u32[]{:S(2)}) collective-permute-start(f32[2,72,128]{2,1,0:T(8,128)S(1)} %get-tuple-element.46), channel_id=1, source_target_pairs={{0,16},{16,0},{1,17},{17,1},{2,18},{18,2},{3,19},{19,3},{4,20},{20... | collective-permute-start | bytes 221192 | tf_op jit(solution)/shard_map/ppermute | solution.py:610

commit v7 on v5

--- a/solution.py
+++ b/solution.py
@@ -182,6 +182,34 @@
         copies[k].wait()
         for i in range(n):
             edges(f + i)
+
+    def y_edges(wanted):
+        for up, msg in ((-1, ya), (1, yb)):
+            entries = side_entries(1, up)
+            for e, (f, d) in enumerate(entries):
+                if wanted(f):
+                    msg[pl.ds(e, 1), :] = mini[f, pl.ds(15 - d if up < 0 else d, 1), :]
+            lines = [(side, *entry) for side in (-1, 1) for entry in edge_entries(side, up)]
+            for e, (side, f, dx, dy) in enumerate(lines):
+                plane = nx + 1 - dx if side < 0 else 2 + dx
+                if wanted(f):
+                    msg[pl.ds(len(entries) + e, 1), :] = ext[f, plane, pl.ds(15 - dy if up < 0 else dy, 1), :]
+
+    y_edges(lambda f: f < RHO)
+    place = lax.broadcasted_iota(jnp.int32, (EDGE_LINES, 128), 0)
+    for up, msg in ((-1, ya), (1, yb)):
+        entries = side_entries(1, up)
+        lines = [(side, *entry) for side in (-1, 1) for entry in edge_entries(side, up)]
+        v = msg[pl.ds(len(entries), EDGE_LINES), :]
+        turned = v
+        for step in (-1, 1):
+            here = None
+            for k in (0, 1):
+                hits = [e for e in range(CORNER) if z_part(lines[CORNER * k + e][1]) == step]
+                hit = (place >= CORNER * k + hits[0]) & (place <= CORNER * k + hits[-1])
+                here = hit if here is None else here | hit
+            turned = jnp.where(here, lroll(v, -step), turned)
+        msg[pl.ds(len(entries), EDGE_LINES), :] = turned
     for c in copies[5:]:
         c.wait()
 
@@ -203,25 +231,7 @@
     lax.fori_loop(0, nx, moments, 0, unroll=2)
     for f in range(RHO, FIELDS):
         edges(f)
-    place = lax.broadcasted_iota(jnp.int32, (EDGE_LINES, 128), 0)
-    for up, msg in ((-1, ya), (1, yb)):
-        entries = side_entries(1, up)
-        for e, (f, d) in enumerate(entries):
-            msg[pl.ds(e, 1), :] = mini[f, pl.ds(15 - d if up < 0 else d, 1), :]
-        lines = [(side, *entry) for side in (-1, 1) for entry in edge_entries(side, up)]
-        for e, (side, f, dx, dy) in enumerate(lines):
-            plane = nx + 1 - dx if side < 0 else 2 + dx
-            msg[pl.ds(len(entries) + e, 1), :] = ext[f, plane, pl.ds(15 - dy if up < 0 else dy, 1), :]
-        v = msg[pl.ds(len(entries), EDGE_LINES), :]
-        turned = v
-        for step in (-1, 1):
-            here = None
-            for k in (0, 1):
-                hits = [e for e in range(CORNER) if z_part(lines[CORNER * k + e][1]) == step]
-                hit = (place >= CORNER * k + hits[0]) & (place <= CORNER * k + hits[-1])
-                here = hit if here is None else here | hit
-            turned = jnp.where(here, lroll(v, -step), turned)
-        msg[pl.ds(len(entries), EDGE_LINES), :] = turned
+    y_edges(lambda f: f >= RHO)
     ya[...], yb[...] = by_parity("gy", ya[...], yb[...])
 
 
@@ -233,13 +243,14 @@
     return sorted(found, key=lambda entry: z_part(entry[0]))
 
 
-def y_lines(ext, low, high):
-    for side, msg in ((-1, low), (1, high)):
+def y_lines(ext, msg, on_odd, on_even):
+    six = ext.shape[1] - 6
+
+    def fill(side):
         entries = y_entries(side)
-        six = ext.shape[1] - 6
-        msg[pl.ds(six * len(entries), 8), :] = jnp.zeros((8, 128), F32)
         for e, (f, d, first) in enumerate(entries):
             msg[pl.ds(six * e, six), :] = ext[f, pl.ds(first, six), 15 - d if side < 0 else d, :]
+        msg[pl.ds(six * len(entries), 8), :] = jnp.zeros((8, 128), F32)
         for step in (-1, 1):
             hits = [e for e, (f, _, _) in enumerate(entries) if z_part(f) == step]
             start, stop = six * hits[0], six * (hits[-1] + 1)
@@ -248,11 +259,14 @@
             place = bottom + lax.broadcasted_iota(jnp.int32, v.shape, 0)
             msg[pl.ds(bottom, top - bottom), :] = jnp.where((place >= start) & (place < stop), lroll(v, -step), v)
 
-
-def pair_kernel(ext, small, msg, low, high):
-    y_lines(ext, low, high)
+    odd = lax.axis_index("gy") % 2
+    pl.when(odd == 1)(lambda: fill(on_odd))
+    pl.when(odd == 0)(lambda: fill(on_even))
+
+
+def pair_kernel(ext, small, msg):
     msg[pl.ds(0, small.shape[0]), :] = small[...]
-    msg[pl.ds(small.shape[0], low.shape[0]), :] = by_parity("gy", low[...], high[...])[1]
+    y_lines(ext, msg.at[pl.ds(small.shape[0], msg.shape[0] - small.shape[0]), :], 1, -1)
 
 
 def x_kernel(ext, xmsg):
@@ -285,9 +299,8 @@
         msg[pl.ds(ROWS + 8, 8), :] = tiles[1][16:]
 
 
-def y_kernel(ext, mini, msg, low, high):
-    y_lines(ext, low, high)
-    msg[...] = by_parity("gy", low[...], high[...])[0]
+def y_kernel(ext, mini, msg):
+    y_lines(ext, msg, -1, 1)
 
 
 Z_PAIRS = ((5, 6), (11, 13), (14, 12), (15, 17), (18, 16))
@@ -616,9 +629,8 @@
         name="load",
     )
     large_y = (24 * (nx - 2) + 8, 128)
-    two_large = [pltpu.VMEM(large_y, F32), pltpu.VMEM(large_y, F32)]
     (yb,) = call(
-        pair_kernel, (ext, yb), ((small_y[0] + large_y[0], 128),), scratch=two_large, name="pair", cost=COSTLY
+        pair_kernel, (ext, yb), ((small_y[0] + large_y[0], 128),), name="pair", cost=COSTLY
     )
     (xmsg,) = call(x_kernel, (ext,), ((2, 24, 16, 128),), name="xpack", cost=COSTLY)
     x1 = swap_both(xmsg, "gx")
@@ -630,7 +642,7 @@
         aliases={0: 0},
         name="yz",
     )
-    (y2a,) = call(y_kernel, (ext, mini), (large_y,), scratch=two_large, name="ypack", cost=COSTLY)
+    (y2a,) = call(y_kernel, (ext, mini), (large_y,), name="ypack", cost=COSTLY)
     y2a = ppermute_pairs(y2a, "gy", 1)
     za, zb = swap(za, zb, "gz")
     mini, xmsg2 = call(

time: 20.2 us -> 20.1 us (level)
  no operation moved by 1% of the time
where the time goes in v7:
time: 20.1 us; the launch traced here: 19.9 us
  starting transfers between devices  11.4 us (57%)
  Pallas kernels  7.18 us (36%)
  waiting for transfers between devices  1.31 us (7%)
    pallas_call x10, Pallas kernels, call(): pl.pallas_call(body, in_specs=in_specs or [VM] * len(ins), out_specs=out_...  7.18 us
    ppermute x3, starting transfers between devices, ppermute_pairs(): return lax.ppermute(msg, axis, found)  4.23 us
    ppermute x2, starting transfers between devices, swap_both(): return lax.ppermute(msg, axis, [(0, 1), (1, 0)])  3.12 us
    ppermute x1, starting transfers between devices, swap(): lax.ppermute(high, axis, [(j, i) for i, j in up])  2.09 us
    ppermute x1, starting transfers between devices, swap(): lax.ppermute(low, axis, up)  1.95 us
    ppermute x1, waiting for transfers between devices, swap(): lax.ppermute(low, axis, up)  0.65 us
    ppermute x2, waiting for transfers between devices, swap_both(): return lax.ppermute(msg, axis, [(0, 1), (1, 0)])  0.57 us
  transfers between devices with their start and end apart: 7, of which 3 were waited for; matrix products, arithmetic and copies ran while one was open for 0% of the time, Pallas kernels for 17%

profile of v7, /device:TPU:0, one launch (start us, length us, event | category | flops | bytes accessed | tf_op | source)
XLA Modules:
  0.0 19.9 jit_solution(3113155206006922408)
XLA Ops:
  0.0 2.0 %load.1 = (f32[23,12,24,128]{3,2,1,0:T(8,128)S(1)}, f32[23,24,128]{2,1,0:T(8,128)S(1)}, f32[80,128]{1,0:T(8,128)S(1)}, f32[80,128]{1,0:T(8,128)S(1)}) custom-call(f32[19,8,16,128]{3,2,1,0:T(8,128)} %pop_hbm.1, f32[19,8,16,128]{3,2,1,0:T(8,128)} %adj_hbm.1), custom_call_target="tpu_custom_call" | custom-call | tf_op jit(solution)/shard_map/load/pallas_call | solution.py:148
  2.0 2.5 %collective-permute-start = (f32[80,128]{1,0:T(8,128)S(1)}, f32[80,128]{1,0:T(8,128)S(1)}, u32[]{:S(2)}, u32[]{:S(2)}) collective-permute-start(f32[80,128]{1,0:T(8,128)S(1)} %get-tuple-element.31), channel_id=1, source_target_pairs={{4,8},{8,4},{12,0},{0,12},{5,9},{9,5},{13,1},{1,13},{6,10},{10,6},... | collective-permute-start | bytes 122888 | tf_op jit(solution)/shard_map/ppermute | solution.py:609
  4.5 0.1 pair.1
  4.6 0.7 %collective-permute-start.1 = (f32[232,128]{1,0:T(8,128)S(1)}, f32[232,128]{1,0:T(8,128)S(1)}, u32[]{:S(2)}, u32[]{:S(2)}) collective-permute-start(f32[232,128]{1,0:T(8,128)S(1)} %pair.1), channel_id=1, source_target_pairs={{0,4},{4,0},{8,12},{12,8},{1,5},{5,1},{9,13},{13,9},{2,6},{6,2},{1... | collective-permute-start | bytes 356360 | tf_op jit(solution)/shard_map/ppermute | solution.py:609
  5.3 0.1 xpack.1
  5.5 1.6 %collective-permute-start.5 = (f32[2,24,16,128]{3,2,1,0:T(8,128)S(1)}, f32[2,24,16,128]{3,2,1,0:T(8,128)S(1)}, u32[]{:S(2)}, u32[]{:S(2)}) collective-permute-start(f32[2,24,16,128]{3,2,1,0:T(8,128)S(1)} %xpack.1), channel_id=1, source_target_pairs={{0,16},{16,0},{1,17},{17,1},{2,18},{18,2},{3,19},{19,3},{4,20},{20... | collective-permute-start | bytes 1179656 | tf_op jit(solution)/shard_map/ppermute | solution.py:615
  7.0 0.0 collective-permute-done.ra
  7.0 0.0 collective-permute-done.1.rb
  7.0 0.2 %yz.1 = (f32[23,24,128]{2,1,0:T(8,128)S(1)}, f32[40,128]{1,0:T(8,128)S(1)}, f32[40,128]{1,0:T(8,128)S(1)}, f32[80,128]{1,0:T(8,128)S(1)}, f32[80,128]{1,0:T(8,128)S(1)}) custom-call(f32[23,24,128]{2,1,0:T(8,128)S(1)} %get-tuple-element.30.mini_in, f32[80,128]{1,0:T(8,128)S(1)} %collective-permute-done.ra, ...), custom_call_target="tpu_custom_call", output_to_operand_aliasing={{0}: (0, {})} | custom-call | tf_op jit(solution)/shard_map/yz/pallas_call | solution.py:148
  7.3 2.0 %collective-permute-start.2 = (f32[40,128]{1,0:T(8,128)S(1)}, f32[40,128]{1,0:T(8,128)S(1)}, u32[]{:S(2)}, u32[]{:S(2)}) collective-permute-start(f32[40,128]{1,0:T(8,128)S(1)} %get-tuple-element.34), channel_id=1, source_target_pairs={{0,1},{1,2},{2,3},{3,0},{4,5},{5,6},{6,7},{7,4},{8,9},{9,10},{10,1... | collective-permute-start | bytes 61448 | tf_op jit(solution)/shard_map/ppermute | solution.py:601
  9.2 2.1 %collective-permute-start.3 = (f32[40,128]{1,0:T(8,128)S(1)}, f32[40,128]{1,0:T(8,128)S(1)}, u32[]{:S(2)}, u32[]{:S(2)}) collective-permute-start(f32[40,128]{1,0:T(8,128)S(1)} %get-tuple-element.35), channel_id=1, source_target_pairs={{1,0},{2,1},{3,2},{0,3},{5,4},{6,5},{7,6},{4,7},{9,8},{10,9},{11,1... | collective-permute-start | bytes 61448 | tf_op jit(solution)/shard_map/ppermute | solution.py:601
  11.3 0.1 ypack.1
  11.4 1.1 %collective-permute-start.4 = (f32[152,128]{1,0:T(8,128)S(1)}, f32[152,128]{1,0:T(8,128)S(1)}, u32[]{:S(2)}, u32[]{:S(2)}) collective-permute-start(f32[152,128]{1,0:T(8,128)S(1)} %ypack.1), channel_id=1, source_target_pairs={{4,8},{8,4},{12,0},{0,12},{5,9},{9,5},{13,1},{1,13},{6,10},{10,6},... | collective-permute-start | bytes 233480 | tf_op jit(solution)/shard_map/ppermute | solution.py:609
  12.5 0.6 %collective-permute-done.2.ra = f32[40,128]{1,0:T(8,128)S(1)} collective-permute-done((f32[40,128]{1,0:T(8,128)S(1)}, f32[40,128]{1,0:T(8,128)S(1)}, u32[]{:S(2)}, u32[]{:S(2)}) %collective-permute-start.2) | collective-permute-done | bytes 20512 | tf_op jit(solution)/shard_map/ppermute | solution.py:601
  13.1 0.1 collective-permute-done.3.rb
  13.2 0.4 %zx.1 = (f32[23,24,128]{2,1,0:T(8,128)S(1)}, f32[2,72,128]{2,1,0:T(8,128)S(1)}) custom-call(f32[23,24,128]{2,1,0:T(8,128)S(1)} %get-tuple-element.33.mini_in.mini, f32[40,128]{1,0:T(8,128)S(1)} %collective-permute-done.2.ra, f32[40,128]{1,0:T(8,128)S(1)} %collective-permute-done.3.rb, ...), custom_call_target="tpu_custom_call", output_to_operand_aliasing={{0}: (0, {})} | custom-call | tf_op jit(solution)/shard_map/zx/pallas_call | solution.py:148
  13.6 1.6 %collective-permute-start.6 = (f32[2,72,128]{2,1,0:T(8,128)S(1)}, f32[2,72,128]{2,1,0:T(8,128)S(1)}, u32[]{:S(2)}, u32[]{:S(2)}) collective-permute-start(f32[2,72,128]{2,1,0:T(8,128)S(1)} %get-tuple-element.46), channel_id=1, source_target_pairs={{0,16},{16,0},{1,17},{17,1},{2,18},{18,2},{3,19},{19,3},{4,20},{20... | collective-permute-start | bytes 221192 | tf_op jit(solution)/shard_map/ppermute | solution.py:615
  15.2 1.2 %turn.1 = (f32[23,12,24,128]{3,2,1,0:T(8,128)S(1)}, f32[24,128]{1,0:T(8,128)S(1)}, f32[24,128]{1,0:T(8,128)S(1)}, f32[12,24,128]{2,1,0:T(8,128)S(1)}, f32[12,24,...) custom-call(f32[23,12,24,128]{3,2,1,0:T(8,128)S(1)} %get-tuple-element.29.ext.ext_in, ...), custom_call_target="tpu_custom_call", output_to_operand_aliasing={{0}: (0, {})} | custom-call | tf_op jit(solution)/shard_map/turn/pallas_call | solution.py:148
  16.3 0.0 collective-permute-done.4.r2
  16.4 1.2 %mid.1 = (f32[23,12,24,128]{3,2,1,0:T(8,128)S(1)}, f32[12,24,128]{2,1,0:T(8,128)S(1)}, f32[12,24,128]{2,1,0:T(8,128)S(1)}, f32[12,24,128]{2,1,0:T(8,128)S(1)}, f...) custom-call(f32[23,12,24,128]{3,2,1,0:T(8,128)S(1)} %get-tuple-eleme, ...), custom_call_target="tpu_custom_call", output_to_operand_aliasing={{0}: (0, {}), {1}: (8, {}), {2}: (9, {}), {3}: (10, {})} | custom-call | tf_op jit(solution)/shard_map/mid/pallas_call | solution.py:148
  17.5 0.0 collective-permute-done.5.r1
  17.6 0.6 %collective-permute-done.6.r2 = f32[2,72,128]{2,1,0:T(8,128)S(1)} collective-permute-done((f32[2,72,128]{2,1,0:T(8,128)S(1)}, f32[2,72,128]{2,1,0:T(8,128)S(1)}, u32[]{:S(2)}, u32[]{:S(2)}) %collective-permute-start.6) | collective-permute-done | bytes 73760 | tf_op jit(solution)/shard_map/ppermute | solution.py:615
  18.1 1.8 %last.1 = (f32[23,12,24,128]{3,2,1,0:T(8,128)S(1)}, f32[23,24,128]{2,1,0:T(8,128)S(1)}, f32[12,24,128]{2,1,0:T(8,128)S(1)}, f32[12,24,128]{2,1,0:T(8,128)S(1)}, ...) custom-call(f32[23,12,24,128]{3,2,1,0:T(8,128)S(1)} %fill.1.ext_in, ...), custom_call_target="tpu_custom_call", output_to_operand_aliasing={{0}: (0, {}), {1}: (1, {}), {2}: (3, {}), {3}: (4, {}), {4}... | custom-call | tf_op jit(solution)/shard_map/last/pallas_call | solution.py:148
  (1 shorter events, 0.0 us)
Async XLA Ops:
  2.0 5.0 %collective-permute-start = (f32[80,128]{1,0:T(8,128)S(1)}, f32[80,128]{1,0:T(8,128)S(1)}, u32[]{:S(2)}, u32[]{:S(2)}) collective-permute-start(f32[80,128]{1,0:T(8,128)S(1)} %get-tuple-element.31), channel_id=1, source_target_pairs={{4,8},{8,4},{12,0},{0,12},{5,9},{9,5},{13,1},{1,13},{6,10},{10,6},... | collective-permute-start | bytes 122888 | tf_op jit(solution)/shard_map/ppermute | solution.py:609
  4.6 2.4 %collective-permute-start.1 = (f32[232,128]{1,0:T(8,128)S(1)}, f32[232,128]{1,0:T(8,128)S(1)}, u32[]{:S(2)}, u32[]{:S(2)}) collective-permute-start(f32[232,128]{1,0:T(8,128)S(1)} %pair.1), channel_id=1, source_target_pairs={{0,4},{4,0},{8,12},{12,8},{1,5},{5,1},{9,13},{13,9},{2,6},{6,2},{1... | collective-permute-start | bytes 356360 | tf_op jit(solution)/shard_map/ppermute | solution.py:609
  5.5 12.1 %collective-permute-start.5 = (f32[2,24,16,128]{3,2,1,0:T(8,128)S(1)}, f32[2,24,16,128]{3,2,1,0:T(8,128)S(1)}, u32[]{:S(2)}, u32[]{:S(2)}) collective-permute-start(f32[2,24,16,128]{3,2,1,0:T(8,128)S(1)} %xpack.1), channel_id=1, source_target_pairs={{0,16},{16,0},{1,17},{17,1},{2,18},{18,2},{3,19},{19,3},{4,20},{20... | collective-permute-start | bytes 1179656 | tf_op jit(solution)/shard_map/ppermute | solution.py:615
  7.3 5.9 %collective-permute-start.2 = (f32[40,128]{1,0:T(8,128)S(1)}, f32[40,128]{1,0:T(8,128)S(1)}, u32[]{:S(2)}, u32[]{:S(2)}) collective-permute-start(f32[40,128]{1,0:T(8,128)S(1)} %get-tuple-element.34), channel_id=1, source_target_pairs={{0,1},{1,2},{2,3},{3,0},{4,5},{5,6},{6,7},{7,4},{8,9},{9,10},{10,1... | collective-permute-start | bytes 61448 | tf_op jit(solution)/shard_map/ppermute | solution.py:601
  9.2 4.0 %collective-permute-start.3 = (f32[40,128]{1,0:T(8,128)S(1)}, f32[40,128]{1,0:T(8,128)S(1)}, u32[]{:S(2)}, u32[]{:S(2)}) collective-permute-start(f32[40,128]{1,0:T(8,128)S(1)} %get-tuple-element.35), channel_id=1, source_target_pairs={{1,0},{2,1},{3,2},{0,3},{5,4},{6,5},{7,6},{4,7},{9,8},{10,9},{11,1... | collective-permute-start | bytes 61448 | tf_op jit(solution)/shard_map/ppermute | solution.py:601
  11.4 4.9 %collective-permute-start.4 = (f32[152,128]{1,0:T(8,128)S(1)}, f32[152,128]{1,0:T(8,128)S(1)}, u32[]{:S(2)}, u32[]{:S(2)}) collective-permute-start(f32[152,128]{1,0:T(8,128)S(1)} %ypack.1), channel_id=1, source_target_pairs={{4,8},{8,4},{12,0},{0,12},{5,9},{9,5},{13,1},{1,13},{6,10},{10,6},... | collective-permute-start | bytes 233480 | tf_op jit(solution)/shard_map/ppermute | solution.py:609
  13.6 4.5 %collective-permute-start.6 = (f32[2,72,128]{2,1,0:T(8,128)S(1)}, f32[2,72,128]{2,1,0:T(8,128)S(1)}, u32[]{:S(2)}, u32[]{:S(2)}) collective-permute-start(f32[2,72,128]{2,1,0:T(8,128)S(1)} %get-tuple-element.46), channel_id=1, source_target_pairs={{0,16},{16,0},{1,17},{17,1},{2,18},{18,2},{3,19},{19,3},{4,20},{20... | collective-permute-start | bytes 221192 | tf_op jit(solution)/shard_map/ppermute | solution.py:615

commit v8 on v5

--- a/solution.py
+++ b/solution.py
@@ -263,26 +263,37 @@
             xmsg[s, e] = lroll(ext[f, plane, pl.ds(0, 16), :], -z_part(f))
 
 
-def yz_kernel(mini_in, ra, rb, mini, za, zb, low, high):
-    lane = lane_ids(ROWS)
+def z_tiles(side, mini, rows):
+    lane = lane_ids(rows.size)
+    tiles = [None, None]
+    for f, unit, kind in z_pieces(side):
+        block, shift, slots = z_place(side, unit, kind)
+        v = lroll(mini[f, rows, :], shift)
+        here = lane % 4 == slots[0]
+        for k in slots[1:]:
+            here = here | (lane % 4 == k)
+        t = unit // 8
+        tiles[t] = v if tiles[t] is None else jnp.where((lane // 32 == block) & here, v, tiles[t])
+    return tiles
+
+
+def z_kernel(mini, za, zb):
+    for side, msg in ((-1, za), (1, zb)):
+        tiles = z_tiles(side, mini, pl.ds(0, 16))
+        msg[pl.ds(0, 16), :] = tiles[0]
+        msg[pl.ds(ROWS, 8), :] = jnp.where(lane_ids(8) < 64, tiles[1][:8], lroll(tiles[1][8:], 64))
+
+
+def yz_kernel(mini_in, ra, rb, za_in, zb_in, mini, za, zb, low, high):
     low[...], high[...] = by_parity("gy", rb[pl.ds(0, low.shape[0]), :], ra[...])
     for side, msg in ((-1, low), (1, high)):
         entries = side_entries(1, side)
         for e, (f, d) in enumerate(entries):
             mini[f, pl.ds(23 - d if side < 0 else 16 + d, 1), :] = msg[pl.ds(e, 1), :]
     for side, msg in ((-1, za), (1, zb)):
-        tiles = [None, None]
-        for f, unit, kind in z_pieces(side):
-            block, shift, slots = z_place(side, unit, kind)
-            v = lroll(mini[f], shift)
-            here = lane % 4 == slots[0]
-            for k in slots[1:]:
-                here = here | (lane % 4 == k)
-            t = unit // 8
-            tiles[t] = v if tiles[t] is None else jnp.where((lane // 32 == block) & here, v, tiles[t])
-        msg[pl.ds(0, ROWS), :] = tiles[0]
-        msg[pl.ds(ROWS, 8), :] = jnp.where(lane[:8] < 64, tiles[1][:8], lroll(tiles[1][8:16], 64))
-        msg[pl.ds(ROWS + 8, 8), :] = tiles[1][16:]
+        tiles = z_tiles(side, mini, pl.ds(16, 8))
+        msg[pl.ds(16, 8), :] = tiles[0]
+        msg[pl.ds(ROWS + 8, 8), :] = tiles[1]
 
 
 def y_kernel(ext, mini, msg, low, high):
@@ -623,11 +634,12 @@
     (xmsg,) = call(x_kernel, (ext,), ((2, 24, 16, 128),), name="xpack", cost=COSTLY)
     x1 = swap_both(xmsg, "gx")
     ya, y2b = ppermute_pairs(ya, "gy", 1), ppermute_pairs(yb, "gy", 0)
+    za, zb = call(z_kernel, (mini,), ((ROWS + 16, 128), (ROWS + 16, 128)), name="zpack", cost=COSTLY)
     mini, za, zb, ya, yb = call(
         yz_kernel,
-        (mini, ya, y2b),
+        (mini, ya, y2b, za, zb),
         (mini_shape, (ROWS + 16, 128), (ROWS + 16, 128), small_y, small_y),
-        aliases={0: 0},
+        aliases={0: 0, 3: 1, 4: 2},
         name="yz",
     )
     (y2a,) = call(y_kernel, (ext, mini), (large_y,), scratch=two_large, name="ypack", cost=COSTLY)

time: 20.2 us -> 20.1 us (level)
    pallas_call x10 -> x11, Pallas kernels: 7.26 us -> 7.3 us  [call(): pl.pallas_call(body, in_specs=in_specs or [VM] * len(ins), out_specs=out_...]
  transfers between devices with their start and end apart: 7 -> 7, of which waited for: 3 -> 2; matrix products, arithmetic and copies ran while one was open for 0% -> 0% of each run, Pallas kernels for 17% -> 17%
where the time goes in v8:
time: 20.1 us; the launch traced here: 20 us
  starting transfers between devices  11.2 us (56%)
  Pallas kernels  7.3 us (36%)
  waiting for transfers between devices  1.43 us (7%)
    pallas_call x11, Pallas kernels, call(): pl.pallas_call(body, in_specs=in_specs or [VM] * len(ins), out_specs=out_...  7.3 us
    ppermute x3, starting transfers between devices, ppermute_pairs(): return lax.ppermute(msg, axis, found)  4.21 us
    ppermute x2, starting transfers between devices, swap_both(): return lax.ppermute(msg, axis, [(0, 1), (1, 0)])  3.11 us
    ppermute x1, starting transfers between devices, swap(): lax.ppermute(high, axis, [(j, i) for i, j in up])  2.17 us
    ppermute x1, starting transfers between devices, swap(): lax.ppermute(low, axis, up)  1.7 us
    ppermute x2, waiting for transfers between devices, swap_both(): return lax.ppermute(msg, axis, [(0, 1), (1, 0)])  0.77 us
    ppermute x1, waiting for transfers between devices, swap(): lax.ppermute(low, axis, up)  0.65 us
  transfers between devices with their start and end apart: 7, of which 2 were waited for; matrix products, arithmetic and copies ran while one was open for 0% of the time, Pallas kernels for 17%

profile of v8, /device:TPU:0, one launch (start us, length us, event | category | flops | bytes accessed | tf_op | source)
XLA Modules:
  0.0 20.0 jit_solution(16433677593527605283)
XLA Ops:
  0.0 2.0 %load.1 = (f32[23,12,24,128]{3,2,1,0:T(8,128)S(1)}, f32[23,24,128]{2,1,0:T(8,128)S(1)}, f32[80,128]{1,0:T(8,128)S(1)}, f32[80,128]{1,0:T(8,128)S(1)}) custom-call(f32[19,8,16,128]{3,2,1,0:T(8,128)} %pop_hbm.1, f32[19,8,16,128]{3,2,1,0:T(8,128)} %adj_hbm.1), custom_call_target="tpu_custom_call" | custom-call | tf_op jit(solution)/shard_map/load/pallas_call | solution.py:148
  2.0 2.5 %collective-permute-start = (f32[80,128]{1,0:T(8,128)S(1)}, f32[80,128]{1,0:T(8,128)S(1)}, u32[]{:S(2)}, u32[]{:S(2)}) collective-permute-start(f32[80,128]{1,0:T(8,128)S(1)} %get-tuple-element.33), channel_id=1, source_target_pairs={{4,8},{8,4},{12,0},{0,12},{5,9},{9,5},{13,1},{1,13},{6,10},{10,6},... | collective-permute-start | bytes 122888 | tf_op jit(solution)/shard_map/ppermute | solution.py:607
  4.5 0.2 pair.1
  4.7 0.7 %collective-permute-start.1 = (f32[232,128]{1,0:T(8,128)S(1)}, f32[232,128]{1,0:T(8,128)S(1)}, u32[]{:S(2)}, u32[]{:S(2)}) collective-permute-start(f32[232,128]{1,0:T(8,128)S(1)} %pair.1), channel_id=1, source_target_pairs={{0,4},{4,0},{8,12},{12,8},{1,5},{5,1},{9,13},{13,9},{2,6},{6,2},{1... | collective-permute-start | bytes 356360 | tf_op jit(solution)/shard_map/ppermute | solution.py:607
  5.4 0.1 xpack.1
  5.5 1.6 %collective-permute-start.5 = (f32[2,24,16,128]{3,2,1,0:T(8,128)S(1)}, f32[2,24,16,128]{3,2,1,0:T(8,128)S(1)}, u32[]{:S(2)}, u32[]{:S(2)}) collective-permute-start(f32[2,24,16,128]{3,2,1,0:T(8,128)S(1)} %xpack.1), channel_id=1, source_target_pairs={{0,16},{16,0},{1,17},{17,1},{2,18},{18,2},{3,19},{19,3},{4,20},{20... | collective-permute-start | bytes 1179656 | tf_op jit(solution)/shard_map/ppermute | solution.py:613
  7.1 0.1 zpack.1
  7.2 0.0 collective-permute-done.ra
  7.2 0.0 collective-permute-done.1.rb
  7.2 0.1 yz.1
  7.4 1.7 %collective-permute-start.2 = (f32[40,128]{1,0:T(8,128)S(1)}, f32[40,128]{1,0:T(8,128)S(1)}, u32[]{:S(2)}, u32[]{:S(2)}) collective-permute-start(f32[40,128]{1,0:T(8,128)S(1)} %get-tuple-element.38), channel_id=1, source_target_pairs={{0,1},{1,2},{2,3},{3,0},{4,5},{5,6},{6,7},{7,4},{8,9},{9,10},{10,1... | collective-permute-start | bytes 61448 | tf_op jit(solution)/shard_map/ppermute | solution.py:599
  9.1 2.2 %collective-permute-start.3 = (f32[40,128]{1,0:T(8,128)S(1)}, f32[40,128]{1,0:T(8,128)S(1)}, u32[]{:S(2)}, u32[]{:S(2)}) collective-permute-start(f32[40,128]{1,0:T(8,128)S(1)} %get-tuple-element.39), channel_id=1, source_target_pairs={{1,0},{2,1},{3,2},{0,3},{5,4},{6,5},{7,6},{4,7},{9,8},{10,9},{11,1... | collective-permute-start | bytes 61448 | tf_op jit(solution)/shard_map/ppermute | solution.py:599
  11.3 0.2 ypack.1
  11.4 1.0 %collective-permute-start.4 = (f32[152,128]{1,0:T(8,128)S(1)}, f32[152,128]{1,0:T(8,128)S(1)}, u32[]{:S(2)}, u32[]{:S(2)}) collective-permute-start(f32[152,128]{1,0:T(8,128)S(1)} %ypack.1), channel_id=1, source_target_pairs={{4,8},{8,4},{12,0},{0,12},{5,9},{9,5},{13,1},{1,13},{6,10},{10,6},... | collective-permute-start | bytes 233480 | tf_op jit(solution)/shard_map/ppermute | solution.py:607
  12.4 0.7 %collective-permute-done.2.ra = f32[40,128]{1,0:T(8,128)S(1)} collective-permute-done((f32[40,128]{1,0:T(8,128)S(1)}, f32[40,128]{1,0:T(8,128)S(1)}, u32[]{:S(2)}, u32[]{:S(2)}) %collective-permute-start.2) | collective-permute-done | bytes 20512 | tf_op jit(solution)/shard_map/ppermute | solution.py:599
  13.1 0.0 collective-permute-done.3.rb
  13.1 0.4 %zx.1 = (f32[23,24,128]{2,1,0:T(8,128)S(1)}, f32[2,72,128]{2,1,0:T(8,128)S(1)}) custom-call(f32[23,24,128]{2,1,0:T(8,128)S(1)} %get-tuple-element.37.mini_in.mini, f32[40,128]{1,0:T(8,128)S(1)} %collective-permute-done.2.ra, f32[40,128]{1,0:T(8,128)S(1)} %collective-permute-done.3.rb, ...), custom_call_target="tpu_custom_call", output_to_operand_aliasing={{0}: (0, {})} | custom-call | tf_op jit(solution)/shard_map/zx/pallas_call | solution.py:148
  13.5 1.6 %collective-permute-start.6 = (f32[2,72,128]{2,1,0:T(8,128)S(1)}, f32[2,72,128]{2,1,0:T(8,128)S(1)}, u32[]{:S(2)}, u32[]{:S(2)}) collective-permute-start(f32[2,72,128]{2,1,0:T(8,128)S(1)} %get-tuple-element.50), channel_id=1, source_target_pairs={{0,16},{16,0},{1,17},{17,1},{2,18},{18,2},{3,19},{19,3},{4,20},{20... | collective-permute-start | bytes 221192 | tf_op jit(solution)/shard_map/ppermute | solution.py:613
  15.0 1.2 %turn.1 = (f32[23,12,24,128]{3,2,1,0:T(8,128)S(1)}, f32[24,128]{1,0:T(8,128)S(1)}, f32[24,128]{1,0:T(8,128)S(1)}, f32[12,24,128]{2,1,0:T(8,128)S(1)}, f32[12,24,...) custom-call(f32[23,12,24,128]{3,2,1,0:T(8,128)S(1)} %get-tuple-element.31.ext.ext_in, ...), custom_call_target="tpu_custom_call", output_to_operand_aliasing={{0}: (0, {})} | custom-call | tf_op jit(solution)/shard_map/turn/pallas_call | solution.py:148
  16.2 0.0 collective-permute-done.4.r2
  16.2 1.2 %mid.1 = (f32[23,12,24,128]{3,2,1,0:T(8,128)S(1)}, f32[12,24,128]{2,1,0:T(8,128)S(1)}, f32[12,24,128]{2,1,0:T(8,128)S(1)}, f32[12,24,128]{2,1,0:T(8,128)S(1)}, f...) custom-call(f32[23,12,24,128]{3,2,1,0:T(8,128)S(1)} %get-tuple-eleme, ...), custom_call_target="tpu_custom_call", output_to_operand_aliasing={{0}: (0, {}), {1}: (8, {}), {2}: (9, {}), {3}: (10, {})} | custom-call | tf_op jit(solution)/shard_map/mid/pallas_call | solution.py:148
  17.4 0.0 collective-permute-done.5.r1
  17.4 0.8 %collective-permute-done.6.r2 = f32[2,72,128]{2,1,0:T(8,128)S(1)} collective-permute-done((f32[2,72,128]{2,1,0:T(8,128)S(1)}, f32[2,72,128]{2,1,0:T(8,128)S(1)}, u32[]{:S(2)}, u32[]{:S(2)}) %collective-permute-start.6) | collective-permute-done | bytes 73760 | tf_op jit(solution)/shard_map/ppermute | solution.py:613
  18.2 1.8 %last.1 = (f32[23,12,24,128]{3,2,1,0:T(8,128)S(1)}, f32[23,24,128]{2,1,0:T(8,128)S(1)}, f32[12,24,128]{2,1,0:T(8,128)S(1)}, f32[12,24,128]{2,1,0:T(8,128)S(1)}, ...) custom-call(f32[23,12,24,128]{3,2,1,0:T(8,128)S(1)} %fill.1.ext_in, ...), custom_call_target="tpu_custom_call", output_to_operand_aliasing={{0}: (0, {}), {1}: (1, {}), {2}: (3, {}), {3}: (4, {}), {4}... | custom-call | tf_op jit(solution)/shard_map/last/pallas_call | solution.py:148
  (1 shorter events, 0.0 us)
Async XLA Ops:
  2.0 5.2 %collective-permute-start = (f32[80,128]{1,0:T(8,128)S(1)}, f32[80,128]{1,0:T(8,128)S(1)}, u32[]{:S(2)}, u32[]{:S(2)}) collective-permute-start(f32[80,128]{1,0:T(8,128)S(1)} %get-tuple-element.33), channel_id=1, source_target_pairs={{4,8},{8,4},{12,0},{0,12},{5,9},{9,5},{13,1},{1,13},{6,10},{10,6},... | collective-permute-start | bytes 122888 | tf_op jit(solution)/shard_map/ppermute | solution.py:607
  4.7 2.6 %collective-permute-start.1 = (f32[232,128]{1,0:T(8,128)S(1)}, f32[232,128]{1,0:T(8,128)S(1)}, u32[]{:S(2)}, u32[]{:S(2)}) collective-permute-start(f32[232,128]{1,0:T(8,128)S(1)} %pair.1), channel_id=1, source_target_pairs={{0,4},{4,0},{8,12},{12,8},{1,5},{5,1},{9,13},{13,9},{2,6},{6,2},{1... | collective-permute-start | bytes 356360 | tf_op jit(solution)/shard_map/ppermute | solution.py:607
  5.5 11.9 %collective-permute-start.5 = (f32[2,24,16,128]{3,2,1,0:T(8,128)S(1)}, f32[2,24,16,128]{3,2,1,0:T(8,128)S(1)}, u32[]{:S(2)}, u32[]{:S(2)}) collective-permute-start(f32[2,24,16,128]{3,2,1,0:T(8,128)S(1)} %xpack.1), channel_id=1, source_target_pairs={{0,16},{16,0},{1,17},{17,1},{2,18},{18,2},{3,19},{19,3},{4,20},{20... | collective-permute-start | bytes 1179656 | tf_op jit(solution)/shard_map/ppermute | solution.py:613
  7.4 5.7 %collective-permute-start.2 = (f32[40,128]{1,0:T(8,128)S(1)}, f32[40,128]{1,0:T(8,128)S(1)}, u32[]{:S(2)}, u32[]{:S(2)}) collective-permute-start(f32[40,128]{1,0:T(8,128)S(1)} %get-tuple-element.38), channel_id=1, source_target_pairs={{0,1},{1,2},{2,3},{3,0},{4,5},{5,6},{6,7},{7,4},{8,9},{9,10},{10,1... | collective-permute-start | bytes 61448 | tf_op jit(solution)/shard_map/ppermute | solution.py:599
  9.1 4.0 %collective-permute-start.3 = (f32[40,128]{1,0:T(8,128)S(1)}, f32[40,128]{1,0:T(8,128)S(1)}, u32[]{:S(2)}, u32[]{:S(2)}) collective-permute-start(f32[40,128]{1,0:T(8,128)S(1)} %get-tuple-element.39), channel_id=1, source_target_pairs={{1,0},{2,1},{3,2},{0,3},{5,4},{6,5},{7,6},{4,7},{9,8},{10,9},{11,1... | collective-permute-start | bytes 61448 | tf_op jit(solution)/shard_map/ppermute | solution.py:599
  11.4 4.8 %collective-permute-start.4 = (f32[152,128]{1,0:T(8,128)S(1)}, f32[152,128]{1,0:T(8,128)S(1)}, u32[]{:S(2)}, u32[]{:S(2)}) collective-permute-start(f32[152,128]{1,0:T(8,128)S(1)} %ypack.1), channel_id=1, source_target_pairs={{4,8},{8,4},{12,0},{0,12},{5,9},{9,5},{13,1},{1,13},{6,10},{10,6},... | collective-permute-start | bytes 233480 | tf_op jit(solution)/shard_map/ppermute | solution.py:607
  13.5 4.7 %collective-permute-start.6 = (f32[2,72,128]{2,1,0:T(8,128)S(1)}, f32[2,72,128]{2,1,0:T(8,128)S(1)}, u32[]{:S(2)}, u32[]{:S(2)}) collective-permute-start(f32[2,72,128]{2,1,0:T(8,128)S(1)} %get-tuple-element.50), channel_id=1, source_target_pairs={{0,16},{16,0},{1,17},{17,1},{2,18},{18,2},{3,19},{19,3},{4,20},{20... | collective-permute-start | bytes 221192 | tf_op jit(solution)/shard_map/ppermute | solution.py:613

commit v9 on v7

--- a/solution.py
+++ b/solution.py
@@ -243,14 +243,13 @@
     return sorted(found, key=lambda entry: z_part(entry[0]))
 
 
-def y_lines(ext, msg, on_odd, on_even):
-    six = ext.shape[1] - 6
-
-    def fill(side):
+def y_lines(ext, low, high):
+    for side, msg in ((-1, low), (1, high)):
         entries = y_entries(side)
+        six = ext.shape[1] - 6
+        msg[pl.ds(six * len(entries), 8), :] = jnp.zeros((8, 128), F32)
         for e, (f, d, first) in enumerate(entries):
             msg[pl.ds(six * e, six), :] = ext[f, pl.ds(first, six), 15 - d if side < 0 else d, :]
-        msg[pl.ds(six * len(entries), 8), :] = jnp.zeros((8, 128), F32)
         for step in (-1, 1):
             hits = [e for e, (f, _, _) in enumerate(entries) if z_part(f) == step]
             start, stop = six * hits[0], six * (hits[-1] + 1)
@@ -259,14 +258,11 @@
             place = bottom + lax.broadcasted_iota(jnp.int32, v.shape, 0)
             msg[pl.ds(bottom, top - bottom), :] = jnp.where((place >= start) & (place < stop), lroll(v, -step), v)
 
-    odd = lax.axis_index("gy") % 2
-    pl.when(odd == 1)(lambda: fill(on_odd))
-    pl.when(odd == 0)(lambda: fill(on_even))
-
-
-def pair_kernel(ext, small, msg):
+
+def pair_kernel(ext, small, msg, low, high):
+    y_lines(ext, low, high)
     msg[pl.ds(0, small.shape[0]), :] = small[...]
-    y_lines(ext, msg.at[pl.ds(small.shape[0], msg.shape[0] - small.shape[0]), :], 1, -1)
+    msg[pl.ds(small.shape[0], low.shape[0]), :] = by_parity("gy", low[...], high[...])[1]
 
 
 def x_kernel(ext, xmsg):
@@ -299,8 +295,9 @@
         msg[pl.ds(ROWS + 8, 8), :] = tiles[1][16:]
 
 
-def y_kernel(ext, mini, msg):
-    y_lines(ext, msg, -1, 1)
+def y_kernel(ext, mini, msg, low, high):
+    y_lines(ext, low, high)
+    msg[...] = by_parity("gy", low[...], high[...])[0]
 
 
 Z_PAIRS = ((5, 6), (11, 13), (14, 12), (15, 17), (18, 16))
@@ -629,8 +626,9 @@
         name="load",
     )
     large_y = (24 * (nx - 2) + 8, 128)
+    two_large = [pltpu.VMEM(large_y, F32), pltpu.VMEM(large_y, F32)]
     (yb,) = call(
-        pair_kernel, (ext, yb), ((small_y[0] + large_y[0], 128),), name="pair", cost=COSTLY
+        pair_kernel, (ext, yb), ((small_y[0] + large_y[0], 128),), scratch=two_large, name="pair", cost=COSTLY
     )
     (xmsg,) = call(x_kernel, (ext,), ((2, 24, 16, 128),), name="xpack", cost=COSTLY)
     x1 = swap_both(xmsg, "gx")
@@ -642,7 +640,7 @@
         aliases={0: 0},
         name="yz",
     )
-    (y2a,) = call(y_kernel, (ext, mini), (large_y,), name="ypack", cost=COSTLY)
+    (y2a,) = call(y_kernel, (ext, mini), (large_y,), scratch=two_large, name="ypack", cost=COSTLY)
     y2a = ppermute_pairs(y2a, "gy", 1)
     za, zb = swap(za, zb, "gz")
     mini, xmsg2 = call(

time: 20.1 us -> 20.2 us (level)
  no operation moved by 1% of the time
where the time goes in v9:
time: 20.2 us; the launch traced here: 20 us
  starting transfers between devices  11.4 us (56%)
  Pallas kernels  7.28 us (36%)
  waiting for transfers between devices  1.31 us (6%)
    pallas_call x10, Pallas kernels, call(): pl.pallas_call(body, in_specs=in_specs or [VM] * len(ins), out_specs=out_...  7.28 us
    ppermute x3, starting transfers between devices, ppermute_pairs(): return lax.ppermute(msg, axis, found)  4.29 us
    ppermute x2, starting transfers between devices, swap_both(): return lax.ppermute(msg, axis, [(0, 1), (1, 0)])  3.12 us
    ppermute x1, starting transfers between devices, swap(): lax.ppermute(high, axis, [(j, i) for i, j in up])  2.09 us
    ppermute x1, starting transfers between devices, swap(): lax.ppermute(low, axis, up)  1.87 us
    ppermute x2, waiting for transfers between devices, swap_both(): return lax.ppermute(msg, axis, [(0, 1), (1, 0)])  0.65 us
    ppermute x1, waiting for transfers between devices, swap(): lax.ppermute(low, axis, up)  0.56 us
  transfers between devices with their start and end apart: 7, of which 3 were waited for; matrix products, arithmetic and copies ran while one was open for 0% of the time, Pallas kernels for 17%

profile of v9, /device:TPU:0, one launch (start us, length us, event | category | flops | bytes accessed | tf_op | source)
XLA Modules:
  0.0 20.0 jit_solution(6055653361094955982)
XLA Ops:
  0.0 2.0 %load.1 = (f32[23,12,24,128]{3,2,1,0:T(8,128)S(1)}, f32[23,24,128]{2,1,0:T(8,128)S(1)}, f32[80,128]{1,0:T(8,128)S(1)}, f32[80,128]{1,0:T(8,128)S(1)}) custom-call(f32[19,8,16,128]{3,2,1,0:T(8,128)} %pop_hbm.1, f32[19,8,16,128]{3,2,1,0:T(8,128)} %adj_hbm.1), custom_call_target="tpu_custom_call" | custom-call | tf_op jit(solution)/shard_map/load/pallas_call | solution.py:148
  2.0 2.5 %collective-permute-start = (f32[80,128]{1,0:T(8,128)S(1)}, f32[80,128]{1,0:T(8,128)S(1)}, u32[]{:S(2)}, u32[]{:S(2)}) collective-permute-start(f32[80,128]{1,0:T(8,128)S(1)} %get-tuple-element.31), channel_id=1, source_target_pairs={{4,8},{8,4},{12,0},{0,12},{5,9},{9,5},{13,1},{1,13},{6,10},{10,6},... | collective-permute-start | bytes 122888 | tf_op jit(solution)/shard_map/ppermute | solution.py:606
  4.5 0.2 pair.1
  4.7 0.7 %collective-permute-start.1 = (f32[232,128]{1,0:T(8,128)S(1)}, f32[232,128]{1,0:T(8,128)S(1)}, u32[]{:S(2)}, u32[]{:S(2)}) collective-permute-start(f32[232,128]{1,0:T(8,128)S(1)} %pair.1), channel_id=1, source_target_pairs={{0,4},{4,0},{8,12},{12,8},{1,5},{5,1},{9,13},{13,9},{2,6},{6,2},{1... | collective-permute-start | bytes 356360 | tf_op jit(solution)/shard_map/ppermute | solution.py:606
  5.4 0.1 xpack.1
  5.5 1.6 %collective-permute-start.5 = (f32[2,24,16,128]{3,2,1,0:T(8,128)S(1)}, f32[2,24,16,128]{3,2,1,0:T(8,128)S(1)}, u32[]{:S(2)}, u32[]{:S(2)}) collective-permute-start(f32[2,24,16,128]{3,2,1,0:T(8,128)S(1)} %xpack.1), channel_id=1, source_target_pairs={{0,16},{16,0},{1,17},{17,1},{2,18},{18,2},{3,19},{19,3},{4,20},{20... | collective-permute-start | bytes 1179656 | tf_op jit(solution)/shard_map/ppermute | solution.py:612
  7.1 0.0 collective-permute-done.ra
  7.1 0.0 collective-permute-done.1.rb
  7.1 0.2 %yz.1 = (f32[23,24,128]{2,1,0:T(8,128)S(1)}, f32[40,128]{1,0:T(8,128)S(1)}, f32[40,128]{1,0:T(8,128)S(1)}, f32[80,128]{1,0:T(8,128)S(1)}, f32[80,128]{1,0:T(8,128)S(1)}) custom-call(f32[23,24,128]{2,1,0:T(8,128)S(1)} %get-tuple-element.30.mini_in, f32[80,128]{1,0:T(8,128)S(1)} %collective-permute-done.ra, ...), custom_call_target="tpu_custom_call", output_to_operand_aliasing={{0}: (0, {})} | custom-call | tf_op jit(solution)/shard_map/yz/pallas_call | solution.py:148
  7.3 1.9 %collective-permute-start.2 = (f32[40,128]{1,0:T(8,128)S(1)}, f32[40,128]{1,0:T(8,128)S(1)}, u32[]{:S(2)}, u32[]{:S(2)}) collective-permute-start(f32[40,128]{1,0:T(8,128)S(1)} %get-tuple-element.34), channel_id=1, source_target_pairs={{0,1},{1,2},{2,3},{3,0},{4,5},{5,6},{6,7},{7,4},{8,9},{9,10},{10,1... | collective-permute-start | bytes 61448 | tf_op jit(solution)/shard_map/ppermute | solution.py:598
  9.2 2.1 %collective-permute-start.3 = (f32[40,128]{1,0:T(8,128)S(1)}, f32[40,128]{1,0:T(8,128)S(1)}, u32[]{:S(2)}, u32[]{:S(2)}) collective-permute-start(f32[40,128]{1,0:T(8,128)S(1)} %get-tuple-element.35), channel_id=1, source_target_pairs={{1,0},{2,1},{3,2},{0,3},{5,4},{6,5},{7,6},{4,7},{9,8},{10,9},{11,1... | collective-permute-start | bytes 61448 | tf_op jit(solution)/shard_map/ppermute | solution.py:598
  11.3 0.2 ypack.1
  11.5 1.1 %collective-permute-start.4 = (f32[152,128]{1,0:T(8,128)S(1)}, f32[152,128]{1,0:T(8,128)S(1)}, u32[]{:S(2)}, u32[]{:S(2)}) collective-permute-start(f32[152,128]{1,0:T(8,128)S(1)} %ypack.1), channel_id=1, source_target_pairs={{4,8},{8,4},{12,0},{0,12},{5,9},{9,5},{13,1},{1,13},{6,10},{10,6},... | collective-permute-start | bytes 233480 | tf_op jit(solution)/shard_map/ppermute | solution.py:606
  12.6 0.6 %collective-permute-done.2.ra = f32[40,128]{1,0:T(8,128)S(1)} collective-permute-done((f32[40,128]{1,0:T(8,128)S(1)}, f32[40,128]{1,0:T(8,128)S(1)}, u32[]{:S(2)}, u32[]{:S(2)}) %collective-permute-start.2) | collective-permute-done | bytes 20512 | tf_op jit(solution)/shard_map/ppermute | solution.py:598
  13.1 0.1 collective-permute-done.3.rb
  13.2 0.4 %zx.1 = (f32[23,24,128]{2,1,0:T(8,128)S(1)}, f32[2,72,128]{2,1,0:T(8,128)S(1)}) custom-call(f32[23,24,128]{2,1,0:T(8,128)S(1)} %get-tuple-element.33.mini_in.mini, f32[40,128]{1,0:T(8,128)S(1)} %collective-permute-done.2.ra, f32[40,128]{1,0:T(8,128)S(1)} %collective-permute-done.3.rb, ...), custom_call_target="tpu_custom_call", output_to_operand_aliasing={{0}: (0, {})} | custom-call | tf_op jit(solution)/shard_map/zx/pallas_call | solution.py:148
  13.6 1.6 %collective-permute-start.6 = (f32[2,72,128]{2,1,0:T(8,128)S(1)}, f32[2,72,128]{2,1,0:T(8,128)S(1)}, u32[]{:S(2)}, u32[]{:S(2)}) collective-permute-start(f32[2,72,128]{2,1,0:T(8,128)S(1)} %get-tuple-element.46), channel_id=1, source_target_pairs={{0,16},{16,0},{1,17},{17,1},{2,18},{18,2},{3,19},{19,3},{4,20},{20... | collective-permute-start | bytes 221192 | tf_op jit(solution)/shard_map/ppermute | solution.py:612
  15.2 1.2 %turn.1 = (f32[23,12,24,128]{3,2,1,0:T(8,128)S(1)}, f32[24,128]{1,0:T(8,128)S(1)}, f32[24,128]{1,0:T(8,128)S(1)}, f32[12,24,128]{2,1,0:T(8,128)S(1)}, f32[12,24,...) custom-call(f32[23,12,24,128]{3,2,1,0:T(8,128)S(1)} %get-tuple-element.29.ext.ext_in, ...), custom_call_target="tpu_custom_call", output_to_operand_aliasing={{0}: (0, {})} | custom-call | tf_op jit(solution)/shard_map/turn/pallas_call | solution.py:148
  16.3 0.0 collective-permute-done.4.r2
  16.4 1.2 %mid.1 = (f32[23,12,24,128]{3,2,1,0:T(8,128)S(1)}, f32[12,24,128]{2,1,0:T(8,128)S(1)}, f32[12,24,128]{2,1,0:T(8,128)S(1)}, f32[12,24,128]{2,1,0:T(8,128)S(1)}, f...) custom-call(f32[23,12,24,128]{3,2,1,0:T(8,128)S(1)} %get-tuple-eleme, ...), custom_call_target="tpu_custom_call", output_to_operand_aliasing={{0}: (0, {}), {1}: (8, {}), {2}: (9, {}), {3}: (10, {})} | custom-call | tf_op jit(solution)/shard_map/mid/pallas_call | solution.py:148
  17.5 0.0 collective-permute-done.5.r1
  17.6 0.6 %collective-permute-done.6.r2 = f32[2,72,128]{2,1,0:T(8,128)S(1)} collective-permute-done((f32[2,72,128]{2,1,0:T(8,128)S(1)}, f32[2,72,128]{2,1,0:T(8,128)S(1)}, u32[]{:S(2)}, u32[]{:S(2)}) %collective-permute-start.6) | collective-permute-done | bytes 73760 | tf_op jit(solution)/shard_map/ppermute | solution.py:612
  18.2 1.8 %last.1 = (f32[23,12,24,128]{3,2,1,0:T(8,128)S(1)}, f32[23,24,128]{2,1,0:T(8,128)S(1)}, f32[12,24,128]{2,1,0:T(8,128)S(1)}, f32[12,24,128]{2,1,0:T(8,128)S(1)}, ...) custom-call(f32[23,12,24,128]{3,2,1,0:T(8,128)S(1)} %fill.1.ext_in, ...), custom_call_target="tpu_custom_call", output_to_operand_aliasing={{0}: (0, {}), {1}: (1, {}), {2}: (3, {}), {3}: (4, {}), {4}... | custom-call | tf_op jit(solution)/shard_map/last/pallas_call | solution.py:148
  (1 shorter events, 0.0 us)
Async XLA Ops:
  2.0 5.1 %collective-permute-start = (f32[80,128]{1,0:T(8,128)S(1)}, f32[80,128]{1,0:T(8,128)S(1)}, u32[]{:S(2)}, u32[]{:S(2)}) collective-permute-start(f32[80,128]{1,0:T(8,128)S(1)} %get-tuple-element.31), channel_id=1, source_target_pairs={{4,8},{8,4},{12,0},{0,12},{5,9},{9,5},{13,1},{1,13},{6,10},{10,6},... | collective-permute-start | bytes 122888 | tf_op jit(solution)/shard_map/ppermute | solution.py:606
  4.7 2.4 %collective-permute-start.1 = (f32[232,128]{1,0:T(8,128)S(1)}, f32[232,128]{1,0:T(8,128)S(1)}, u32[]{:S(2)}, u32[]{:S(2)}) collective-permute-start(f32[232,128]{1,0:T(8,128)S(1)} %pair.1), channel_id=1, source_target_pairs={{0,4},{4,0},{8,12},{12,8},{1,5},{5,1},{9,13},{13,9},{2,6},{6,2},{1... | collective-permute-start | bytes 356360 | tf_op jit(solution)/shard_map/ppermute | solution.py:606
  5.5 12.0 %collective-permute-start.5 = (f32[2,24,16,128]{3,2,1,0:T(8,128)S(1)}, f32[2,24,16,128]{3,2,1,0:T(8,128)S(1)}, u32[]{:S(2)}, u32[]{:S(2)}) collective-permute-start(f32[2,24,16,128]{3,2,1,0:T(8,128)S(1)} %xpack.1), channel_id=1, source_target_pairs={{0,16},{16,0},{1,17},{17,1},{2,18},{18,2},{3,19},{19,3},{4,20},{20... | collective-permute-start | bytes 1179656 | tf_op jit(solution)/shard_map/ppermute | solution.py:612
  7.3 5.8 %collective-permute-start.2 = (f32[40,128]{1,0:T(8,128)S(1)}, f32[40,128]{1,0:T(8,128)S(1)}, u32[]{:S(2)}, u32[]{:S(2)}) collective-permute-start(f32[40,128]{1,0:T(8,128)S(1)} %get-tuple-element.34), channel_id=1, source_target_pairs={{0,1},{1,2},{2,3},{3,0},{4,5},{5,6},{6,7},{7,4},{8,9},{9,10},{10,1... | collective-permute-start | bytes 61448 | tf_op jit(solution)/shard_map/ppermute | solution.py:598
  9.2 4.0 %collective-permute-start.3 = (f32[40,128]{1,0:T(8,128)S(1)}, f32[40,128]{1,0:T(8,128)S(1)}, u32[]{:S(2)}, u32[]{:S(2)}) collective-permute-start(f32[40,128]{1,0:T(8,128)S(1)} %get-tuple-element.35), channel_id=1, source_target_pairs={{1,0},{2,1},{3,2},{0,3},{5,4},{6,5},{7,6},{4,7},{9,8},{10,9},{11,1... | collective-permute-start | bytes 61448 | tf_op jit(solution)/shard_map/ppermute | solution.py:598
  11.5 4.9 %collective-permute-start.4 = (f32[152,128]{1,0:T(8,128)S(1)}, f32[152,128]{1,0:T(8,128)S(1)}, u32[]{:S(2)}, u32[]{:S(2)}) collective-permute-start(f32[152,128]{1,0:T(8,128)S(1)} %ypack.1), channel_id=1, source_target_pairs={{4,8},{8,4},{12,0},{0,12},{5,9},{9,5},{13,1},{1,13},{6,10},{10,6},... | collective-permute-start | bytes 233480 | tf_op jit(solution)/shard_map/ppermute | solution.py:606
  13.6 4.6 %collective-permute-start.6 = (f32[2,72,128]{2,1,0:T(8,128)S(1)}, f32[2,72,128]{2,1,0:T(8,128)S(1)}, u32[]{:S(2)}, u32[]{:S(2)}) collective-permute-start(f32[2,72,128]{2,1,0:T(8,128)S(1)} %get-tuple-element.46), channel_id=1, source_target_pairs={{0,16},{16,0},{1,17},{17,1},{2,18},{18,2},{3,19},{19,3},{4,20},{20... | collective-permute-start | bytes 221192 | tf_op jit(solution)/shard_map/ppermute | solution.py:612
